TPU v7x, 32 devices: a whole 2x2x4 slice. The times are simulated.
32 devices in a mesh: context: 8 (over y, x, core), tensor: 4 (over z).
Axes of the slice: x: 2, y: 2, z: 4, core: 2. Of those that a mesh axis runs over, the one named last changes fastest.
Arguments:
- query_proj: bfloat16 [1024, 4096], P('context', 'tensor'), may hold values from -6 to 6
- key_proj: bfloat16 [1024, 4096], P('context', 'tensor'), may hold values from -6 to 6
- value_proj: bfloat16 [1024, 4096], P('context', 'tensor'), may hold values from -6 to 6
- short_taps: float32 [3, 7, 4096], P(None, None, 'tensor'), may hold values from -2.4 to 2.4
- long_filter: float32 [4, 1024, 1024], P('tensor', 'context'), may hold values from -1 to 1
- grad_mixed: bfloat16 [1024, 4096], P('context', 'tensor'), may hold values from -6 to 6
Outputs:
- mixed_out: bfloat16 [1024, 4096], P('context', 'tensor')
- input_grads: bfloat16 [3, 1024, 4096], P(None, 'context', 'tensor')
- filter_grad: float32 [4, 1024, 1024], P('tensor', 'context')
All inputs are finite; a program needn't handle non-finite values.
Results may differ from a plain program's by a relative error of at most 0.0064.
Values may be sent and summed in bfloat16 or wider, within the bound.
No kernel may reach another device: no remote copies, remote signals or barrier semaphores. Data moves between devices by JAX's collectives and lax.ppermute only.
A program may use at most 64 MiB of HBM per device.

v0:
```python
import functools
import math

import jax
import jax.numpy as jnp
import numpy as np
from jax import lax
from jax.experimental import pallas as pl
from jax.experimental.pallas import tpu as pltpu
from jax.sharding import PartitionSpec as P

precise = lax.Precision.HIGHEST


def from_behind(value, axis, steps):
    count = lax.axis_size(axis)
    first, last = (max(0, -steps), min(count, count - steps))
    return lax.ppermute(value, axis, [(source, source + steps) for source in range(first, last)])


def build_tables(blocks, tok_rows):
    outer_len = 2 * blocks
    full_len = outer_len * tok_rows
    k_one = jnp.arange(outer_len, dtype=jnp.int32)
    n_one = jnp.arange(blocks, dtype=jnp.int32)
    position = jnp.arange(tok_rows, dtype=jnp.int32)
    first_idx = k_one[:, None] * n_one[None, :] % outer_len
    first_angle = -2.0 * math.pi / outer_len * first_idx.astype(jnp.float32)
    second = position[:, None] * position[None, :] % tok_rows
    second_angle = -2.0 * math.pi / tok_rows * second.astype(jnp.float32)
    twist_idx = k_one[:, None] * position[None, :] % full_len
    twist_angle = -2.0 * math.pi / full_len * twist_idx.astype(jnp.float32)
    return (
        jnp.cos(first_angle),
        jnp.sin(first_angle),
        jnp.cos(second_angle),
        jnp.sin(second_angle),
        jnp.cos(twist_angle),
        jnp.sin(twist_angle),
    )


def transform(signal, tables):
    cos_first, sin_first, cos_second, sin_second, cos_twist, sin_twist = tables
    first_re = jnp.einsum("kn,gnm->gkm", cos_first, signal, precision=precise)
    first_im = jnp.einsum("kn,gnm->gkm", sin_first, signal, precision=precise)
    mid_re = first_re * cos_twist - first_im * sin_twist
    mid_im = first_re * sin_twist + first_im * cos_twist
    out_re = jnp.einsum("gkn,nm->gkm", mid_re, cos_second, precision=precise) - jnp.einsum(
        "gkn,nm->gkm", mid_im, sin_second, precision=precise
    )
    out_im = jnp.einsum("gkn,nm->gkm", mid_re, sin_second, precision=precise) + jnp.einsum(
        "gkn,nm->gkm", mid_im, cos_second, precision=precise
    )
    return (out_re, out_im)


def inverse(spec_re, spec_im, tables):
    cos_first, sin_first, cos_second, sin_second, cos_twist, sin_twist = tables
    full_len = cos_first.shape[0] * cos_second.shape[0]
    mid_re = jnp.einsum("gkn,nm->gkm", spec_re, cos_second, precision=precise) + jnp.einsum(
        "gkn,nm->gkm", spec_im, sin_second, precision=precise
    )
    mid_im = jnp.einsum("gkn,nm->gkm", spec_im, cos_second, precision=precise) - jnp.einsum(
        "gkn,nm->gkm", spec_re, sin_second, precision=precise
    )
    turn_re = mid_re * cos_twist + mid_im * sin_twist
    turn_im = mid_im * cos_twist - mid_re * sin_twist
    result = jnp.einsum("kn,gkm->gnm", cos_first, turn_re, precision=precise) + jnp.einsum(
        "kn,gkm->gnm", sin_first, turn_im, precision=precise
    )
    return result * (1.0 / full_len)


def causal_taps(series, preceding, tap_weights):
    tok_rows = series.shape[0]
    span = tap_weights.shape[0]
    joined = jnp.concatenate([preceding, series], axis=0).astype(jnp.float32)
    running = jnp.zeros(series.shape, jnp.float32)
    for offset in range(span):
        first_row = span - 1 - offset
        running = running + tap_weights[offset][None, :] * joined[first_row : first_row + tok_rows]
    return running


def reverse_taps(series, following, tap_weights):
    tok_rows = series.shape[0]
    span = tap_weights.shape[0]
    joined = jnp.concatenate([series, following], axis=0).astype(jnp.float32)
    running = jnp.zeros(series.shape, jnp.float32)
    for offset in range(span):
        running = running + tap_weights[offset][None, :] * joined[offset : offset + tok_rows]
    return running


def general_shards(query_proj, key_proj, value_proj, short_taps, long_filter, grad_mixed):
    tok_rows, channels = query_proj.shape
    blocks = lax.axis_size("context")
    halo_rows = short_taps.shape[1] - 1
    per_device = channels // blocks
    seq_len = tok_rows * blocks
    tables = build_tables(blocks, tok_rows)
    preceding = from_behind(
        (
            query_proj[tok_rows - halo_rows :],
            key_proj[tok_rows - halo_rows :],
            value_proj[tok_rows - halo_rows :],
        ),
        "context",
        1,
    )
    query_f = causal_taps(query_proj, preceding[0], short_taps[0])
    key_f = causal_taps(key_proj, preceding[1], short_taps[1])
    value_f = causal_taps(value_proj, preceding[2], short_taps[2])
    gated_prod = (key_f * value_f).astype(jnp.bfloat16)
    grad_f = grad_mixed.astype(jnp.float32)
    grad_long = (grad_f * query_f).astype(jnp.bfloat16)

    def to_spectrum(series):
        arranged = series.T.reshape(blocks, per_device, tok_rows)
        received = lax.all_to_all(arranged, "context", split_axis=0, concat_axis=2, tiled=True)
        item_count = received.shape[1]
        signal = received.reshape(item_count, blocks, tok_rows).astype(jnp.float32)
        return transform(signal, tables)

    def to_token_rows(spatial):
        arrived = lax.all_to_all(spatial, "context", split_axis=1, concat_axis=0, tiled=True)
        return arrived.reshape(channels, tok_rows).T

    gate_re, gate_im = to_spectrum(gated_prod)
    filter_re, filter_im = transform(long_filter.reshape(per_device, blocks, tok_rows), tables)
    long_spatial = inverse(
        gate_re * filter_re - gate_im * filter_im, gate_re * filter_im + gate_im * filter_re, tables
    ).astype(jnp.bfloat16)
    long_conv = to_token_rows(long_spatial)
    long_f = long_conv.astype(jnp.float32)
    mixed_out = (query_f * long_f).astype(jnp.bfloat16)
    grad_query_f = (grad_f * long_f).astype(jnp.bfloat16)
    grad_after = lax.optimization_barrier((grad_long, long_conv))[0]
    grad_re, grad_im = to_spectrum(grad_after)
    back_spatial = inverse(
        filter_re * grad_re + filter_im * grad_im, filter_re * grad_im - filter_im * grad_re, tables
    ).astype(jnp.bfloat16)
    corr_spatial = inverse(
        gate_re * grad_re + gate_im * grad_im, gate_re * grad_im - gate_im * grad_re, tables
    )
    grad_gated = to_token_rows(back_spatial).astype(jnp.float32)
    grad_key_f = (grad_gated * value_f).astype(jnp.bfloat16)
    grad_value_f = (grad_gated * key_f).astype(jnp.bfloat16)
    following = from_behind(
        (grad_query_f[:halo_rows], grad_key_f[:halo_rows], grad_value_f[:halo_rows]), "context", -1
    )
    input_grads = jnp.stack(
        [
            reverse_taps(grad_query_f, following[0], short_taps[0]),
            reverse_taps(grad_key_f, following[1], short_taps[1]),
            reverse_taps(grad_value_f, following[2], short_taps[2]),
        ]
    ).astype(jnp.bfloat16)
    filter_grad = (corr_spatial * (1.0 / math.sqrt(seq_len))).reshape(1, per_device, seq_len)
    return (mixed_out, input_grads, filter_grad)


LANES = 128
VMEM_BYTES = 48 * 1024 * 1024


def split_bf16(table):
    high = table.astype(jnp.bfloat16)
    low = (table - high.astype(np.float64)).astype(jnp.bfloat16)
    return (high, low)


@functools.cache
def block_tables(rows):
    bins = np.pi * (np.arange(rows) + 0.5)[:, None] / rows
    lag = np.arange(-rows, rows)[None, :]
    window = np.concatenate([np.cos(bins * lag), -np.sin(bins * lag)], axis=0)
    window_hi, window_lo = split_bf16(window)
    doubled = np.concatenate([window_hi[:, rows:], window_lo[:, rows:]], axis=1)
    inv_hi, inv_lo = split_bf16(window[:, rows:].T / rows)
    return (window_hi, window_lo, doubled, inv_hi, inv_lo)


def round_up(count, unit):
    return (count + unit - 1) // unit * unit


def head_rows(fresh, whole, halo):
    row = lax.broadcasted_iota(jnp.int32, fresh.shape, 0)
    return jnp.concatenate([jnp.where(row < halo, fresh, whole[:8]), whole[8:]], axis=0)


def tap_rows(taps_ref, which, lanes):
    return [taps_ref[which, pl.ds(offset, 1), lanes] for offset in range(taps_ref.shape[1])]


def short_filter(padded, rows, weights):
    running = weights[0] * padded[pl.ds(8, rows), :]
    for offset in range(1, len(weights)):
        running = running + weights[offset] * padded[pl.ds(8 - offset, rows), :]
    return running


def send_kernel(q_ref, k_ref, v_ref, g_ref, taps_ref, out_ref, padded, extra):
    rows = q_ref.shape[0]
    halo = taps_ref.shape[1] - 1
    groups = out_ref.shape[0]
    padded[:, pl.ds(0, 8), :] = jnp.zeros((3, 8, LANES), jnp.float32)
    extra[...] = jnp.zeros(extra.shape, jnp.float32)

    def body(group, carry):
        lanes = pl.ds(pl.multiple_of(group * LANES, LANES), LANES)
        filtered = []
        for which, ref in enumerate((q_ref, k_ref, v_ref)):
            padded[which, pl.ds(8, rows), :] = ref[:, lanes].astype(jnp.float32)
            filtered.append(short_filter(padded.at[which], rows, tap_rows(taps_ref, which, lanes)))
        query_f, key_f, value_f = filtered
        cotangent = g_ref[:, lanes].astype(jnp.float32)
        gated = head_rows(padded[1, pl.ds(8, 8), :], key_f * value_f, halo)
        grad_long = head_rows(cotangent[:8], cotangent * query_f, halo)
        out_ref[group, pl.ds(0, rows), :] = gated.astype(jnp.bfloat16)
        out_ref[group, pl.ds(rows, rows), :] = grad_long.astype(jnp.bfloat16)
        pieces = ((1, rows - halo), (2, 0), (2, rows - halo), (0, 0), (0, rows - halo))
        for place, (which, first) in enumerate(pieces):
            extra[pl.ds(place * halo, halo), :] = padded[which, pl.ds(8 + first, halo), :]
        out_ref[group, pl.ds(2 * rows, extra.shape[0]), :] = extra[...].astype(jnp.bfloat16)
        return carry

    lax.fori_loop(0, groups, body, 0)


def repair_heads(in_ref, taps_ref, edges, joined, rows):
    blocks = in_ref.shape[0]
    span = taps_ref.shape[1]
    halo = span - 1
    joined[...] = jnp.zeros(joined.shape, jnp.float32)
    for block in range(blocks):
        edges[block] = in_ref[block, pl.ds(2 * rows, edges.shape[1]), :].astype(jnp.float32)
    heads = []
    for block in range(blocks):
        key_head = in_ref[block, pl.ds(0, 16), :].astype(jnp.float32)
        grad_head = in_ref[block, pl.ds(rows, 16), :].astype(jnp.float32)[:8]
        joined[1, block, pl.ds(halo, 8), :] = key_head[:8]
        joined[2, block, pl.ds(halo, halo), :] = edges[block, pl.ds(halo, halo), :]
        joined[0, block, pl.ds(halo, halo), :] = edges[block, pl.ds(3 * halo, halo), :]
        if block > 0:
            for which, place in ((1, 0), (2, 2), (0, 4)):
                joined[which, block, pl.ds(0, halo), :] = edges[block - 1, pl.ds(place * halo, halo), :]
        filtered = []
        for which in range(3):
            running = jnp.zeros((8, LANES), jnp.float32)
            for offset in range(span):
                weight = taps_ref[which, pl.ds(offset, 1), :]
                running = running + weight * joined[which, block, pl.ds(halo - offset, 8), :]
            filtered.append(running)
        heads.append((filtered[0], filtered[1], filtered[2], grad_head))
    return heads


def to_spectra(in_ref, heads, doubled, spec_x, spec_g, rows, halo):
    for block, (query_f, key_f, value_f, cotangent) in enumerate(heads):
        parts = []
        for first, fresh in ((0, key_f * value_f), (rows, cotangent * query_f)):
            head = in_ref[block, pl.ds(first, 16), :].astype(jnp.float32)
            head = head_rows(fresh, head, halo).astype(jnp.bfloat16)
            parts.append(
                jnp.concatenate([head, in_ref[block, pl.ds(first + 16, rows - 16), :]], axis=0)
            )
        pair = jnp.concatenate(parts, axis=1)
        spectrum = jnp.dot(
            doubled, jnp.concatenate([pair, pair], axis=0), preferred_element_type=jnp.float32
        )
        spec_x[block] = spectrum[:, :LANES]
        spec_g[block] = spectrum[:, LANES:]


def filter_kernel(h_ref, window_hi, window_lo, out_ref):
    blocks, two_rows, _ = out_ref.shape
    rows = two_rows // 2
    for block in range(blocks):
        here = h_ref[:, pl.ds(block * rows, rows)]
        if block > 0:
            before = h_ref[:, pl.ds((block - 1) * rows, rows)]
        else:
            before = jnp.zeros_like(here)
        signal = jnp.concatenate([before, here], axis=1)
        high = signal.astype(jnp.bfloat16)
        low = (signal - high.astype(jnp.float32)).astype(jnp.bfloat16)

        def product(table, values):
            return lax.dot_general(
                table, values, (((1,), (1,)), ((), ())), preferred_element_type=jnp.float32
            )

        out_ref[block] = (
            product(window_hi[...], high) + product(window_lo[...], high) + product(window_hi[...], low)
        )


def load_tile(ref, count, tile, bins):
    real = [ref[index, pl.ds(pl.multiple_of(tile * 8, 8), 8), :] for index in range(count)]
    imag = [ref[index, pl.ds(pl.multiple_of(bins + tile * 8, 8), 8), :] for index in range(count)]
    return (real, imag)


def mixed_products(left, right, sums, conjugate):
    (left_re, left_im), (right_re, right_im) = left, right
    results = []
    for pairs in sums:
        total_re, total_im = None, None
        for one, two in pairs:
            a, b, c, d = left_re[one], left_im[one], right_re[two], right_im[two]
            if conjugate:
                real, imag = a * c + b * d, a * d - b * c
            else:
                real, imag = a * c - b * d, a * d + b * c
            total_re = real if total_re is None else total_re + real
            total_im = imag if total_im is None else total_im + imag
        results.append((total_re, total_im))
    return results


def back_to_rows(spectrum, inv_hi, inv_lo):
    high = spectrum.astype(jnp.bfloat16)
    low = (spectrum - high.astype(jnp.float32)).astype(jnp.bfloat16)
    return (
        jnp.dot(inv_hi, high, preferred_element_type=jnp.float32)
        + jnp.dot(inv_lo, high, preferred_element_type=jnp.float32)
        + jnp.dot(inv_hi, low, preferred_element_type=jnp.float32)
    )


def store_tile(ref, first_lane, results, tile, bins):
    lanes = pl.ds(first_lane, LANES)
    for index, (real, imag) in enumerate(results):
        ref[index, pl.ds(pl.multiple_of(tile * 8, 8), 8), lanes] = real
        ref[index, pl.ds(pl.multiple_of(bins + tile * 8, 8), 8), lanes] = imag


def convolve_kernel(
    in_ref, taps_ref, spec_h, doubled, inv_hi, inv_lo, out_ref,
    edges, joined, spec_x, spec_g, spec_y, extra,
):
    blocks = in_ref.shape[0]
    rows = inv_hi.shape[0]
    halo = taps_ref.shape[1] - 1
    heads = repair_heads(in_ref, taps_ref, edges, joined, rows)
    to_spectra(in_ref, heads, doubled[...], spec_x, spec_g, rows, halo)

    def body(tile, carry):
        filt = load_tile(spec_h, blocks, tile, rows)
        sums = [[(i - j, j) for j in range(i + 1)] for i in range(blocks)]
        store_tile(spec_y, 0, mixed_products(filt, load_tile(spec_x, blocks, tile, rows), sums, False), tile, rows)
        sums = [[(j - i, j) for j in range(i, blocks)] for i in range(blocks)]
        store_tile(spec_y, LANES, mixed_products(filt, load_tile(spec_g, blocks, tile, rows), sums, True), tile, rows)
        return carry

    lax.fori_loop(0, rows // 8, body, 0)
    extra[...] = jnp.zeros(extra.shape, jnp.float32)
    for block, (query_f, key_f, value_f, cotangent) in enumerate(heads):
        both = back_to_rows(spec_y[block], inv_hi[...], inv_lo[...])
        both = both.astype(jnp.bfloat16)
        out_ref[block, pl.ds(0, rows), :] = both[:, :LANES]
        head = both[:16].astype(jnp.float32)
        long_head, back_head = head[:8, :LANES], head[:8, LANES:]
        grad_key = back_head * value_f
        back = jnp.concatenate([head_rows(grad_key, head[:, LANES:], halo).astype(jnp.bfloat16), both[16:, LANES:]], axis=0)
        out_ref[block, pl.ds(rows, rows), :] = back
        grad_value = back_head * key_f
        own = (query_f * long_head, grad_value)
        following = (cotangent * long_head, grad_key, grad_value)
        for place, value in enumerate(own):
            extra[block, pl.ds(place * halo, halo), :] = value[:halo]
        if block > 0:
            for place, value in enumerate(following):
                extra[block - 1, pl.ds((2 + place) * halo, halo), :] = value[:halo]
    for block in range(blocks):
        out_ref[block, pl.ds(2 * rows, extra.shape[1]), :] = extra[block].astype(jnp.bfloat16)


def correlate_kernel(
    scale, in_ref, taps_ref, doubled, inv_hi, inv_lo, out_ref, edges, joined, spec_x, spec_g, spec_y
):
    blocks = in_ref.shape[0]
    rows = inv_hi.shape[0]
    halo = taps_ref.shape[1] - 1
    heads = repair_heads(in_ref, taps_ref, edges, joined, rows)
    to_spectra(in_ref, heads, doubled[...], spec_x, spec_g, rows, halo)

    def body(tile, carry):
        real, imag = load_tile(spec_x, blocks, tile, rows)
        row = lax.broadcasted_iota(jnp.int32, (8, LANES), 0)
        sign = jnp.where(row % 2 == 0, 1.0, -1.0)
        window_re = [real[0]] + [real[i] - sign * imag[i - 1] for i in range(1, blocks)]
        window_im = [imag[0]] + [imag[i] + sign * real[i - 1] for i in range(1, blocks)]
        sums = [[(j - lag, j) for j in range(lag, blocks)] for lag in range(blocks)]
        results = mixed_products((window_re, window_im), load_tile(spec_g, blocks, tile, rows), sums, True)
        store_tile(spec_y, 0, results, tile, rows)
        return carry

    lax.fori_loop(0, rows // 8, body, 0)
    for block in range(blocks):
        result = back_to_rows(spec_y[block], inv_hi[...], inv_lo[...])
        out_ref[0, :, pl.ds(block * rows, rows)] = result.T * scale


def receive_kernel(q_ref, k_ref, v_ref, g_ref, taps_ref, in_ref, mixed_ref, grads_ref, padded, extra):
    rows = q_ref.shape[0]
    span = taps_ref.shape[1]
    halo = span - 1
    groups = in_ref.shape[0]
    for which in range(3):
        padded[which, pl.ds(0, 8), :] = jnp.zeros((8, LANES), jnp.float32)
        padded[which, pl.ds(rows, 16), :] = jnp.zeros((16, LANES), jnp.float32)

    def body(group, carry):
        lanes = pl.ds(pl.multiple_of(group * LANES, LANES), LANES)
        filtered = []
        for which, ref in enumerate((q_ref, k_ref, v_ref)):
            padded[which, pl.ds(0, 8), :] = jnp.zeros((8, LANES), jnp.float32)
            padded[which, pl.ds(8, rows), :] = ref[:, lanes].astype(jnp.float32)
            filtered.append(short_filter(padded.at[which], rows, tap_rows(taps_ref, which, lanes)))
        query_f, key_f, value_f = filtered
        cotangent = g_ref[:, lanes].astype(jnp.float32)
        long_conv = in_ref[group, pl.ds(0, rows), :].astype(jnp.float32)
        back = in_ref[group, pl.ds(rows, rows), :].astype(jnp.float32)
        extra[pl.ds(0, in_ref.shape[1] - 2 * rows), :] = in_ref[group, pl.ds(2 * rows, in_ref.shape[1] - 2 * rows), :].astype(jnp.float32)
        mixed = head_rows(extra[pl.ds(0, 8), :], query_f * long_conv, halo)
        mixed_ref[:, lanes] = mixed.astype(jnp.bfloat16)
        grads = (
            cotangent * long_conv,
            head_rows(back[:8], back * value_f, halo),
            head_rows(extra[pl.ds(halo, 8), :], back * key_f, halo),
        )
        for which, grad in enumerate(grads):
            padded[which, pl.ds(0, rows), :] = grad.astype(jnp.bfloat16).astype(jnp.float32)
            padded[which, pl.ds(rows, halo), :] = extra[pl.ds((2 + which) * halo, halo), :]
            weights = tap_rows(taps_ref, which, lanes)
            running = weights[0] * padded[which, pl.ds(0, rows), :]
            for offset in range(1, span):
                running = running + weights[offset] * padded[which, pl.ds(offset, rows), :]
            grads_ref[which, :, lanes] = running.astype(jnp.bfloat16)
        return carry

    lax.fori_loop(0, groups, body, 0)


def in_vmem(kernel, out_shape, scratch, args):
    whole = pl.BlockSpec(memory_space=pltpu.VMEM)
    single = not isinstance(out_shape, tuple)
    return pl.pallas_call(
        kernel,
        out_shape=out_shape,
        in_specs=[whole] * len(args),
        out_specs=whole if single else (whole,) * len(out_shape),
        scratch_shapes=[pltpu.VMEM(shape, jnp.float32) for shape in scratch],
        compiler_params=pltpu.CompilerParams(vmem_limit_bytes=VMEM_BYTES),
    )(*args)


def block_shards(query_proj, key_proj, value_proj, short_taps, long_filter, grad_mixed):
    rows, channels = query_proj.shape
    blocks = lax.axis_size("context")
    halo = short_taps.shape[1] - 1
    seq_len = rows * blocks
    window_hi, window_lo, doubled, inv_hi, inv_lo = [jnp.asarray(t) for t in block_tables(rows)]
    edge_rows = round_up(5 * halo, 16)
    parcel = jax.ShapeDtypeStruct((blocks, 2 * rows + edge_rows, LANES), jnp.bfloat16)
    spectra = (blocks, 2 * rows, LANES)
    own = lax.dynamic_slice_in_dim(short_taps, lax.axis_index("context") * LANES, LANES, axis=2)

    sent = in_vmem(
        send_kernel,
        parcel,
        [(3, rows + 8, LANES), (edge_rows, LANES)],
        (query_proj, key_proj, value_proj, grad_mixed, short_taps),
    )
    arrived = lax.all_to_all(sent, "context", split_axis=0, concat_axis=0, tiled=True)
    spec_h = in_vmem(
        filter_kernel,
        jax.ShapeDtypeStruct(spectra, jnp.float32),
        [],
        (long_filter[0], window_hi, window_lo),
    )
    repair = [(blocks, edge_rows, LANES), (3, blocks, 24, LANES)]
    results = in_vmem(
        convolve_kernel,
        parcel,
        repair + [spectra, spectra, (blocks, 2 * rows, 2 * LANES), (blocks, edge_rows, LANES)],
        (arrived, own, spec_h, doubled, inv_hi, inv_lo),
    )
    returned = lax.all_to_all(results, "context", split_axis=0, concat_axis=0, tiled=True)
    filter_grad = in_vmem(
        functools.partial(correlate_kernel, 1.0 / math.sqrt(seq_len)),
        jax.ShapeDtypeStruct(long_filter.shape, jnp.float32),
        repair + [spectra, spectra, spectra],
        (arrived, own, doubled, inv_hi, inv_lo),
    )
    mixed_out, input_grads = in_vmem(
        receive_kernel,
        (
            jax.ShapeDtypeStruct((rows, channels), jnp.bfloat16),
            jax.ShapeDtypeStruct((3, rows, channels), jnp.bfloat16),
        ),
        [(3, rows + 16, LANES), (edge_rows + 8, LANES)],
        (query_proj, key_proj, value_proj, grad_mixed, short_taps, returned),
    )
    return (mixed_out, input_grads, filter_grad)


def shards(query_proj, key_proj, value_proj, short_taps, long_filter, grad_mixed):
    rows, channels = query_proj.shape
    halo = short_taps.shape[1] - 1
    fits = channels == lax.axis_size("context") * LANES and rows % 128 == 0 and halo <= 8
    chosen = block_shards if fits else general_shards
    return chosen(query_proj, key_proj, value_proj, short_taps, long_filter, grad_mixed)


def solution(mesh):
    return jax.shard_map(
        shards,
        mesh=mesh,
        in_specs=(
            P("context", "tensor"),
            P("context", "tensor"),
            P("context", "tensor"),
            P(None, None, "tensor"),
            P("tensor", "context", None),
            P("context", "tensor"),
        ),
        out_specs=(
            P("context", "tensor"),
            P(None, "context", "tensor"),
            P("tensor", "context", None),
        ),
        check_vma=False,
    )
```

profile of v0, /device:TPU:0, one launch (start us, length us, event | category | flops | bytes accessed | tf_op | source)
XLA Modules:
  0.0 43.1 jit_solution(3216967977617711418)
XLA Ops:
  0.6 0.0 copy-start
  0.6 0.9 %copy-done = bf16[128,1024]{1,0:T(8,128)(2,1)S(1)} copy-done((bf16[128,1024]{1,0:T(8,128)(2,1)S(1)}, bf16[128,1024]{1,0:T(8,128)(2,1)}, u32[]{:S(2)}) %copy-start) | copy-done | bytes 262168
  1.6 0.0 copy-start.2
  1.6 0.9 %copy-done.2 = bf16[128,1024]{1,0:T(8,128)(2,1)S(1)} copy-done((bf16[128,1024]{1,0:T(8,128)(2,1)S(1)}, bf16[128,1024]{1,0:T(8,128)(2,1)}, u32[]{:S(2)}) %copy-start.2) | copy-done | bytes 262168
  2.5 0.0 copy-start.4
  2.5 0.9 %copy-done.4 = bf16[128,1024]{1,0:T(8,128)(2,1)S(1)} copy-done((bf16[128,1024]{1,0:T(8,128)(2,1)S(1)}, bf16[128,1024]{1,0:T(8,128)(2,1)}, u32[]{:S(2)}) %copy-start.4) | copy-done | bytes 262168
  3.5 0.0 copy-start.6
  3.5 0.9 %copy-done.6 = bf16[128,1024]{1,0:T(8,128)(2,1)S(1)} copy-done((bf16[128,1024]{1,0:T(8,128)(2,1)S(1)}, bf16[128,1024]{1,0:T(8,128)(2,1)}, u32[]{:S(2)}) %copy-start.6) | copy-done | bytes 262168
  4.4 0.0 copy-start.10
  4.4 0.9 %copy-done.10 = f32[3,7,1024]{2,1,0:T(8,128)S(1)} copy-done((f32[3,7,1024]{2,1,0:T(8,128)S(1)}, f32[3,7,1024]{2,1,0:T(8,128)}, u32[]{:S(2)}) %copy-start.10) | copy-done | bytes 86040
  5.3 1.9 %shard_map.130 = bf16[8,288,128]{2,1,0:T(8,128)(2,1)} custom-call(bf16[128,1024]{1,0:T(8,128)(2,1)S(1)} %copy-done, bf16[128,1024]{1,0:T(8,128)(2,1)S(1)} %copy-done.2, bf16[128,1024]{1,0:T(8,128)(2,1)S(1)} %copy-done.4, bf16[128,1024]{1,0:T(8,128)(2,1)S(1)} %copy-done.6, f32[3,7,1024]{2,1,0:T(8,128)S(1)} %copy-done.10), custom_call_target="tpu_custom_call" | custom-call | tf_op jit(solution)/shard_map/pallas_call | solution.py:452
  7.2 0.0 copy-start.8
  7.2 0.0 copy-start.14
  7.2 0.0 copy-start.15
  7.2 5.3 %all-to-all-start = ((bf16[8,288,128]{2,1,0:T(8,128)(2,1)}), bf16[8,288,128]{2,1,0:T(8,128)(2,1)S(1)}, u32[]{:S(2)}, u32[]{:S(2)}) async-start(bf16[8,288,128]{2,1,0:T(8,128)(2,1)} %shard_map.130), calls=%async_computation | async-start | bytes 1179648 | tf_op jit(solution)/shard_map/all_to_all | solution.py:479
  12.5 0.0 copy-done.8
  12.5 0.0 copy-done.14
  12.5 0.0 copy-done.15
  12.5 0.0 copy-start.11
  12.5 0.0 copy-start.9
  12.5 0.0 copy-start.12
  12.6 0.0 copy-start.13
  12.6 1.0 %shard_map.131.spec_h = f32[8,256,128]{2,1,0:T(8,128)S(1)} custom-call(f32[128,1024]{1,0:T(8,128)S(1)} %bitcast.1, bf16[256,256]{1,0:T(8,128)(2,1)S(1)} %copy-done.14, bf16[256,256]{1,0:T(8,128)(2,1)S(1)} %copy-done.15), custom_call_target="tpu_custom_call" | custom-call | tf_op jit(solution)/shard_map/pallas_call | solution.py:452
  13.5 0.0 copy-done.11
  13.6 9.4 %all-to-all-done.in_ref = bf16[8,288,128]{2,1,0:T(8,128)(2,1)S(1)} async-done(((bf16[8,288,128]{2,1,0:T(8,128)(2,1)}), bf16[8,288,128]{2,1,0:T(8,128)(2,1)S(1)}, u32[]{:S(2)}, u32[]{:S(2)}) %all-to-all-start) | async-done | bytes 589856 | tf_op jit(solution)/shard_map/all_to_all | solution.py:479
  22.9 0.0 copy-done.9
  22.9 0.0 copy-done.12
  22.9 0.0 copy-done.13
  22.9 3.2 %shard_map.132 = bf16[8,288,128]{2,1,0:T(8,128)(2,1)} custom-call(bf16[8,288,128]{2,1,0:T(8,128)(2,1)S(1)} %all-to-all-done.in_ref, f32[3,7,128]{2,1,0:T(8,128)S(1)} %constant_dynamic-slice_fusion.taps_ref, f32[8,256,128]{2,1,0:T(8,128)S(1)} %shard_map.131.spec_h, bf16[256,256]{1,0:T(8,128)(2,1)S(1)} %copy-done.9, bf16[128,256]{1,0:T(8,128)(2,1)S(1)} %copy-done.12, ...), custom_call_target="tpu_custom_call" | custom-call | tf_op jit(solution)/shard_map/pallas_call | solution.py:452
  26.1 3.5 %all-to-all-start.1 = ((bf16[8,288,128]{2,1,0:T(8,128)(2,1)}), bf16[8,288,128]{2,1,0:T(8,128)(2,1)S(1)}, u32[]{:S(2)}, u32[]{:S(2)}) async-start(bf16[8,288,128]{2,1,0:T(8,128)(2,1)} %shard_map.132), calls=%async_computation.1 | async-start | bytes 1179648 | tf_op jit(solution)/shard_map/all_to_all | solution.py:493
  29.7 0.0 copy-start.1
  29.7 0.0 copy-start.3
  29.7 0.0 copy-start.5
  29.7 0.0 copy-start.7
  29.7 2.7 %shard_map.134 = f32[1,128,1024]{2,1,0:T(8,128)} custom-call(bf16[8,288,128]{2,1,0:T(8,128)(2,1)S(1)} %all-to-all-done.in_ref, f32[3,7,128]{2,1,0:T(8,128)S(1)} %constant_dynamic-slice_fusion.taps_ref, bf16[256,256]{1,0:T(8,128)(2,1)S(1)} %copy-done.9, bf16[128,256]{1,0:T(8,128)(2,1)S(1)} %copy-done.12, bf16[128,256]{1,0:T(8,128)(2,1)S(1)} %copy-done.13), custom_call_target="tpu_custom_call" | custom-call | tf_op jit(solution)/shard_map/pallas_call | solution.py:452
  32.5 7.6 %all-to-all-done.1.in_ref = bf16[8,288,128]{2,1,0:T(8,128)(2,1)S(1)} async-done(((bf16[8,288,128]{2,1,0:T(8,128)(2,1)}), bf16[8,288,128]{2,1,0:T(8,128)(2,1)S(1)}, u32[]{:S(2)}, u32[]{:S(2)}) %all-to-all-start.1) | async-done | bytes 589856 | tf_op jit(solution)/shard_map/all_to_all | solution.py:493
  40.0 0.0 copy-done.1
  40.0 0.0 copy-done.3
  40.0 0.0 copy-done.5
  40.1 0.0 copy-done.7
  40.1 3.1 %shard_map.133 = (bf16[128,1024]{1,0:T(8,128)(2,1)}, bf16[3,128,1024]{2,1,0:T(8,128)(2,1)}) custom-call(bf16[128,1024]{1,0:T(8,128)(2,1)S(1)} %copy-done.1, bf16[128,1024]{1,0:T(8,128)(2,1)S(1)} %copy-done.3, bf16[128,1024]{1,0:T(8,128)(2,1)S(1)} %copy-done.5, bf16[128,1024]{1,0:T(8,128)(2,1)S(1)} %copy-done.7, f32[3,7,1024]{2,1,0:T(8,128)S(1)} %copy-done.11, ...), custom_call_target="tpu_custom_call" | custom-call | tf_op jit(solution)/shard_map/pallas_call | solution.py:452
  (1 shorter events, 0.0 us)
Async XLA Ops:
  0.6 1.0 %copy-start = (bf16[128,1024]{1,0:T(8,128)(2,1)S(1)}, bf16[128,1024]{1,0:T(8,128)(2,1)}, u32[]{:S(2)}) copy-start(bf16[128,1024]{1,0:T(8,128)(2,1)} %q_ref.3) | copy-start | bytes 786436
  1.6 0.9 %copy-start.2 = (bf16[128,1024]{1,0:T(8,128)(2,1)S(1)}, bf16[128,1024]{1,0:T(8,128)(2,1)}, u32[]{:S(2)}) copy-start(bf16[128,1024]{1,0:T(8,128)(2,1)} %k_ref.3) | copy-start | bytes 786436
  2.5 0.9 %copy-start.4 = (bf16[128,1024]{1,0:T(8,128)(2,1)S(1)}, bf16[128,1024]{1,0:T(8,128)(2,1)}, u32[]{:S(2)}) copy-start(bf16[128,1024]{1,0:T(8,128)(2,1)} %v_ref.3) | copy-start | bytes 786436
  3.5 0.9 %copy-start.6 = (bf16[128,1024]{1,0:T(8,128)(2,1)S(1)}, bf16[128,1024]{1,0:T(8,128)(2,1)}, u32[]{:S(2)}) copy-start(bf16[128,1024]{1,0:T(8,128)(2,1)} %g_ref.3) | copy-start | bytes 786436
  4.4 0.9 %copy-start.10 = (f32[3,7,1024]{2,1,0:T(8,128)S(1)}, f32[3,7,1024]{2,1,0:T(8,128)}, u32[]{:S(2)}) copy-start(f32[3,7,1024]{2,1,0:T(8,128)} %taps_ref.3) | copy-start | bytes 258052
  7.2 5.3 %copy-start.8 = (f32[1,128,1024]{2,1,0:T(8,128)S(1)}, f32[1,128,1024]{2,1,0:T(8,128)}, u32[]{:S(2)}) copy-start(f32[1,128,1024]{2,1,0:T(8,128)} %param.15) | copy-start | bytes 1572868
  7.2 5.3 %copy-start.14 = (bf16[256,256]{1,0:T(8,128)(2,1)S(1)}, bf16[256,256]{1,0:T(8,128)(2,1)}, u32[]{:S(2)}) copy-start(bf16[256,256]{1,0:T(8,128)(2,1)} %constant.22.clone.window_hi) | copy-start | bytes 393220
  7.2 5.3 %copy-start.15 = (bf16[256,256]{1,0:T(8,128)(2,1)S(1)}, bf16[256,256]{1,0:T(8,128)(2,1)}, u32[]{:S(2)}) copy-start(bf16[256,256]{1,0:T(8,128)(2,1)} %constant.23.clone.window_lo) | copy-start | bytes 393220
  7.2 15.7 %all-to-all-start = ((bf16[8,288,128]{2,1,0:T(8,128)(2,1)}), bf16[8,288,128]{2,1,0:T(8,128)(2,1)S(1)}, u32[]{:S(2)}, u32[]{:S(2)}) async-start(bf16[8,288,128]{2,1,0:T(8,128)(2,1)} %shard_map.130), calls=%async_computation | async-start | bytes 1179648 | tf_op jit(solution)/shard_map/all_to_all | solution.py:479
  12.5 1.0 %copy-start.11 = (f32[3,7,1024]{2,1,0:T(8,128)S(1)}, f32[3,7,1024]{2,1,0:T(8,128)}, u32[]{:S(2)}) copy-start(f32[3,7,1024]{2,1,0:T(8,128)} %taps_ref.3) | copy-start | bytes 258052
  12.5 10.4 %copy-start.9 = (bf16[256,256]{1,0:T(8,128)(2,1)S(1)}, bf16[256,256]{1,0:T(8,128)(2,1)}, u32[]{:S(2)}) copy-start(bf16[256,256]{1,0:T(8,128)(2,1)} %constant.24.clone.doubled) | copy-start | bytes 393220
  12.5 10.4 %copy-start.12 = (bf16[128,256]{1,0:T(8,128)(2,1)S(1)}, bf16[128,256]{1,0:T(8,128)(2,1)}, u32[]{:S(2)}) copy-start(bf16[128,256]{1,0:T(8,128)(2,1)} %constant.25.clone.inv_hi) | copy-start | bytes 196612
  12.6 10.4 %copy-start.13 = (bf16[128,256]{1,0:T(8,128)(2,1)S(1)}, bf16[128,256]{1,0:T(8,128)(2,1)}, u32[]{:S(2)}) copy-start(bf16[128,256]{1,0:T(8,128)(2,1)} %constant.26.clone.inv_lo) | copy-start | bytes 196612
  26.1 13.9 %all-to-all-start.1 = ((bf16[8,288,128]{2,1,0:T(8,128)(2,1)}), bf16[8,288,128]{2,1,0:T(8,128)(2,1)S(1)}, u32[]{:S(2)}, u32[]{:S(2)}) async-start(bf16[8,288,128]{2,1,0:T(8,128)(2,1)} %shard_map.132), calls=%async_computation.1 | async-start | bytes 1179648 | tf_op jit(solution)/shard_map/all_to_all | solution.py:493
  29.7 10.4 %copy-start.1 = (bf16[128,1024]{1,0:T(8,128)(2,1)S(1)}, bf16[128,1024]{1,0:T(8,128)(2,1)}, u32[]{:S(2)}) copy-start(bf16[128,1024]{1,0:T(8,128)(2,1)} %q_ref.3) | copy-start | bytes 786436
  29.7 10.4 %copy-start.3 = (bf16[128,1024]{1,0:T(8,128)(2,1)S(1)}, bf16[128,1024]{1,0:T(8,128)(2,1)}, u32[]{:S(2)}) copy-start(bf16[128,1024]{1,0:T(8,128)(2,1)} %k_ref.3) | copy-start | bytes 786436
  29.7 10.4 %copy-start.5 = (bf16[128,1024]{1,0:T(8,128)(2,1)S(1)}, bf16[128,1024]{1,0:T(8,128)(2,1)}, u32[]{:S(2)}) copy-start(bf16[128,1024]{1,0:T(8,128)(2,1)} %v_ref.3) | copy-start | bytes 786436
  29.7 10.4 %copy-start.7 = (bf16[128,1024]{1,0:T(8,128)(2,1)S(1)}, bf16[128,1024]{1,0:T(8,128)(2,1)}, u32[]{:S(2)}) copy-start(bf16[128,1024]{1,0:T(8,128)(2,1)} %g_ref.3) | copy-start | bytes 786436
where the time goes:
time: 43.6 us; the launch traced here: 43.1 us
  waiting for transfers between devices  17 us (39%)
  Pallas kernels  11.8 us (27%)
  starting transfers between devices  8.84 us (20%)
  local copies, waits for them, and re-layouts  4.76 us (11%)
  between operations  0.78 us (2%)
    pallas_call x5, Pallas kernels, in_vmem(): pl.pallas_call(kernel, out_shape=out_shape, in_specs=[whole] * len(args),...  11.8 us
    all_to_all x1, waiting for transfers between devices, block_shards(): lax.all_to_all(sent, 'context', split_axis=0, concat_axis=0, tiled=True)  9.36 us
    all_to_all x1, waiting for transfers between devices, block_shards(): lax.all_to_all(results, 'context', split_axis=0, concat_axis=0, tiled=True)  7.59 us
    all_to_all x1, starting transfers between devices, block_shards(): lax.all_to_all(sent, 'context', split_axis=0, concat_axis=0, tiled=True)  5.3 us
    unnamed x32, local copies, waits for them, and re-layouts  4.75 us
    all_to_all x1, starting transfers between devices, block_shards(): lax.all_to_all(results, 'context', split_axis=0, concat_axis=0, tiled=True)  3.54 us
  transfers between devices with their start and end apart: 2, of which 2 were waited for; matrix products, arithmetic and copies ran while one was open for 0% of the time, Pallas kernels for 9%

commit v1 on v0

--- a/solution.py
+++ b/solution.py
@@ -202,46 +202,91 @@
     return running
 
 
-def send_kernel(q_ref, k_ref, v_ref, g_ref, taps_ref, out_ref, padded, extra):
+def send_kernel(order, q_ref, k_ref, v_ref, g_ref, taps_ref, h_ref, hi_ref, lo_ref, *refs):
+    count = len(order)
+    outs = refs[:count]
+    filtered_ref, own_ref, h_here, hi_here, lo_here = refs[count : count + 5]
+    landed, taps, padded, extra, arrivals, kept = refs[count + 5 :]
+    me = lax.axis_index("context")
     rows = q_ref.shape[0]
     halo = taps_ref.shape[1] - 1
-    groups = out_ref.shape[0]
-    padded[:, pl.ds(0, 8), :] = jnp.zeros((3, 8, LANES), jnp.float32)
-    extra[...] = jnp.zeros(extra.shape, jnp.float32)
-
-    def body(group, carry):
-        lanes = pl.ds(pl.multiple_of(group * LANES, LANES), LANES)
+
+    def lanes_of(place):
+        return pl.ds(pl.multiple_of((me ^ order[place]) * LANES, LANES), LANES)
+
+    def fetches(place):
+        lanes = lanes_of(place)
+        copies = [
+            pltpu.make_async_copy(
+                taps_ref.at[:, :, lanes], taps.at[place], arrivals.at[place, 4]
+            )
+        ]
+        for which, ref in enumerate((q_ref, k_ref, v_ref, g_ref)):
+            copies.append(
+                pltpu.make_async_copy(
+                    ref.at[:, lanes], landed.at[place, which], arrivals.at[place, which]
+                )
+            )
+        return copies
+
+    keeps = [
+        pltpu.make_async_copy(source, target, kept.at[index])
+        for index, (source, target) in enumerate(
+            ((h_ref, h_here), (hi_ref, hi_here), (lo_ref, lo_here))
+        )
+    ]
+    for place in range(count):
+        for copy in fetches(place):
+            copy.start()
+    for copy in keeps:
+        copy.start()
+    for place in range(count):
+        slot = place % padded.shape[0]
+        out_ref = outs[place]
+        padded[slot, :, pl.ds(0, 8), :] = jnp.zeros((3, 8, LANES), jnp.float32)
+        extra[slot, pl.ds(5 * halo, extra.shape[1] - 5 * halo), :] = jnp.zeros(
+            (extra.shape[1] - 5 * halo, LANES), jnp.float32
+        )
+        for copy in fetches(place):
+            copy.wait()
         filtered = []
-        for which, ref in enumerate((q_ref, k_ref, v_ref)):
-            padded[which, pl.ds(8, rows), :] = ref[:, lanes].astype(jnp.float32)
-            filtered.append(short_filter(padded.at[which], rows, tap_rows(taps_ref, which, lanes)))
+        for which in range(3):
+            padded[slot, which, pl.ds(8, rows), :] = landed[place, which].astype(jnp.float32)
+            weights = tap_rows(taps.at[place], which, pl.ds(0, LANES))
+            result = short_filter(padded.at[slot, which], rows, weights)
+            filtered_ref[which, place] = result
+            filtered.append(result)
         query_f, key_f, value_f = filtered
-        cotangent = g_ref[:, lanes].astype(jnp.float32)
-        gated = head_rows(padded[1, pl.ds(8, 8), :], key_f * value_f, halo)
+        cotangent = landed[place, 3].astype(jnp.float32)
+        gated = head_rows(padded[slot, 1, pl.ds(8, 8), :], key_f * value_f, halo)
         grad_long = head_rows(cotangent[:8], cotangent * query_f, halo)
-        out_ref[group, pl.ds(0, rows), :] = gated.astype(jnp.bfloat16)
-        out_ref[group, pl.ds(rows, rows), :] = grad_long.astype(jnp.bfloat16)
+        out_ref[pl.ds(0, rows), :] = gated.astype(jnp.bfloat16)
+        out_ref[pl.ds(rows, rows), :] = grad_long.astype(jnp.bfloat16)
         pieces = ((1, rows - halo), (2, 0), (2, rows - halo), (0, 0), (0, rows - halo))
-        for place, (which, first) in enumerate(pieces):
-            extra[pl.ds(place * halo, halo), :] = padded[which, pl.ds(8 + first, halo), :]
-        out_ref[group, pl.ds(2 * rows, extra.shape[0]), :] = extra[...].astype(jnp.bfloat16)
-        return carry
-
-    lax.fori_loop(0, groups, body, 0)
-
-
-def repair_heads(in_ref, taps_ref, edges, joined, rows):
-    blocks = in_ref.shape[0]
+        for position, (which, first) in enumerate(pieces):
+            extra[slot, pl.ds(position * halo, halo), :] = padded[slot, which, pl.ds(8 + first, halo), :]
+        out_ref[pl.ds(2 * rows, extra.shape[1]), :] = extra[slot].astype(jnp.bfloat16)
+    own_ref[...] = taps[order.index(0)]
+    for copy in keeps:
+        copy.wait()
+
+
+def gather_heads(order, in_refs, edges, firsts, rows):
+    me = lax.axis_index("context")
+    for mask, in_ref in zip(order, in_refs):
+        block = me ^ mask
+        edges[block] = in_ref[pl.ds(2 * rows, edges.shape[1]), :].astype(jnp.float32)
+        firsts[block, 0] = in_ref[pl.ds(0, 16), :].astype(jnp.float32)[:8]
+        firsts[block, 1] = in_ref[pl.ds(rows, 16), :].astype(jnp.float32)[:8]
+
+
+def repair_heads(taps_ref, edges, firsts, joined, heads):
+    blocks = edges.shape[0]
     span = taps_ref.shape[1]
     halo = span - 1
     joined[...] = jnp.zeros(joined.shape, jnp.float32)
     for block in range(blocks):
-        edges[block] = in_ref[block, pl.ds(2 * rows, edges.shape[1]), :].astype(jnp.float32)
-    heads = []
-    for block in range(blocks):
-        key_head = in_ref[block, pl.ds(0, 16), :].astype(jnp.float32)
-        grad_head = in_ref[block, pl.ds(rows, 16), :].astype(jnp.float32)[:8]
-        joined[1, block, pl.ds(halo, 8), :] = key_head[:8]
+        joined[1, block, pl.ds(halo, 8), :] = firsts[block, 0]
         joined[2, block, pl.ds(halo, halo), :] = edges[block, pl.ds(halo, halo), :]
         joined[0, block, pl.ds(halo, halo), :] = edges[block, pl.ds(3 * halo, halo), :]
         if block > 0:
@@ -254,19 +299,22 @@
                 weight = taps_ref[which, pl.ds(offset, 1), :]
                 running = running + weight * joined[which, block, pl.ds(halo - offset, 8), :]
             filtered.append(running)
-        heads.append((filtered[0], filtered[1], filtered[2], grad_head))
-    return heads
-
-
-def to_spectra(in_ref, heads, doubled, spec_x, spec_g, rows, halo):
-    for block, (query_f, key_f, value_f, cotangent) in enumerate(heads):
+            heads[block, which] = running
+        cotangent = firsts[block, 1]
+        heads[block, 3] = cotangent
+        heads[block, 4] = filtered[1] * filtered[2]
+        heads[block, 5] = cotangent * filtered[0]
+
+
+def to_spectra(order, in_refs, heads, doubled, spec_x, spec_g, rows, halo):
+    me = lax.axis_index("context")
+    for mask, in_ref in zip(order, in_refs):
+        block = me ^ mask
         parts = []
-        for first, fresh in ((0, key_f * value_f), (rows, cotangent * query_f)):
-            head = in_ref[block, pl.ds(first, 16), :].astype(jnp.float32)
-            head = head_rows(fresh, head, halo).astype(jnp.bfloat16)
-            parts.append(
-                jnp.concatenate([head, in_ref[block, pl.ds(first + 16, rows - 16), :]], axis=0)
-            )
+        for first, place in ((0, 4), (rows, 5)):
+            head = in_ref[pl.ds(first, 16), :].astype(jnp.float32)
+            head = head_rows(heads[block, place], head, halo).astype(jnp.bfloat16)
+            parts.append(jnp.concatenate([head, in_ref[pl.ds(first + 16, rows - 16), :]], axis=0))
         pair = jnp.concatenate(parts, axis=1)
         spectrum = jnp.dot(
             doubled, jnp.concatenate([pair, pair], axis=0), preferred_element_type=jnp.float32
@@ -275,7 +323,8 @@
         spec_g[block] = spectrum[:, LANES:]
 
 
-def filter_kernel(h_ref, window_hi, window_lo, out_ref):
+def filter_kernel(parcel_ref, h_ref, window_hi, window_lo, out_ref):
+    del parcel_ref
     blocks, two_rows, _ = out_ref.shape
     rows = two_rows // 2
     for block in range(blocks):
@@ -338,125 +387,147 @@
         ref[index, pl.ds(pl.multiple_of(bins + tile * 8, 8), 8), lanes] = imag
 
 
-def convolve_kernel(
-    in_ref, taps_ref, spec_h, doubled, inv_hi, inv_lo, out_ref,
-    edges, joined, spec_x, spec_g, spec_y, extra,
-):
-    blocks = in_ref.shape[0]
+def convolve_kernel(order, taps_ref, spec_h, doubled, inv_hi, inv_lo, *refs):
+    count = len(order)
+    in_refs, out_refs = refs[:count], refs[count : 2 * count]
+    spec_x, spec_g, edges, firsts, joined, heads, spec_y, extra = refs[2 * count :]
+    me = lax.axis_index("context")
     rows = inv_hi.shape[0]
     halo = taps_ref.shape[1] - 1
-    heads = repair_heads(in_ref, taps_ref, edges, joined, rows)
-    to_spectra(in_ref, heads, doubled[...], spec_x, spec_g, rows, halo)
+    gather_heads(order, in_refs, edges, firsts, rows)
+    repair_heads(taps_ref, edges, firsts, joined, heads)
+    to_spectra(order, in_refs, heads, doubled[...], spec_x, spec_g, rows, halo)
 
     def body(tile, carry):
-        filt = load_tile(spec_h, blocks, tile, rows)
-        sums = [[(i - j, j) for j in range(i + 1)] for i in range(blocks)]
-        store_tile(spec_y, 0, mixed_products(filt, load_tile(spec_x, blocks, tile, rows), sums, False), tile, rows)
-        sums = [[(j - i, j) for j in range(i, blocks)] for i in range(blocks)]
-        store_tile(spec_y, LANES, mixed_products(filt, load_tile(spec_g, blocks, tile, rows), sums, True), tile, rows)
+        filt = load_tile(spec_h, count, tile, rows)
+        sums = [[(i - j, j) for j in range(i + 1)] for i in range(count)]
+        results = mixed_products(filt, load_tile(spec_x, count, tile, rows), sums, False)
+        store_tile(spec_y, 0, results, tile, rows)
+        sums = [[(j - i, j) for j in range(i, count)] for i in range(count)]
+        results = mixed_products(filt, load_tile(spec_g, count, tile, rows), sums, True)
+        store_tile(spec_y, LANES, results, tile, rows)
         return carry
 
     lax.fori_loop(0, rows // 8, body, 0)
     extra[...] = jnp.zeros(extra.shape, jnp.float32)
-    for block, (query_f, key_f, value_f, cotangent) in enumerate(heads):
-        both = back_to_rows(spec_y[block], inv_hi[...], inv_lo[...])
-        both = both.astype(jnp.bfloat16)
-        out_ref[block, pl.ds(0, rows), :] = both[:, :LANES]
+    for mask, out_ref in zip(order, out_refs):
+        block = me ^ mask
+        query_f, key_f, value_f, cotangent = [heads[block, which] for which in range(4)]
+        both = back_to_rows(spec_y[block], inv_hi[...], inv_lo[...]).astype(jnp.bfloat16)
+        out_ref[pl.ds(0, rows), :] = both[:, :LANES]
         head = both[:16].astype(jnp.float32)
         long_head, back_head = head[:8, :LANES], head[:8, LANES:]
-        grad_key = back_head * value_f
-        back = jnp.concatenate([head_rows(grad_key, head[:, LANES:], halo).astype(jnp.bfloat16), both[16:, LANES:]], axis=0)
-        out_ref[block, pl.ds(rows, rows), :] = back
-        grad_value = back_head * key_f
+        grad_key, grad_value = back_head * value_f, back_head * key_f
+        back = head_rows(grad_key, head[:, LANES:], halo).astype(jnp.bfloat16)
+        out_ref[pl.ds(rows, rows), :] = jnp.concatenate([back, both[16:, LANES:]], axis=0)
         own = (query_f * long_head, grad_value)
         following = (cotangent * long_head, grad_key, grad_value)
         for place, value in enumerate(own):
-            extra[block, pl.ds(place * halo, halo), :] = value[:halo]
-        if block > 0:
-            for place, value in enumerate(following):
-                extra[block - 1, pl.ds((2 + place) * halo, halo), :] = value[:halo]
-    for block in range(blocks):
-        out_ref[block, pl.ds(2 * rows, extra.shape[1]), :] = extra[block].astype(jnp.bfloat16)
-
-
-def correlate_kernel(
-    scale, in_ref, taps_ref, doubled, inv_hi, inv_lo, out_ref, edges, joined, spec_x, spec_g, spec_y
-):
-    blocks = in_ref.shape[0]
+            extra[block + 1, pl.ds(place * halo, halo), :] = value[:halo]
+        for place, value in enumerate(following):
+            extra[block, pl.ds((2 + place) * halo, halo), :] = value[:halo]
+    for mask, out_ref in zip(order, out_refs):
+        block = me ^ mask
+        out_ref[pl.ds(2 * rows, extra.shape[1]), :] = extra[block + 1].astype(jnp.bfloat16)
+
+
+def correlate_kernel(scale, spec_x, spec_g, inv_hi, inv_lo, out_ref, spec_y):
+    count = spec_x.shape[0]
     rows = inv_hi.shape[0]
-    halo = taps_ref.shape[1] - 1
-    heads = repair_heads(in_ref, taps_ref, edges, joined, rows)
-    to_spectra(in_ref, heads, doubled[...], spec_x, spec_g, rows, halo)
 
     def body(tile, carry):
-        real, imag = load_tile(spec_x, blocks, tile, rows)
+        real, imag = load_tile(spec_x, count, tile, rows)
         row = lax.broadcasted_iota(jnp.int32, (8, LANES), 0)
         sign = jnp.where(row % 2 == 0, 1.0, -1.0)
-        window_re = [real[0]] + [real[i] - sign * imag[i - 1] for i in range(1, blocks)]
-        window_im = [imag[0]] + [imag[i] + sign * real[i - 1] for i in range(1, blocks)]
-        sums = [[(j - lag, j) for j in range(lag, blocks)] for lag in range(blocks)]
-        results = mixed_products((window_re, window_im), load_tile(spec_g, blocks, tile, rows), sums, True)
+        window_re = [real[0]] + [real[i] - sign * imag[i - 1] for i in range(1, count)]
+        window_im = [imag[0]] + [imag[i] + sign * real[i - 1] for i in range(1, count)]
+        sums = [[(j - lag, j) for j in range(lag, count)] for lag in range(count)]
+        results = mixed_products((window_re, window_im), load_tile(spec_g, count, tile, rows), sums, True)
         store_tile(spec_y, 0, results, tile, rows)
         return carry
 
     lax.fori_loop(0, rows // 8, body, 0)
-    for block in range(blocks):
+    for block in range(count):
         result = back_to_rows(spec_y[block], inv_hi[...], inv_lo[...])
         out_ref[0, :, pl.ds(block * rows, rows)] = result.T * scale
 
 
-def receive_kernel(q_ref, k_ref, v_ref, g_ref, taps_ref, in_ref, mixed_ref, grads_ref, padded, extra):
-    rows = q_ref.shape[0]
+def receive_kernel(places, order, g_ref, taps_ref, filtered_ref, *refs):
+    count = len(places)
+    in_refs = refs[:count]
+    mixed_ref, grads_ref, padded, extra, leaving, departures = refs[-6:]
+    me = lax.axis_index("context")
+    rows = g_ref.shape[0]
     span = taps_ref.shape[1]
     halo = span - 1
-    groups = in_ref.shape[0]
-    for which in range(3):
-        padded[which, pl.ds(0, 8), :] = jnp.zeros((8, LANES), jnp.float32)
-        padded[which, pl.ds(rows, 16), :] = jnp.zeros((16, LANES), jnp.float32)
-
-    def body(group, carry):
-        lanes = pl.ds(pl.multiple_of(group * LANES, LANES), LANES)
-        filtered = []
-        for which, ref in enumerate((q_ref, k_ref, v_ref)):
-            padded[which, pl.ds(0, 8), :] = jnp.zeros((8, LANES), jnp.float32)
-            padded[which, pl.ds(8, rows), :] = ref[:, lanes].astype(jnp.float32)
-            filtered.append(short_filter(padded.at[which], rows, tap_rows(taps_ref, which, lanes)))
-        query_f, key_f, value_f = filtered
+    copies = []
+    for index, (place, in_ref) in enumerate(zip(places, in_refs)):
+        lanes = pl.ds(pl.multiple_of((me ^ order[place]) * LANES, LANES), LANES)
+        slot = index % padded.shape[0]
+        edge_rows = in_ref.shape[0] - 2 * rows
+        query_f, key_f, value_f = [filtered_ref[which, place] for which in range(3)]
         cotangent = g_ref[:, lanes].astype(jnp.float32)
-        long_conv = in_ref[group, pl.ds(0, rows), :].astype(jnp.float32)
-        back = in_ref[group, pl.ds(rows, rows), :].astype(jnp.float32)
-        extra[pl.ds(0, in_ref.shape[1] - 2 * rows), :] = in_ref[group, pl.ds(2 * rows, in_ref.shape[1] - 2 * rows), :].astype(jnp.float32)
-        mixed = head_rows(extra[pl.ds(0, 8), :], query_f * long_conv, halo)
-        mixed_ref[:, lanes] = mixed.astype(jnp.bfloat16)
+        long_conv = in_ref[pl.ds(0, rows), :].astype(jnp.float32)
+        back = in_ref[pl.ds(rows, rows), :].astype(jnp.float32)
+        extra[slot, pl.ds(0, edge_rows), :] = in_ref[pl.ds(2 * rows, edge_rows), :].astype(jnp.float32)
+        mixed = head_rows(extra[slot, pl.ds(0, 8), :], query_f * long_conv, halo)
+        leaving[index, 3] = mixed.astype(jnp.bfloat16)
+        copies.append(
+            pltpu.make_async_copy(leaving.at[index, 3], mixed_ref.at[:, lanes], departures.at[index, 3])
+        )
+        copies[-1].start()
         grads = (
             cotangent * long_conv,
             head_rows(back[:8], back * value_f, halo),
-            head_rows(extra[pl.ds(halo, 8), :], back * key_f, halo),
+            head_rows(extra[slot, pl.ds(halo, 8), :], back * key_f, halo),
         )
         for which, grad in enumerate(grads):
-            padded[which, pl.ds(0, rows), :] = grad.astype(jnp.bfloat16).astype(jnp.float32)
-            padded[which, pl.ds(rows, halo), :] = extra[pl.ds((2 + which) * halo, halo), :]
+            padded[slot, which, pl.ds(0, rows), :] = grad.astype(jnp.bfloat16).astype(jnp.float32)
+            padded[slot, which, pl.ds(rows, halo), :] = extra[slot, pl.ds((2 + which) * halo, halo), :]
             weights = tap_rows(taps_ref, which, lanes)
-            running = weights[0] * padded[which, pl.ds(0, rows), :]
+            running = weights[0] * padded[slot, which, pl.ds(0, rows), :]
             for offset in range(1, span):
-                running = running + weights[offset] * padded[which, pl.ds(offset, rows), :]
-            grads_ref[which, :, lanes] = running.astype(jnp.bfloat16)
-        return carry
-
-    lax.fori_loop(0, groups, body, 0)
-
-
-def in_vmem(kernel, out_shape, scratch, args):
+                running = running + weights[offset] * padded[slot, which, pl.ds(offset, rows), :]
+            leaving[index, which] = running.astype(jnp.bfloat16)
+            copies.append(
+                pltpu.make_async_copy(
+                    leaving.at[index, which], grads_ref.at[which, :, lanes], departures.at[index, which]
+                )
+            )
+            copies[-1].start()
+    for copy in copies:
+        copy.wait()
+
+
+def on_device(kernel, out_shape, scratch, args, in_hbm=0, pin=True, updated=0):
     whole = pl.BlockSpec(memory_space=pltpu.VMEM)
-    single = not isinstance(out_shape, tuple)
+    outside = pl.BlockSpec(memory_space=pltpu.HBM if pin else pl.ANY)
+    last = len(args) - updated
+    args = [
+        pltpu.with_memory_space_constraint(arg, pltpu.HBM) if pin and place < in_hbm else arg
+        for place, arg in enumerate(args)
+    ]
     return pl.pallas_call(
         kernel,
         out_shape=out_shape,
-        in_specs=[whole] * len(args),
-        out_specs=whole if single else (whole,) * len(out_shape),
-        scratch_shapes=[pltpu.VMEM(shape, jnp.float32) for shape in scratch],
+        in_specs=[outside if place < in_hbm or place >= last else whole for place in range(len(args))],
+        out_specs=jax.tree.map(
+            lambda out: whole if isinstance(out, jax.ShapeDtypeStruct) else outside, out_shape
+        ),
+        input_output_aliases={last + place: place for place in range(updated)},
+        scratch_shapes=[
+            pltpu.VMEM(shape, jnp.float32) if isinstance(shape, tuple) else shape for shape in scratch
+        ],
         compiler_params=pltpu.CompilerParams(vmem_limit_bytes=VMEM_BYTES),
     )(*args)
+
+
+def exchange(order, parcels):
+    count = lax.axis_size("context")
+    return [
+        parcel if mask == 0 else lax.ppermute(parcel, "context", [(i, i ^ mask) for i in range(count)])
+        for mask, parcel in zip(order, parcels)
+    ]
 
 
 def block_shards(query_proj, key_proj, value_proj, short_taps, long_filter, grad_mixed):
@@ -466,53 +537,88 @@
     seq_len = rows * blocks
     window_hi, window_lo, doubled, inv_hi, inv_lo = [jnp.asarray(t) for t in block_tables(rows)]
     edge_rows = round_up(5 * halo, 16)
-    parcel = jax.ShapeDtypeStruct((blocks, 2 * rows + edge_rows, LANES), jnp.bfloat16)
+    order = sorted(range(blocks), key=lambda mask: (mask == 0, -(mask >> 1).bit_count()))
+    parcels = [jax.ShapeDtypeStruct((2 * rows + edge_rows, LANES), jnp.bfloat16)] * blocks
     spectra = (blocks, 2 * rows, LANES)
-    own = lax.dynamic_slice_in_dim(short_taps, lax.axis_index("context") * LANES, LANES, axis=2)
-
-    sent = in_vmem(
-        send_kernel,
-        parcel,
-        [(3, rows + 8, LANES), (edge_rows, LANES)],
-        (query_proj, key_proj, value_proj, grad_mixed, short_taps),
-    )
-    arrived = lax.all_to_all(sent, "context", split_axis=0, concat_axis=0, tiled=True)
-    spec_h = in_vmem(
+    own_taps = (*short_taps.shape[:2], LANES)
+    kept = (long_filter[0], window_hi, window_lo)
+
+    *sent, filtered, own, filter_here, hi_here, lo_here = on_device(
+        functools.partial(send_kernel, order),
+        parcels
+        + [
+            jax.ShapeDtypeStruct((3, blocks, rows, LANES), jnp.float32),
+            jax.ShapeDtypeStruct(own_taps, jnp.float32),
+        ]
+        + [jax.ShapeDtypeStruct(value.shape, value.dtype) for value in kept],
+        [
+            pltpu.VMEM((blocks, 4, rows, LANES), jnp.bfloat16),
+            (blocks, *own_taps),
+            (2, 3, rows + 8, LANES),
+            (2, edge_rows, LANES),
+            pltpu.SemaphoreType.DMA((blocks, 5)),
+            pltpu.SemaphoreType.DMA((len(kept),)),
+        ],
+        (query_proj, key_proj, value_proj, grad_mixed, short_taps, *kept),
+        in_hbm=8,
+    )
+    arrived = exchange(order, sent)
+    spec_h = on_device(
         filter_kernel,
         jax.ShapeDtypeStruct(spectra, jnp.float32),
         [],
-        (long_filter[0], window_hi, window_lo),
-    )
-    repair = [(blocks, edge_rows, LANES), (3, blocks, 24, LANES)]
-    results = in_vmem(
-        convolve_kernel,
-        parcel,
-        repair + [spectra, spectra, (blocks, 2 * rows, 2 * LANES), (blocks, edge_rows, LANES)],
-        (arrived, own, spec_h, doubled, inv_hi, inv_lo),
-    )
-    returned = lax.all_to_all(results, "context", split_axis=0, concat_axis=0, tiled=True)
-    filter_grad = in_vmem(
+        (arrived[2], filter_here, hi_here, lo_here),
+        in_hbm=1,
+        pin=False,
+    )
+    *results, spec_x, spec_g = on_device(
+        functools.partial(convolve_kernel, order),
+        parcels + [jax.ShapeDtypeStruct(spectra, jnp.float32)] * 2,
+        [
+            (blocks, edge_rows, LANES),
+            (blocks, 2, 8, LANES),
+            (3, blocks, 24, LANES),
+            (blocks, 6, 8, LANES),
+            (blocks, 2 * rows, 2 * LANES),
+            (blocks + 1, edge_rows, LANES),
+        ],
+        (own, spec_h, doubled, inv_hi, inv_lo, *arrived),
+    )
+    returned = exchange(order, results)
+    filter_grad = on_device(
         functools.partial(correlate_kernel, 1.0 / math.sqrt(seq_len)),
         jax.ShapeDtypeStruct(long_filter.shape, jnp.float32),
-        repair + [spectra, spectra, spectra],
-        (arrived, own, doubled, inv_hi, inv_lo),
-    )
-    mixed_out, input_grads = in_vmem(
-        receive_kernel,
-        (
-            jax.ShapeDtypeStruct((rows, channels), jnp.bfloat16),
-            jax.ShapeDtypeStruct((3, rows, channels), jnp.bfloat16),
-        ),
-        [(3, rows + 16, LANES), (edge_rows + 8, LANES)],
-        (query_proj, key_proj, value_proj, grad_mixed, short_taps, returned),
-    )
+        [spectra],
+        (spec_x, spec_g, inv_hi, inv_lo),
+    )
+    finished = ()
+    halves = (range(blocks // 2), range(blocks // 2, blocks))
+    for places in halves:
+        finished = on_device(
+            functools.partial(receive_kernel, places, order),
+            (
+                pltpu.HBM((rows, channels), jnp.bfloat16),
+                pltpu.HBM((3, rows, channels), jnp.bfloat16),
+            ),
+            [
+                (2, 3, rows + 16, LANES),
+                (2, edge_rows + 8, LANES),
+                pltpu.VMEM((len(places), 4, rows, LANES), jnp.bfloat16),
+                pltpu.SemaphoreType.DMA((len(places), 4)),
+            ],
+            (grad_mixed, short_taps, filtered, *(returned[place] for place in places), *finished),
+            updated=len(finished),
+        )
+    mixed_out, input_grads = finished
     return (mixed_out, input_grads, filter_grad)
 
 
 def shards(query_proj, key_proj, value_proj, short_taps, long_filter, grad_mixed):
     rows, channels = query_proj.shape
     halo = short_taps.shape[1] - 1
-    fits = channels == lax.axis_size("context") * LANES and rows % 128 == 0 and halo <= 8
+    blocks = lax.axis_size("context")
+    power_of_two = blocks & (blocks - 1) == 0
+    fits = power_of_two and channels == blocks * LANES and rows % 128 == 0 and halo <= 8
     chosen = block_shards if fits else general_shards
     return chosen(query_proj, key_proj, value_proj, short_taps, long_filter, grad_mixed)
 

time: 43.6 us -> 30.8 us (0.71)
  waiting for transfers between devices: 17 us -> 5.82 us
  local copies, waits for them, and re-layouts: 4.76 us -> 0.03 us
  starting transfers between devices: 8.84 us -> 13.3 us
  Pallas kernels: 11.8 us -> 10.6 us
    all_to_all x2 -> x0, waiting for transfers between devices: 17 us -> none  [the longest x1 9.36 us: block_shards(): lax.all_to_all(sent, 'context', split_axis=0, concat_axis=0, tiled=True)]
    ppermute x0 -> x14, starting transfers between devices: none -> 13.3 us  [exchange(): lax.ppermute(parcel, 'context', [(i, i ^ mask) for i in range(count)])]
    all_to_all x2 -> x0, starting transfers between devices: 8.84 us -> none  [the longest x1 5.3 us: block_shards(): lax.all_to_all(sent, 'context', split_axis=0, concat_axis=0, tiled=True)]
    ppermute x0 -> x14, waiting for transfers between devices: none -> 5.82 us  [exchange(): lax.ppermute(parcel, 'context', [(i, i ^ mask) for i in range(count)])]
    unnamed x32 -> x10, local copies, waits for them, and re-layouts: 4.75 us -> 0.03 us
    pallas_call x5 -> x6, Pallas kernels: 11.8 us -> 10.6 us  [on_device(): pl.pallas_call(kernel, out_shape=out_shape, in_specs=[outside if place <...]
  transfers between devices with their start and end apart: 2 -> 14, of which waited for: 2 -> 6; matrix products, arithmetic and copies ran while one was open for 0% -> 0% of each run, Pallas kernels for 9% -> 15%
where the time goes in v1:
time: 30.8 us; the launch traced here: 30.5 us
  starting transfers between devices  13.3 us (43%)
  Pallas kernels  10.6 us (34%)
  waiting for transfers between devices  5.82 us (19%)
  between operations  0.75 us (2%)
    ppermute x14, starting transfers between devices, exchange(): lax.ppermute(parcel, 'context', [(i, i ^ mask) for i in range(count)])  13.3 us
    pallas_call x6, Pallas kernels, on_device(): pl.pallas_call(kernel, out_shape=out_shape, in_specs=[outside if place <...  10.6 us
    ppermute x14, waiting for transfers between devices, exchange(): lax.ppermute(parcel, 'context', [(i, i ^ mask) for i in range(count)])  5.82 us
  transfers between devices with their start and end apart: 14, of which 6 were waited for; matrix products, arithmetic and copies ran while one was open for 0% of the time, Pallas kernels for 15%

profile of v1, /device:TPU:0, one launch (start us, length us, event | category | flops | bytes accessed | tf_op | source)
XLA Modules:
  0.0 30.5 jit_solution(4193957704329194768)
XLA Ops:
  0.6 0.0 copy-start.2
  0.6 0.0 copy-start.3
  0.7 0.0 copy-start.4
  0.7 2.3 %shard_map.130 = (bf16[288,128]{1,0:T(8,128)(2,1)S(1)}, bf16[288,128]{1,0:T(8,128)(2,1)S(1)}, bf16[288,128]{1,0:T(8,128)(2,1)S(1)}, bf16[288,128]{1,0:T(8,128)(2...) custom-call(bf16[128,1024]{1,0:T(8,128)(2,1)} %q_ref.1, ...), custom_call_target="tpu_custom_call" | custom-call | tf_op jit(solution)/shard_map/pallas_call | solution.py:510
  3.0 3.0 %collective-permute-start = (bf16[288,128]{1,0:T(8,128)(2,1)S(1)}, bf16[288,128]{1,0:T(8,128)(2,1)S(1)}, u32[]{:S(2)}, u32[]{:S(2)}) collective-permute-start(bf16[288,128]{1,0:T(8,128)(2,1)S(1)} %get-tuple-element.32), channel_id=1, source_target_pairs={{0,8},{4,12},{8,0},{12,4},{16,24},{20,28},{24,16},{28,20},{1,9},{5... | collective-permute-start | bytes 221192 | tf_op jit(solution)/shard_map/ppermute | solution.py:528
  6.0 1.5 %collective-permute-start.1 = (bf16[288,128]{1,0:T(8,128)(2,1)S(1)}, bf16[288,128]{1,0:T(8,128)(2,1)S(1)}, u32[]{:S(2)}, u32[]{:S(2)}) collective-permute-start(bf16[288,128]{1,0:T(8,128)(2,1)S(1)} %get-tuple-element.36), channel_id=1, source_target_pairs={{0,24},{4,28},{8,16},{12,20},{16,8},{20,12},{24,0},{28,4},{1,25},{... | collective-permute-start | bytes 221192 | tf_op jit(solution)/shard_map/ppermute | solution.py:528
  7.5 0.3 %collective-permute-start.2 = (bf16[288,128]{1,0:T(8,128)(2,1)S(1)}, bf16[288,128]{1,0:T(8,128)(2,1)S(1)}, u32[]{:S(2)}, u32[]{:S(2)}) collective-permute-start(bf16[288,128]{1,0:T(8,128)(2,1)S(1)} %get-tuple-element.37), channel_id=1, source_target_pairs={{0,28},{4,24},{8,20},{12,16},{16,12},{20,8},{24,4},{28,0},{1,29},{... | collective-permute-start | bytes 221192 | tf_op jit(solution)/shard_map/ppermute | solution.py:528
  7.8 0.9 %collective-permute-start.3 = (bf16[288,128]{1,0:T(8,128)(2,1)S(1)}, bf16[288,128]{1,0:T(8,128)(2,1)S(1)}, u32[]{:S(2)}, u32[]{:S(2)}) collective-permute-start(bf16[288,128]{1,0:T(8,128)(2,1)S(1)} %get-tuple-element.38), channel_id=1, source_target_pairs={{0,12},{4,8},{8,4},{12,0},{16,28},{20,24},{24,20},{28,16},{1,13},{... | collective-permute-start | bytes 221192 | tf_op jit(solution)/shard_map/ppermute | solution.py:528
  8.7 2.0 %collective-permute-start.4 = (bf16[288,128]{1,0:T(8,128)(2,1)S(1)}, bf16[288,128]{1,0:T(8,128)(2,1)S(1)}, u32[]{:S(2)}, u32[]{:S(2)}) collective-permute-start(bf16[288,128]{1,0:T(8,128)(2,1)S(1)} %get-tuple-element.39), channel_id=1, source_target_pairs={{0,16},{4,20},{8,24},{12,28},{16,0},{20,4},{24,8},{28,12},{1,17},{... | collective-permute-start | bytes 221192 | tf_op jit(solution)/shard_map/ppermute | solution.py:528
  10.7 0.0 collective-permute-done.parcel_ref.refs_2_
  10.7 0.0 collective-permute-start.5
  10.7 0.7 %collective-permute-done.1.refs_0_ = bf16[288,128]{1,0:T(8,128)(2,1)S(1)} collective-permute-done((bf16[288,128]{1,0:T(8,128)(2,1)S(1)}, bf16[288,128]{1,0:T(8,128)(2,1)S(1)}, u32[]{:S(2)}, u32[]{:S(2)}) %collective-permute-start.1) | collective-permute-done | bytes 73760 | tf_op jit(solution)/shard_map/ppermute | solution.py:528
  11.4 0.0 collective-permute-start.6
  11.4 1.0 %shard_map.131.spec_h = f32[8,256,128]{2,1,0:T(8,128)S(1)} custom-call(bf16[288,128]{1,0:T(8,128)(2,1)S(1)} %collective-permute-done.parcel_ref.refs_2_, f32[128,1024]{1,0:T(8,128)S(1)} %get-tuple-element.33.h_ref, bf16[256,256]{1,0:T(8,128)(2,1)S(1)} %get-tuple-element.34.window_hi, bf16[256,256]{1,0:T(8,128)(2,1)S(1)} %get-tuple-element.35.window_lo), custom_call_target="tpu_custom_call" | custom-call | tf_op jit(solution)/shard_map/pallas_call | solution.py:510
  12.4 0.7 %collective-permute-done.2.refs_1_ = bf16[288,128]{1,0:T(8,128)(2,1)S(1)} collective-permute-done((bf16[288,128]{1,0:T(8,128)(2,1)S(1)}, bf16[288,128]{1,0:T(8,128)(2,1)S(1)}, u32[]{:S(2)}, u32[]{:S(2)}) %collective-permute-start.2) | collective-permute-done | bytes 73760 | tf_op jit(solution)/shard_map/ppermute | solution.py:528
  13.1 0.0 collective-permute-done.3.refs_3_
  13.1 1.5 %collective-permute-done.4.refs_4_ = bf16[288,128]{1,0:T(8,128)(2,1)S(1)} collective-permute-done((bf16[288,128]{1,0:T(8,128)(2,1)S(1)}, bf16[288,128]{1,0:T(8,128)(2,1)S(1)}, u32[]{:S(2)}, u32[]{:S(2)}) %collective-permute-start.4) | collective-permute-done | bytes 73760 | tf_op jit(solution)/shard_map/ppermute | solution.py:528
  14.6 1.5 %collective-permute-done.5.refs_5_ = bf16[288,128]{1,0:T(8,128)(2,1)S(1)} collective-permute-done((bf16[288,128]{1,0:T(8,128)(2,1)S(1)}, bf16[288,128]{1,0:T(8,128)(2,1)S(1)}, u32[]{:S(2)}, u32[]{:S(2)}) %collective-permute-start.5) | collective-permute-done | bytes 73760 | tf_op jit(solution)/shard_map/ppermute | solution.py:528
  16.1 0.0 collective-permute-done.6.refs_6_
  16.1 0.0 copy-done.2
  16.1 0.0 copy-done.3
  16.1 0.0 copy-done.4
  16.1 2.5 %shard_map.132 = (bf16[288,128]{1,0:T(8,128)(2,1)S(1)}, bf16[288,128]{1,0:T(8,128)(2,1)S(1)}, bf16[288,128]{1,0:T(8,128)(2,1)S(1)}, bf16[288,128]{1,0:T(8,128)(2...) custom-call(f32[3,7,128]{2,1,0:T(8,128)S(1)} %get-tuple-element.31.t, ...), custom_call_target="tpu_custom_call" | custom-call | tf_op jit(solution)/shard_map/pallas_call | solution.py:510
  18.6 0.0 copy-start
  18.6 0.0 copy-start.1
  18.6 0.8 %collective-permute-start.10 = (bf16[288,128]{1,0:T(8,128)(2,1)S(1)}, bf16[288,128]{1,0:T(8,128)(2,1)S(1)}, u32[]{:S(2)}, u32[]{:S(2)}) collective-permute-start(bf16[288,128]{1,0:T(8,128)(2,1)S(1)} %get-tuple-element.47), channel_id=1, source_target_pairs={{0,24},{4,28},{8,16},{12,20},{16,8},{20,12},{24,0},{28,4},{1,25},{... | collective-permute-start | bytes 221192 | tf_op jit(solution)/shard_map/ppermute | solution.py:528
  19.4 1.7 %collective-permute-start.11 = (bf16[288,128]{1,0:T(8,128)(2,1)S(1)}, bf16[288,128]{1,0:T(8,128)(2,1)S(1)}, u32[]{:S(2)}, u32[]{:S(2)}) collective-permute-start(bf16[288,128]{1,0:T(8,128)(2,1)S(1)} %get-tuple-element.48), channel_id=1, source_target_pairs={{0,28},{4,24},{8,20},{12,16},{16,12},{20,8},{24,4},{28,0},{1,29},{... | collective-permute-start | bytes 221192 | tf_op jit(solution)/shard_map/ppermute | solution.py:528
  21.1 0.9 %collective-permute-start.7 = (bf16[288,128]{1,0:T(8,128)(2,1)S(1)}, bf16[288,128]{1,0:T(8,128)(2,1)S(1)}, u32[]{:S(2)}, u32[]{:S(2)}) collective-permute-start(bf16[288,128]{1,0:T(8,128)(2,1)S(1)} %get-tuple-element.43), channel_id=1, source_target_pairs={{0,16},{4,20},{8,24},{12,28},{16,0},{20,4},{24,8},{28,12},{1,17},{... | collective-permute-start | bytes 221192 | tf_op jit(solution)/shard_map/ppermute | solution.py:528
  22.0 0.8 %collective-permute-start.12 = (bf16[288,128]{1,0:T(8,128)(2,1)S(1)}, bf16[288,128]{1,0:T(8,128)(2,1)S(1)}, u32[]{:S(2)}, u32[]{:S(2)}) collective-permute-start(bf16[288,128]{1,0:T(8,128)(2,1)S(1)} %get-tuple-element.49), channel_id=1, source_target_pairs={{0,8},{4,12},{8,0},{12,4},{16,24},{20,28},{24,16},{28,20},{1,9},{5... | collective-permute-start | bytes 221192 | tf_op jit(solution)/shard_map/ppermute | solution.py:528
  22.8 0.6 %collective-permute-start.13 = (bf16[288,128]{1,0:T(8,128)(2,1)S(1)}, bf16[288,128]{1,0:T(8,128)(2,1)S(1)}, u32[]{:S(2)}, u32[]{:S(2)}) collective-permute-start(bf16[288,128]{1,0:T(8,128)(2,1)S(1)} %get-tuple-element.50), channel_id=1, source_target_pairs={{0,12},{4,8},{8,4},{12,0},{16,28},{20,24},{24,20},{28,16},{1,13},{... | collective-permute-start | bytes 221192 | tf_op jit(solution)/shard_map/ppermute | solution.py:528
  23.4 1.2 %collective-permute-done.10.refs_0_ = bf16[288,128]{1,0:T(8,128)(2,1)S(1)} collective-permute-done((bf16[288,128]{1,0:T(8,128)(2,1)S(1)}, bf16[288,128]{1,0:T(8,128)(2,1)S(1)}, u32[]{:S(2)}, u32[]{:S(2)}) %collective-permute-start.10) | collective-permute-done | bytes 73760 | tf_op jit(solution)/shard_map/ppermute | solution.py:528
  24.6 0.3 collective-permute-start.8
  24.9 0.0 collective-permute-done.11.refs_1_
  24.9 0.5 %collective-permute-start.9 = (bf16[288,128]{1,0:T(8,128)(2,1)S(1)}, bf16[288,128]{1,0:T(8,128)(2,1)S(1)}, u32[]{:S(2)}, u32[]{:S(2)}) collective-permute-start(bf16[288,128]{1,0:T(8,128)(2,1)S(1)} %get-tuple-element.45), channel_id=1, source_target_pairs={{0,4},{4,0},{8,12},{12,8},{16,20},{20,16},{24,28},{28,24},{1,5},{5... | collective-permute-start | bytes 221192 | tf_op jit(solution)/shard_map/ppermute | solution.py:528
  25.4 2.2 %shard_map.135 = f32[1,128,1024]{2,1,0:T(8,128)} custom-call(f32[8,256,128]{2,1,0:T(8,128)S(1)} %get-tuple-element.55.spec_x, f32[8,256,128]{2,1,0:T(8,128)S(1)} %get-tuple-element.56.spec_g, bf16[128,256]{1,0:T(8,128)(2,1)S(1)} %copy-done.3, bf16[128,256]{1,0:T(8,128)(2,1)S(1)} %copy-done.2), custom_call_target="tpu_custom_call" | custom-call | tf_op jit(solution)/shard_map/pallas_call | solution.py:510
  27.7 0.0 collective-permute-done.12.refs_2_
  27.7 0.2 collective-permute-done.13.refs_3_
  27.8 0.0 copy-done
  27.8 0.0 copy-done.1
  27.8 1.3 %shard_map.133 = (bf16[128,1024]{1,0:T(8,128)(2,1)}, bf16[3,128,1024]{2,1,0:T(8,128)(2,1)}) custom-call(bf16[128,1024]{1,0:T(8,128)(2,1)S(1)} %copy-done, f32[3,7,1024]{2,1,0:T(8,128)S(1)} %copy-done.1, f32[3,8,128,128]{3,2,1,0:T(8,128)S(1)} %get-tuple-element.30.filtered_ref, bf16[288,128]{1,0:T(8,128)(2,1)S(1)} %collective-permute-done.10.refs_0_, ...), custom_call_target="tpu_custom_call" | custom-call | tf_op jit(solution)/shard_map/pallas_call | solution.py:510
  29.2 0.0 collective-permute-done.7.refs_0_
  29.2 0.0 collective-permute-done.8.refs_1_
  29.2 0.0 collective-permute-done.9.refs_2_
  29.2 1.3 %shard_map.134 = (bf16[128,1024]{1,0:T(8,128)(2,1)}, bf16[3,128,1024]{2,1,0:T(8,128)(2,1)}) custom-call(bf16[128,1024]{1,0:T(8,128)(2,1)S(1)} %copy-done, f32[3,7,1024]{2,1,0:T(8,128)S(1)} %copy-done.1, f32[3,8,128,128]{3,2,1,0:T(8,128)S(1)} %get-tuple-element.30.filtered_ref, ...), custom_call_target="tpu_custom_call", output_to_operand_aliasing={{0}: (7, {}), {1}: (8, {})} | custom-call | tf_op jit(solution)/shard_map/pallas_call | solution.py:510
Async XLA Ops:
  0.6 15.4 %copy-start.2 = (bf16[128,256]{1,0:T(8,128)(2,1)S(1)}, bf16[128,256]{1,0:T(8,128)(2,1)}, u32[]{:S(2)}) copy-start(bf16[128,256]{1,0:T(8,128)(2,1)} %constant.14.clone.inv_lo) | copy-start | bytes 196612
  0.6 15.4 %copy-start.3 = (bf16[128,256]{1,0:T(8,128)(2,1)S(1)}, bf16[128,256]{1,0:T(8,128)(2,1)}, u32[]{:S(2)}) copy-start(bf16[128,256]{1,0:T(8,128)(2,1)} %constant.13.clone.inv_hi) | copy-start | bytes 196612
  0.7 15.4 %copy-start.4 = (bf16[256,256]{1,0:T(8,128)(2,1)S(1)}, bf16[256,256]{1,0:T(8,128)(2,1)}, u32[]{:S(2)}) copy-start(bf16[256,256]{1,0:T(8,128)(2,1)} %constant.12.clone.doubled) | copy-start | bytes 393220
  3.0 7.7 %collective-permute-start = (bf16[288,128]{1,0:T(8,128)(2,1)S(1)}, bf16[288,128]{1,0:T(8,128)(2,1)S(1)}, u32[]{:S(2)}, u32[]{:S(2)}) collective-permute-start(bf16[288,128]{1,0:T(8,128)(2,1)S(1)} %get-tuple-element.32), channel_id=1, source_target_pairs={{0,8},{4,12},{8,0},{12,4},{16,24},{20,28},{24,16},{28,20},{1,9},{5... | collective-permute-start | bytes 221192 | tf_op jit(solution)/shard_map/ppermute | solution.py:528
  6.0 5.4 %collective-permute-start.1 = (bf16[288,128]{1,0:T(8,128)(2,1)S(1)}, bf16[288,128]{1,0:T(8,128)(2,1)S(1)}, u32[]{:S(2)}, u32[]{:S(2)}) collective-permute-start(bf16[288,128]{1,0:T(8,128)(2,1)S(1)} %get-tuple-element.36), channel_id=1, source_target_pairs={{0,24},{4,28},{8,16},{12,20},{16,8},{20,12},{24,0},{28,4},{1,25},{... | collective-permute-start | bytes 221192 | tf_op jit(solution)/shard_map/ppermute | solution.py:528
  7.5 5.6 %collective-permute-start.2 = (bf16[288,128]{1,0:T(8,128)(2,1)S(1)}, bf16[288,128]{1,0:T(8,128)(2,1)S(1)}, u32[]{:S(2)}, u32[]{:S(2)}) collective-permute-start(bf16[288,128]{1,0:T(8,128)(2,1)S(1)} %get-tuple-element.37), channel_id=1, source_target_pairs={{0,28},{4,24},{8,20},{12,16},{16,12},{20,8},{24,4},{28,0},{1,29},{... | collective-permute-start | bytes 221192 | tf_op jit(solution)/shard_map/ppermute | solution.py:528
  7.8 5.3 %collective-permute-start.3 = (bf16[288,128]{1,0:T(8,128)(2,1)S(1)}, bf16[288,128]{1,0:T(8,128)(2,1)S(1)}, u32[]{:S(2)}, u32[]{:S(2)}) collective-permute-start(bf16[288,128]{1,0:T(8,128)(2,1)S(1)} %get-tuple-element.38), channel_id=1, source_target_pairs={{0,12},{4,8},{8,4},{12,0},{16,28},{20,24},{24,20},{28,16},{1,13},{... | collective-permute-start | bytes 221192 | tf_op jit(solution)/shard_map/ppermute | solution.py:528
  8.7 5.9 %collective-permute-start.4 = (bf16[288,128]{1,0:T(8,128)(2,1)S(1)}, bf16[288,128]{1,0:T(8,128)(2,1)S(1)}, u32[]{:S(2)}, u32[]{:S(2)}) collective-permute-start(bf16[288,128]{1,0:T(8,128)(2,1)S(1)} %get-tuple-element.39), channel_id=1, source_target_pairs={{0,16},{4,20},{8,24},{12,28},{16,0},{20,4},{24,8},{28,12},{1,17},{... | collective-permute-start | bytes 221192 | tf_op jit(solution)/shard_map/ppermute | solution.py:528
  10.7 5.4 %collective-permute-start.5 = (bf16[288,128]{1,0:T(8,128)(2,1)S(1)}, bf16[288,128]{1,0:T(8,128)(2,1)S(1)}, u32[]{:S(2)}, u32[]{:S(2)}) collective-permute-start(bf16[288,128]{1,0:T(8,128)(2,1)S(1)} %get-tuple-element.40), channel_id=1, source_target_pairs={{0,20},{4,16},{8,28},{12,24},{16,4},{20,0},{24,12},{28,8},{1,21},{... | collective-permute-start | bytes 221192 | tf_op jit(solution)/shard_map/ppermute | solution.py:528
  11.4 4.7 %collective-permute-start.6 = (bf16[288,128]{1,0:T(8,128)(2,1)S(1)}, bf16[288,128]{1,0:T(8,128)(2,1)S(1)}, u32[]{:S(2)}, u32[]{:S(2)}) collective-permute-start(bf16[288,128]{1,0:T(8,128)(2,1)S(1)} %get-tuple-element.41), channel_id=1, source_target_pairs={{0,4},{4,0},{8,12},{12,8},{16,20},{20,16},{24,28},{28,24},{1,5},{5... | collective-permute-start | bytes 221192 | tf_op jit(solution)/shard_map/ppermute | solution.py:528
  18.6 9.3 %copy-start = (bf16[128,1024]{1,0:T(8,128)(2,1)S(1)}, bf16[128,1024]{1,0:T(8,128)(2,1)}, u32[]{:S(2)}) copy-start(bf16[128,1024]{1,0:T(8,128)(2,1)} %g_ref.5) | copy-start | bytes 786436
  18.6 9.2 %copy-start.1 = (f32[3,7,1024]{2,1,0:T(8,128)S(1)}, f32[3,7,1024]{2,1,0:T(8,128)}, u32[]{:S(2)}) copy-start(f32[3,7,1024]{2,1,0:T(8,128)} %taps_ref.5) | copy-start | bytes 258052
  18.6 6.0 %collective-permute-start.10 = (bf16[288,128]{1,0:T(8,128)(2,1)S(1)}, bf16[288,128]{1,0:T(8,128)(2,1)S(1)}, u32[]{:S(2)}, u32[]{:S(2)}) collective-permute-start(bf16[288,128]{1,0:T(8,128)(2,1)S(1)} %get-tuple-element.47), channel_id=1, source_target_pairs={{0,24},{4,28},{8,16},{12,20},{16,8},{20,12},{24,0},{28,4},{1,25},{... | collective-permute-start | bytes 221192 | tf_op jit(solution)/shard_map/ppermute | solution.py:528
  19.4 5.5 %collective-permute-start.11 = (bf16[288,128]{1,0:T(8,128)(2,1)S(1)}, bf16[288,128]{1,0:T(8,128)(2,1)S(1)}, u32[]{:S(2)}, u32[]{:S(2)}) collective-permute-start(bf16[288,128]{1,0:T(8,128)(2,1)S(1)} %get-tuple-element.48), channel_id=1, source_target_pairs={{0,28},{4,24},{8,20},{12,16},{16,12},{20,8},{24,4},{28,0},{1,29},{... | collective-permute-start | bytes 221192 | tf_op jit(solution)/shard_map/ppermute | solution.py:528
  21.1 8.1 %collective-permute-start.7 = (bf16[288,128]{1,0:T(8,128)(2,1)S(1)}, bf16[288,128]{1,0:T(8,128)(2,1)S(1)}, u32[]{:S(2)}, u32[]{:S(2)}) collective-permute-start(bf16[288,128]{1,0:T(8,128)(2,1)S(1)} %get-tuple-element.43), channel_id=1, source_target_pairs={{0,16},{4,20},{8,24},{12,28},{16,0},{20,4},{24,8},{28,12},{1,17},{... | collective-permute-start | bytes 221192 | tf_op jit(solution)/shard_map/ppermute | solution.py:528
  22.0 5.7 %collective-permute-start.12 = (bf16[288,128]{1,0:T(8,128)(2,1)S(1)}, bf16[288,128]{1,0:T(8,128)(2,1)S(1)}, u32[]{:S(2)}, u32[]{:S(2)}) collective-permute-start(bf16[288,128]{1,0:T(8,128)(2,1)S(1)} %get-tuple-element.49), channel_id=1, source_target_pairs={{0,8},{4,12},{8,0},{12,4},{16,24},{20,28},{24,16},{28,20},{1,9},{5... | collective-permute-start | bytes 221192 | tf_op jit(solution)/shard_map/ppermute | solution.py:528
  22.8 5.0 %collective-permute-start.13 = (bf16[288,128]{1,0:T(8,128)(2,1)S(1)}, bf16[288,128]{1,0:T(8,128)(2,1)S(1)}, u32[]{:S(2)}, u32[]{:S(2)}) collective-permute-start(bf16[288,128]{1,0:T(8,128)(2,1)S(1)} %get-tuple-element.50), channel_id=1, source_target_pairs={{0,12},{4,8},{8,4},{12,0},{16,28},{20,24},{24,20},{28,16},{1,13},{... | collective-permute-start | bytes 221192 | tf_op jit(solution)/shard_map/ppermute | solution.py:528
  24.6 4.5 %collective-permute-start.8 = (bf16[288,128]{1,0:T(8,128)(2,1)S(1)}, bf16[288,128]{1,0:T(8,128)(2,1)S(1)}, u32[]{:S(2)}, u32[]{:S(2)}) collective-permute-start(bf16[288,128]{1,0:T(8,128)(2,1)S(1)} %get-tuple-element.44), channel_id=1, source_target_pairs={{0,20},{4,16},{8,28},{12,24},{16,4},{20,0},{24,12},{28,8},{1,21},{... | collective-permute-start | bytes 221192 | tf_op jit(solution)/shard_map/ppermute | solution.py:528
  24.9 4.3 %collective-permute-start.9 = (bf16[288,128]{1,0:T(8,128)(2,1)S(1)}, bf16[288,128]{1,0:T(8,128)(2,1)S(1)}, u32[]{:S(2)}, u32[]{:S(2)}) collective-permute-start(bf16[288,128]{1,0:T(8,128)(2,1)S(1)} %get-tuple-element.45), channel_id=1, source_target_pairs={{0,4},{4,0},{8,12},{12,8},{16,20},{20,16},{24,28},{28,24},{1,5},{5... | collective-permute-start | bytes 221192 | tf_op jit(solution)/shard_map/ppermute | solution.py:528

commit v2 on v1

--- a/solution.py
+++ b/solution.py
@@ -371,20 +371,17 @@
 
 
 def back_to_rows(spectrum, inv_hi, inv_lo):
-    high = spectrum.astype(jnp.bfloat16)
-    low = (spectrum - high.astype(jnp.float32)).astype(jnp.bfloat16)
-    return (
-        jnp.dot(inv_hi, high, preferred_element_type=jnp.float32)
-        + jnp.dot(inv_lo, high, preferred_element_type=jnp.float32)
-        + jnp.dot(inv_hi, low, preferred_element_type=jnp.float32)
-    )
-
-
-def store_tile(ref, first_lane, results, tile, bins):
+    return jnp.dot(inv_hi, spectrum, preferred_element_type=jnp.float32) + jnp.dot(
+        inv_lo, spectrum, preferred_element_type=jnp.float32
+    )
+
+
+def store_tiles(ref, first_lane, tiles, pair, bins):
     lanes = pl.ds(first_lane, LANES)
-    for index, (real, imag) in enumerate(results):
-        ref[index, pl.ds(pl.multiple_of(tile * 8, 8), 8), lanes] = real
-        ref[index, pl.ds(pl.multiple_of(bins + tile * 8, 8), 8), lanes] = imag
+    for index, parts in enumerate(zip(*tiles)):
+        for first, values in zip((0, bins), zip(*parts)):
+            rows = pl.ds(pl.multiple_of(first + pair * 16, 16), 16)
+            ref[index, rows, lanes] = jnp.concatenate(values, axis=0).astype(ref.dtype)
 
 
 def convolve_kernel(order, taps_ref, spec_h, doubled, inv_hi, inv_lo, *refs):
@@ -398,17 +395,19 @@
     repair_heads(taps_ref, edges, firsts, joined, heads)
     to_spectra(order, in_refs, heads, doubled[...], spec_x, spec_g, rows, halo)
 
-    def body(tile, carry):
-        filt = load_tile(spec_h, count, tile, rows)
-        sums = [[(i - j, j) for j in range(i + 1)] for i in range(count)]
-        results = mixed_products(filt, load_tile(spec_x, count, tile, rows), sums, False)
-        store_tile(spec_y, 0, results, tile, rows)
-        sums = [[(j - i, j) for j in range(i, count)] for i in range(count)]
-        results = mixed_products(filt, load_tile(spec_g, count, tile, rows), sums, True)
-        store_tile(spec_y, LANES, results, tile, rows)
+    def body(pair, carry):
+        longs, backs = [], []
+        for tile in (2 * pair, 2 * pair + 1):
+            filt = load_tile(spec_h, count, tile, rows)
+            sums = [[(i - j, j) for j in range(i + 1)] for i in range(count)]
+            longs.append(mixed_products(filt, load_tile(spec_x, count, tile, rows), sums, False))
+            sums = [[(j - i, j) for j in range(i, count)] for i in range(count)]
+            backs.append(mixed_products(filt, load_tile(spec_g, count, tile, rows), sums, True))
+        store_tiles(spec_y, 0, longs, pair, rows)
+        store_tiles(spec_y, LANES, backs, pair, rows)
         return carry
 
-    lax.fori_loop(0, rows // 8, body, 0)
+    lax.fori_loop(0, rows // 16, body, 0)
     extra[...] = jnp.zeros(extra.shape, jnp.float32)
     for mask, out_ref in zip(order, out_refs):
         block = me ^ mask
@@ -435,32 +434,31 @@
     count = spec_x.shape[0]
     rows = inv_hi.shape[0]
 
-    def body(tile, carry):
-        real, imag = load_tile(spec_x, count, tile, rows)
+    def body(pair, carry):
         row = lax.broadcasted_iota(jnp.int32, (8, LANES), 0)
         sign = jnp.where(row % 2 == 0, 1.0, -1.0)
-        window_re = [real[0]] + [real[i] - sign * imag[i - 1] for i in range(1, count)]
-        window_im = [imag[0]] + [imag[i] + sign * real[i - 1] for i in range(1, count)]
-        sums = [[(j - lag, j) for j in range(lag, count)] for lag in range(count)]
-        results = mixed_products((window_re, window_im), load_tile(spec_g, count, tile, rows), sums, True)
-        store_tile(spec_y, 0, results, tile, rows)
+        tiles = []
+        for tile in (2 * pair, 2 * pair + 1):
+            real, imag = load_tile(spec_x, count, tile, rows)
+            window_re = [real[0]] + [real[i] - sign * imag[i - 1] for i in range(1, count)]
+            window_im = [imag[0]] + [imag[i] + sign * real[i - 1] for i in range(1, count)]
+            sums = [[(j - lag, j) for j in range(lag, count)] for lag in range(count)]
+            grad = load_tile(spec_g, count, tile, rows)
+            tiles.append(mixed_products((window_re, window_im), grad, sums, True))
+        store_tiles(spec_y, 0, tiles, pair, rows)
         return carry
 
-    lax.fori_loop(0, rows // 8, body, 0)
+    lax.fori_loop(0, rows // 16, body, 0)
     for block in range(count):
         result = back_to_rows(spec_y[block], inv_hi[...], inv_lo[...])
-        out_ref[0, :, pl.ds(block * rows, rows)] = result.T * scale
-
-
-def receive_kernel(places, order, g_ref, taps_ref, filtered_ref, *refs):
-    count = len(places)
-    in_refs = refs[:count]
-    mixed_ref, grads_ref, padded, extra, leaving, departures = refs[-6:]
+        out_ref[:, pl.ds(block * rows, rows)] = result.T * scale
+
+
+def finish_channels(order, places, in_refs, g_ref, taps_ref, filtered_ref, padded, extra, results, leave):
     me = lax.axis_index("context")
     rows = g_ref.shape[0]
     span = taps_ref.shape[1]
     halo = span - 1
-    copies = []
     for index, (place, in_ref) in enumerate(zip(places, in_refs)):
         lanes = pl.ds(pl.multiple_of((me ^ order[place]) * LANES, LANES), LANES)
         slot = index % padded.shape[0]
@@ -471,11 +469,8 @@
         back = in_ref[pl.ds(rows, rows), :].astype(jnp.float32)
         extra[slot, pl.ds(0, edge_rows), :] = in_ref[pl.ds(2 * rows, edge_rows), :].astype(jnp.float32)
         mixed = head_rows(extra[slot, pl.ds(0, 8), :], query_f * long_conv, halo)
-        leaving[index, 3] = mixed.astype(jnp.bfloat16)
-        copies.append(
-            pltpu.make_async_copy(leaving.at[index, 3], mixed_ref.at[:, lanes], departures.at[index, 3])
-        )
-        copies[-1].start()
+        results[index, 3] = mixed.astype(jnp.bfloat16)
+        leave(index, 3)
         grads = (
             cotangent * long_conv,
             head_rows(back[:8], back * value_f, halo),
@@ -488,21 +483,52 @@
             running = weights[0] * padded[slot, which, pl.ds(0, rows), :]
             for offset in range(1, span):
                 running = running + weights[offset] * padded[slot, which, pl.ds(offset, rows), :]
-            leaving[index, which] = running.astype(jnp.bfloat16)
+            results[index, which] = running.astype(jnp.bfloat16)
+            leave(index, which)
+
+
+def early_kernel(order, places, g_ref, taps_ref, filtered_ref, *refs):
+    *in_refs, results, padded, extra = refs
+    finish_channels(
+        order, places, in_refs, g_ref, taps_ref, filtered_ref, padded, extra, results, lambda *_: None
+    )
+
+
+def last_kernel(order, early, places, g_ref, taps_ref, filtered_ref, early_ref, filter_ref, *refs):
+    in_refs = refs[: len(places)]
+    mixed_ref, grads_ref, filter_out, padded, extra, results, early_sems, sems, filter_sem = refs[
+        len(places) :
+    ]
+    me = lax.axis_index("context")
+    copies = [pltpu.make_async_copy(filter_ref, filter_out.at[0], filter_sem)]
+    copies[0].start()
+
+    def leave_from(source, members, semaphores):
+        def leave(index, which):
+            lanes = pl.ds(pl.multiple_of((me ^ order[members[index]]) * LANES, LANES), LANES)
+            target = mixed_ref.at[:, lanes] if which == 3 else grads_ref.at[which, :, lanes]
             copies.append(
-                pltpu.make_async_copy(
-                    leaving.at[index, which], grads_ref.at[which, :, lanes], departures.at[index, which]
-                )
+                pltpu.make_async_copy(source.at[index, which], target, semaphores.at[index, which])
             )
             copies[-1].start()
+
+        return leave
+
+    leave = leave_from(early_ref, early, early_sems)
+    for index in range(len(early)):
+        for which in range(4):
+            leave(index, which)
+    finish_channels(
+        order, places, in_refs, g_ref, taps_ref, filtered_ref, padded, extra, results,
+        leave_from(results, places, sems),
+    )
     for copy in copies:
         copy.wait()
 
 
-def on_device(kernel, out_shape, scratch, args, in_hbm=0, pin=True, updated=0):
+def on_device(kernel, out_shape, scratch, args, in_hbm=0, pin=True):
     whole = pl.BlockSpec(memory_space=pltpu.VMEM)
     outside = pl.BlockSpec(memory_space=pltpu.HBM if pin else pl.ANY)
-    last = len(args) - updated
     args = [
         pltpu.with_memory_space_constraint(arg, pltpu.HBM) if pin and place < in_hbm else arg
         for place, arg in enumerate(args)
@@ -510,16 +536,22 @@
     return pl.pallas_call(
         kernel,
         out_shape=out_shape,
-        in_specs=[outside if place < in_hbm or place >= last else whole for place in range(len(args))],
+        in_specs=[outside if place < in_hbm else whole for place in range(len(args))],
         out_specs=jax.tree.map(
             lambda out: whole if isinstance(out, jax.ShapeDtypeStruct) else outside, out_shape
         ),
-        input_output_aliases={last + place: place for place in range(updated)},
         scratch_shapes=[
             pltpu.VMEM(shape, jnp.float32) if isinstance(shape, tuple) else shape for shape in scratch
         ],
         compiler_params=pltpu.CompilerParams(vmem_limit_bytes=VMEM_BYTES),
     )(*args)
+
+
+def exchange_order(count):
+    return sorted(
+        range(count),
+        key=lambda mask: (mask == 0, -(mask >> 1).bit_count(), mask % 2, mask if mask % 2 else -mask),
+    )
 
 
 def exchange(order, parcels):
@@ -537,7 +569,7 @@
     seq_len = rows * blocks
     window_hi, window_lo, doubled, inv_hi, inv_lo = [jnp.asarray(t) for t in block_tables(rows)]
     edge_rows = round_up(5 * halo, 16)
-    order = sorted(range(blocks), key=lambda mask: (mask == 0, -(mask >> 1).bit_count()))
+    order = exchange_order(blocks)
     parcels = [jax.ShapeDtypeStruct((2 * rows + edge_rows, LANES), jnp.bfloat16)] * blocks
     spectra = (blocks, 2 * rows, LANES)
     own_taps = (*short_taps.shape[:2], LANES)
@@ -567,7 +599,7 @@
         filter_kernel,
         jax.ShapeDtypeStruct(spectra, jnp.float32),
         [],
-        (arrived[2], filter_here, hi_here, lo_here),
+        (arrived[0], filter_here, hi_here, lo_here),
         in_hbm=1,
         pin=False,
     )
@@ -579,7 +611,7 @@
             (blocks, 2, 8, LANES),
             (3, blocks, 24, LANES),
             (blocks, 6, 8, LANES),
-            (blocks, 2 * rows, 2 * LANES),
+            pltpu.VMEM((blocks, 2 * rows, 2 * LANES), jnp.bfloat16),
             (blocks + 1, edge_rows, LANES),
         ],
         (own, spec_h, doubled, inv_hi, inv_lo, *arrived),
@@ -587,29 +619,36 @@
     returned = exchange(order, results)
     filter_grad = on_device(
         functools.partial(correlate_kernel, 1.0 / math.sqrt(seq_len)),
-        jax.ShapeDtypeStruct(long_filter.shape, jnp.float32),
-        [spectra],
+        jax.ShapeDtypeStruct(long_filter.shape[1:], jnp.float32),
+        [pltpu.VMEM(spectra, jnp.bfloat16)],
         (spec_x, spec_g, inv_hi, inv_lo),
     )
-    finished = ()
-    halves = (range(blocks // 2), range(blocks // 2, blocks))
-    for places in halves:
-        finished = on_device(
-            functools.partial(receive_kernel, places, order),
-            (
-                pltpu.HBM((rows, channels), jnp.bfloat16),
-                pltpu.HBM((3, rows, channels), jnp.bfloat16),
-            ),
-            [
-                (2, 3, rows + 16, LANES),
-                (2, edge_rows + 8, LANES),
-                pltpu.VMEM((len(places), 4, rows, LANES), jnp.bfloat16),
-                pltpu.SemaphoreType.DMA((len(places), 4)),
-            ],
-            (grad_mixed, short_taps, filtered, *(returned[place] for place in places), *finished),
-            updated=len(finished),
-        )
-    mixed_out, input_grads = finished
+    late = list(range(blocks // 2 - 1, blocks - 1))
+    early = [place for place in range(blocks) if place not in late]
+    padded = [(2, 3, rows + 16, LANES), (2, edge_rows + 8, LANES)]
+    common = (grad_mixed, short_taps, filtered)
+    early_results = on_device(
+        functools.partial(early_kernel, order, early),
+        jax.ShapeDtypeStruct((len(early), 4, rows, LANES), jnp.bfloat16),
+        padded,
+        (*common, *(returned[place] for place in early)),
+    )
+    mixed_out, input_grads, filter_grad = on_device(
+        functools.partial(last_kernel, order, early, late),
+        (
+            pltpu.HBM((rows, channels), jnp.bfloat16),
+            pltpu.HBM((3, rows, channels), jnp.bfloat16),
+            pltpu.HBM(long_filter.shape, jnp.float32),
+        ),
+        padded
+        + [
+            pltpu.VMEM((len(late), 4, rows, LANES), jnp.bfloat16),
+            pltpu.SemaphoreType.DMA((len(early), 4)),
+            pltpu.SemaphoreType.DMA((len(late), 4)),
+            pltpu.SemaphoreType.DMA(()),
+        ],
+        (*common, early_results, filter_grad, *(returned[place] for place in late)),
+    )
     return (mixed_out, input_grads, filter_grad)
 
 

time: 30.8 us -> 28.5 us (0.925)
  Pallas kernels: 10.6 us -> 9.04 us
  waiting for transfers between devices: 5.82 us -> 4.54 us
  starting transfers between devices: 13.3 us -> 14 us
    pallas_call x6, Pallas kernels: 10.6 us -> 9.04 us  [on_device(): pl.pallas_call(kernel, out_shape=out_shape, in_specs=[outside if place <...]
    ppermute x14, waiting for transfers between devices: 5.82 us -> 4.54 us  [exchange(): lax.ppermute(parcel, 'context', [(i, i ^ mask) for i in range(count)])]
    ppermute x14, starting transfers between devices: 13.3 us -> 14 us  [exchange(): lax.ppermute(parcel, 'context', [(i, i ^ mask) for i in range(count)])]
  transfers between devices with their start and end apart: 14 -> 14, of which waited for: 6 -> 7; matrix products, arithmetic and copies ran while one was open for 0% -> 0% of each run, Pallas kernels for 15% -> 10%
where the time goes in v2:
time: 28.5 us; the launch traced here: 28.4 us
  starting transfers between devices  14 us (49%)
  Pallas kernels  9.04 us (32%)
  waiting for transfers between devices  4.54 us (16%)
  between operations  0.76 us (3%)
    ppermute x14, starting transfers between devices, exchange(): lax.ppermute(parcel, 'context', [(i, i ^ mask) for i in range(count)])  14 us
    pallas_call x6, Pallas kernels, on_device(): pl.pallas_call(kernel, out_shape=out_shape, in_specs=[outside if place <...  9.04 us
    ppermute x14, waiting for transfers between devices, exchange(): lax.ppermute(parcel, 'context', [(i, i ^ mask) for i in range(count)])  4.54 us
  transfers between devices with their start and end apart: 14, of which 7 were waited for; matrix products, arithmetic and copies ran while one was open for 0% of the time, Pallas kernels for 10%

profile of v2, /device:TPU:0, one launch (start us, length us, event | category | flops | bytes accessed | tf_op | source)
XLA Modules:
  0.0 28.4 jit_solution(11432585659809216259)
XLA Ops:
  0.6 0.0 copy-start.2
  0.6 0.0 copy-start.3
  0.7 0.0 copy-start.4
  0.7 2.3 %shard_map.130 = (bf16[288,128]{1,0:T(8,128)(2,1)S(1)}, bf16[288,128]{1,0:T(8,128)(2,1)S(1)}, bf16[288,128]{1,0:T(8,128)(2,1)S(1)}, bf16[288,128]{1,0:T(8,128)(2...) custom-call(bf16[128,1024]{1,0:T(8,128)(2,1)} %q_ref.1, ...), custom_call_target="tpu_custom_call" | custom-call | tf_op jit(solution)/shard_map/pallas_call | solution.py:536
  3.0 4.0 %collective-permute-start = (bf16[288,128]{1,0:T(8,128)(2,1)S(1)}, bf16[288,128]{1,0:T(8,128)(2,1)S(1)}, u32[]{:S(2)}, u32[]{:S(2)}) collective-permute-start(bf16[288,128]{1,0:T(8,128)(2,1)S(1)} %get-tuple-element.28), channel_id=1, source_target_pairs={{0,24},{4,28},{8,16},{12,20},{16,8},{20,12},{24,0},{28,4},{1,25},{... | collective-permute-start | bytes 221192 | tf_op jit(solution)/shard_map/ppermute | solution.py:560
  6.9 0.0 collective-permute-start.1
  6.9 1.2 %collective-permute-start.2 = (bf16[288,128]{1,0:T(8,128)(2,1)S(1)}, bf16[288,128]{1,0:T(8,128)(2,1)S(1)}, u32[]{:S(2)}, u32[]{:S(2)}) collective-permute-start(bf16[288,128]{1,0:T(8,128)(2,1)S(1)} %get-tuple-element.33), channel_id=1, source_target_pairs={{0,16},{4,20},{8,24},{12,28},{16,0},{20,4},{24,8},{28,12},{1,17},{... | collective-permute-start | bytes 221192 | tf_op jit(solution)/shard_map/ppermute | solution.py:560
  8.1 1.5 %collective-permute-start.3 = (bf16[288,128]{1,0:T(8,128)(2,1)S(1)}, bf16[288,128]{1,0:T(8,128)(2,1)S(1)}, u32[]{:S(2)}, u32[]{:S(2)}) collective-permute-start(bf16[288,128]{1,0:T(8,128)(2,1)S(1)} %get-tuple-element.34), channel_id=1, source_target_pairs={{0,8},{4,12},{8,0},{12,4},{16,24},{20,28},{24,16},{28,20},{1,9},{5... | collective-permute-start | bytes 221192 | tf_op jit(solution)/shard_map/ppermute | solution.py:560
  9.6 0.6 %collective-permute-start.4 = (bf16[288,128]{1,0:T(8,128)(2,1)S(1)}, bf16[288,128]{1,0:T(8,128)(2,1)S(1)}, u32[]{:S(2)}, u32[]{:S(2)}) collective-permute-start(bf16[288,128]{1,0:T(8,128)(2,1)S(1)} %get-tuple-element.35), channel_id=1, source_target_pairs={{0,12},{4,8},{8,4},{12,0},{16,28},{20,24},{24,20},{28,16},{1,13},{... | collective-permute-start | bytes 221192 | tf_op jit(solution)/shard_map/ppermute | solution.py:560
  10.2 0.0 collective-permute-done.parcel_ref.refs_0_
  10.2 0.6 %collective-permute-start.5 = (bf16[288,128]{1,0:T(8,128)(2,1)S(1)}, bf16[288,128]{1,0:T(8,128)(2,1)S(1)}, u32[]{:S(2)}, u32[]{:S(2)}) collective-permute-start(bf16[288,128]{1,0:T(8,128)(2,1)S(1)} %get-tuple-element.36), channel_id=1, source_target_pairs={{0,20},{4,16},{8,28},{12,24},{16,4},{20,0},{24,12},{28,8},{1,21},{... | collective-permute-start | bytes 221192 | tf_op jit(solution)/shard_map/ppermute | solution.py:560
  10.7 1.7 %collective-permute-done.1.refs_1_ = bf16[288,128]{1,0:T(8,128)(2,1)S(1)} collective-permute-done((bf16[288,128]{1,0:T(8,128)(2,1)S(1)}, bf16[288,128]{1,0:T(8,128)(2,1)S(1)}, u32[]{:S(2)}, u32[]{:S(2)}) %collective-permute-start.1) | collective-permute-done | bytes 73760 | tf_op jit(solution)/shard_map/ppermute | solution.py:560
  12.4 0.0 collective-permute-start.6
  12.4 1.0 %shard_map.131.spec_h = f32[8,256,128]{2,1,0:T(8,128)S(1)} custom-call(bf16[288,128]{1,0:T(8,128)(2,1)S(1)} %collective-permute-done.parcel_ref.refs_0_, f32[128,1024]{1,0:T(8,128)S(1)} %get-tuple-element.29.h_ref, bf16[256,256]{1,0:T(8,128)(2,1)S(1)} %get-tuple-element.30.window_hi, bf16[256,256]{1,0:T(8,128)(2,1)S(1)} %get-tuple-element.31.window_lo), custom_call_target="tpu_custom_call" | custom-call | tf_op jit(solution)/shard_map/pallas_call | solution.py:536
  13.4 0.0 collective-permute-done.2.refs_2_
  13.4 0.0 collective-permute-done.3.refs_3_
  13.4 0.8 %collective-permute-done.4.refs_4_ = bf16[288,128]{1,0:T(8,128)(2,1)S(1)} collective-permute-done((bf16[288,128]{1,0:T(8,128)(2,1)S(1)}, bf16[288,128]{1,0:T(8,128)(2,1)S(1)}, u32[]{:S(2)}, u32[]{:S(2)}) %collective-permute-start.4) | collective-permute-done | bytes 73760 | tf_op jit(solution)/shard_map/ppermute | solution.py:560
  14.2 0.3 collective-permute-done.5.refs_5_
  14.5 0.0 collective-permute-done.6.refs_6_
  14.5 0.0 copy-done.2
  14.5 0.0 copy-done.3
  14.5 0.0 copy-done.4
  14.5 2.4 %shard_map.132 = (bf16[288,128]{1,0:T(8,128)(2,1)S(1)}, bf16[288,128]{1,0:T(8,128)(2,1)S(1)}, bf16[288,128]{1,0:T(8,128)(2,1)S(1)}, bf16[288,128]{1,0:T(8,128)(2...) custom-call(f32[3,7,128]{2,1,0:T(8,128)S(1)} %get-tuple-element.27.t, ...), custom_call_target="tpu_custom_call" | custom-call | tf_op jit(solution)/shard_map/pallas_call | solution.py:536
  16.9 0.0 copy-start
  16.9 0.0 copy-start.1
  16.9 2.2 %collective-permute-start.7 = (bf16[288,128]{1,0:T(8,128)(2,1)S(1)}, bf16[288,128]{1,0:T(8,128)(2,1)S(1)}, u32[]{:S(2)}, u32[]{:S(2)}) collective-permute-start(bf16[288,128]{1,0:T(8,128)(2,1)S(1)} %get-tuple-element.39), channel_id=1, source_target_pairs={{0,24},{4,28},{8,16},{12,20},{16,8},{20,12},{24,0},{28,4},{1,25},{... | collective-permute-start | bytes 221192 | tf_op jit(solution)/shard_map/ppermute | solution.py:560
  19.1 0.3 collective-permute-start.8
  19.4 1.5 %collective-permute-start.9 = (bf16[288,128]{1,0:T(8,128)(2,1)S(1)}, bf16[288,128]{1,0:T(8,128)(2,1)S(1)}, u32[]{:S(2)}, u32[]{:S(2)}) collective-permute-start(bf16[288,128]{1,0:T(8,128)(2,1)S(1)} %get-tuple-element.41), channel_id=1, source_target_pairs={{0,16},{4,20},{8,24},{12,28},{16,0},{20,4},{24,8},{28,12},{1,17},{... | collective-permute-start | bytes 221192 | tf_op jit(solution)/shard_map/ppermute | solution.py:560
  20.9 0.6 %collective-permute-start.10 = (bf16[288,128]{1,0:T(8,128)(2,1)S(1)}, bf16[288,128]{1,0:T(8,128)(2,1)S(1)}, u32[]{:S(2)}, u32[]{:S(2)}) collective-permute-start(bf16[288,128]{1,0:T(8,128)(2,1)S(1)} %get-tuple-element.45), channel_id=1, source_target_pairs={{0,8},{4,12},{8,0},{12,4},{16,24},{20,28},{24,16},{28,20},{1,9},{5... | collective-permute-start | bytes 221192 | tf_op jit(solution)/shard_map/ppermute | solution.py:560
  21.5 1.2 %collective-permute-start.11 = (bf16[288,128]{1,0:T(8,128)(2,1)S(1)}, bf16[288,128]{1,0:T(8,128)(2,1)S(1)}, u32[]{:S(2)}, u32[]{:S(2)}) collective-permute-start(bf16[288,128]{1,0:T(8,128)(2,1)S(1)} %get-tuple-element.46), channel_id=1, source_target_pairs={{0,12},{4,8},{8,4},{12,0},{16,28},{20,24},{24,20},{28,16},{1,13},{... | collective-permute-start | bytes 221192 | tf_op jit(solution)/shard_map/ppermute | solution.py:560
  22.7 0.0 collective-permute-done.7.refs_0_
  22.7 0.5 %collective-permute-start.12 = (bf16[288,128]{1,0:T(8,128)(2,1)S(1)}, bf16[288,128]{1,0:T(8,128)(2,1)S(1)}, u32[]{:S(2)}, u32[]{:S(2)}) collective-permute-start(bf16[288,128]{1,0:T(8,128)(2,1)S(1)} %get-tuple-element.47), channel_id=1, source_target_pairs={{0,20},{4,16},{8,28},{12,24},{16,4},{20,0},{24,12},{28,8},{1,21},{... | collective-permute-start | bytes 221192 | tf_op jit(solution)/shard_map/ppermute | solution.py:560
  23.2 0.9 %collective-permute-done.8.refs_1_ = bf16[288,128]{1,0:T(8,128)(2,1)S(1)} collective-permute-done((bf16[288,128]{1,0:T(8,128)(2,1)S(1)}, bf16[288,128]{1,0:T(8,128)(2,1)S(1)}, u32[]{:S(2)}, u32[]{:S(2)}) %collective-permute-start.8) | collective-permute-done | bytes 73760 | tf_op jit(solution)/shard_map/ppermute | solution.py:560
  24.1 0.0 collective-permute-start.13
  24.1 1.3 %shard_map.134.filter_ref = f32[128,1024]{1,0:T(8,128)S(1)} custom-call(f32[8,256,128]{2,1,0:T(8,128)S(1)} %get-tuple-element.43.spec_x, f32[8,256,128]{2,1,0:T(8,128)S(1)} %get-tuple-element.44.spec_g, bf16[128,256]{1,0:T(8,128)(2,1)S(1)} %copy-done.3, bf16[128,256]{1,0:T(8,128)(2,1)S(1)} %copy-done.2), custom_call_target="tpu_custom_call" | custom-call | tf_op jit(solution)/shard_map/pallas_call | solution.py:536
  25.4 0.2 collective-permute-done.9.refs_2_
  25.6 0.0 copy-done
  25.6 0.0 copy-done.1
  25.6 0.6 %shard_map.133.early_ref = bf16[4,4,128,128]{3,2,1,0:T(8,128)(2,1)S(1)} custom-call(bf16[128,1024]{1,0:T(8,128)(2,1)S(1)} %copy-done, f32[3,7,1024]{2,1,0:T(8,128)S(1)} %copy-done.1, f32[3,8,128,128]{3,2,1,0:T(8,128)S(1)} %get-tuple-element.26.filtered_ref, bf16[288,128]{1,0:T(8,128)(2,1)S(1)} %collective-permute-done.7.refs_0_, ...), custom_call_target="tpu_custom_call" | custom-call | tf_op jit(solution)/shard_map/pallas_call | solution.py:536
  26.2 0.0 collective-permute-done.10.refs_0_
  26.2 0.4 %collective-permute-done.11.refs_1_ = bf16[288,128]{1,0:T(8,128)(2,1)S(1)} collective-permute-done((bf16[288,128]{1,0:T(8,128)(2,1)S(1)}, bf16[288,128]{1,0:T(8,128)(2,1)S(1)}, u32[]{:S(2)}, u32[]{:S(2)}) %collective-permute-start.11) | collective-permute-done | bytes 73760 | tf_op jit(solution)/shard_map/ppermute | solution.py:560
  26.6 0.2 collective-permute-done.12.refs_2_
  26.8 0.0 collective-permute-done.13.refs_3_
  26.8 1.5 %shard_map.135 = (bf16[128,1024]{1,0:T(8,128)(2,1)}, bf16[3,128,1024]{2,1,0:T(8,128)(2,1)}, f32[1,128,1024]{2,1,0:T(8,128)}) custom-call(bf16[128,1024]{1,0:T(8,128)(2,1)S(1)} %copy-done, f32[3,7,1024]{2,1,0:T(8,128)S(1)} %copy-done.1, f32[3,8,128,128]{3,2,1,0:T(8,128)S(1)} %get-tuple-element.26.filtered_ref, ...), custom_call_target="tpu_custom_call" | custom-call | tf_op jit(solution)/shard_map/pallas_call | solution.py:536
Async XLA Ops:
  0.6 13.8 %copy-start.2 = (bf16[128,256]{1,0:T(8,128)(2,1)S(1)}, bf16[128,256]{1,0:T(8,128)(2,1)}, u32[]{:S(2)}) copy-start(bf16[128,256]{1,0:T(8,128)(2,1)} %constant.14.clone.inv_lo) | copy-start | bytes 196612
  0.6 13.8 %copy-start.3 = (bf16[128,256]{1,0:T(8,128)(2,1)S(1)}, bf16[128,256]{1,0:T(8,128)(2,1)}, u32[]{:S(2)}) copy-start(bf16[128,256]{1,0:T(8,128)(2,1)} %constant.13.clone.inv_hi) | copy-start | bytes 196612
  0.7 13.8 %copy-start.4 = (bf16[256,256]{1,0:T(8,128)(2,1)S(1)}, bf16[256,256]{1,0:T(8,128)(2,1)}, u32[]{:S(2)}) copy-start(bf16[256,256]{1,0:T(8,128)(2,1)} %constant.12.clone.doubled) | copy-start | bytes 393220
  3.0 7.2 %collective-permute-start = (bf16[288,128]{1,0:T(8,128)(2,1)S(1)}, bf16[288,128]{1,0:T(8,128)(2,1)S(1)}, u32[]{:S(2)}, u32[]{:S(2)}) collective-permute-start(bf16[288,128]{1,0:T(8,128)(2,1)S(1)} %get-tuple-element.28), channel_id=1, source_target_pairs={{0,24},{4,28},{8,16},{12,20},{16,8},{20,12},{24,0},{28,4},{1,25},{... | collective-permute-start | bytes 221192 | tf_op jit(solution)/shard_map/ppermute | solution.py:560
  6.9 5.5 %collective-permute-start.1 = (bf16[288,128]{1,0:T(8,128)(2,1)S(1)}, bf16[288,128]{1,0:T(8,128)(2,1)S(1)}, u32[]{:S(2)}, u32[]{:S(2)}) collective-permute-start(bf16[288,128]{1,0:T(8,128)(2,1)S(1)} %get-tuple-element.32), channel_id=1, source_target_pairs={{0,28},{4,24},{8,20},{12,16},{16,12},{20,8},{24,4},{28,0},{1,29},{... | collective-permute-start | bytes 221192 | tf_op jit(solution)/shard_map/ppermute | solution.py:560
  6.9 6.4 %collective-permute-start.2 = (bf16[288,128]{1,0:T(8,128)(2,1)S(1)}, bf16[288,128]{1,0:T(8,128)(2,1)S(1)}, u32[]{:S(2)}, u32[]{:S(2)}) collective-permute-start(bf16[288,128]{1,0:T(8,128)(2,1)S(1)} %get-tuple-element.33), channel_id=1, source_target_pairs={{0,16},{4,20},{8,24},{12,28},{16,0},{20,4},{24,8},{28,12},{1,17},{... | collective-permute-start | bytes 221192 | tf_op jit(solution)/shard_map/ppermute | solution.py:560
  8.1 5.3 %collective-permute-start.3 = (bf16[288,128]{1,0:T(8,128)(2,1)S(1)}, bf16[288,128]{1,0:T(8,128)(2,1)S(1)}, u32[]{:S(2)}, u32[]{:S(2)}) collective-permute-start(bf16[288,128]{1,0:T(8,128)(2,1)S(1)} %get-tuple-element.34), channel_id=1, source_target_pairs={{0,8},{4,12},{8,0},{12,4},{16,24},{20,28},{24,16},{28,20},{1,9},{5... | collective-permute-start | bytes 221192 | tf_op jit(solution)/shard_map/ppermute | solution.py:560
  9.6 4.6 %collective-permute-start.4 = (bf16[288,128]{1,0:T(8,128)(2,1)S(1)}, bf16[288,128]{1,0:T(8,128)(2,1)S(1)}, u32[]{:S(2)}, u32[]{:S(2)}) collective-permute-start(bf16[288,128]{1,0:T(8,128)(2,1)S(1)} %get-tuple-element.35), channel_id=1, source_target_pairs={{0,12},{4,8},{8,4},{12,0},{16,28},{20,24},{24,20},{28,16},{1,13},{... | collective-permute-start | bytes 221192 | tf_op jit(solution)/shard_map/ppermute | solution.py:560
  10.2 4.3 %collective-permute-start.5 = (bf16[288,128]{1,0:T(8,128)(2,1)S(1)}, bf16[288,128]{1,0:T(8,128)(2,1)S(1)}, u32[]{:S(2)}, u32[]{:S(2)}) collective-permute-start(bf16[288,128]{1,0:T(8,128)(2,1)S(1)} %get-tuple-element.36), channel_id=1, source_target_pairs={{0,20},{4,16},{8,28},{12,24},{16,4},{20,0},{24,12},{28,8},{1,21},{... | collective-permute-start | bytes 221192 | tf_op jit(solution)/shard_map/ppermute | solution.py:560
  12.4 2.1 %collective-permute-start.6 = (bf16[288,128]{1,0:T(8,128)(2,1)S(1)}, bf16[288,128]{1,0:T(8,128)(2,1)S(1)}, u32[]{:S(2)}, u32[]{:S(2)}) collective-permute-start(bf16[288,128]{1,0:T(8,128)(2,1)S(1)} %get-tuple-element.37), channel_id=1, source_target_pairs={{0,4},{4,0},{8,12},{12,8},{16,20},{20,16},{24,28},{28,24},{1,5},{5... | collective-permute-start | bytes 221192 | tf_op jit(solution)/shard_map/ppermute | solution.py:560
  16.9 8.7 %copy-start = (bf16[128,1024]{1,0:T(8,128)(2,1)S(1)}, bf16[128,1024]{1,0:T(8,128)(2,1)}, u32[]{:S(2)}) copy-start(bf16[128,1024]{1,0:T(8,128)(2,1)} %g_ref.5) | copy-start | bytes 786436
  16.9 8.7 %copy-start.1 = (f32[3,7,1024]{2,1,0:T(8,128)S(1)}, f32[3,7,1024]{2,1,0:T(8,128)}, u32[]{:S(2)}) copy-start(f32[3,7,1024]{2,1,0:T(8,128)} %taps_ref.5) | copy-start | bytes 258052
  16.9 5.7 %collective-permute-start.7 = (bf16[288,128]{1,0:T(8,128)(2,1)S(1)}, bf16[288,128]{1,0:T(8,128)(2,1)S(1)}, u32[]{:S(2)}, u32[]{:S(2)}) collective-permute-start(bf16[288,128]{1,0:T(8,128)(2,1)S(1)} %get-tuple-element.39), channel_id=1, source_target_pairs={{0,24},{4,28},{8,16},{12,20},{16,8},{20,12},{24,0},{28,4},{1,25},{... | collective-permute-start | bytes 221192 | tf_op jit(solution)/shard_map/ppermute | solution.py:560
  19.1 5.0 %collective-permute-start.8 = (bf16[288,128]{1,0:T(8,128)(2,1)S(1)}, bf16[288,128]{1,0:T(8,128)(2,1)S(1)}, u32[]{:S(2)}, u32[]{:S(2)}) collective-permute-start(bf16[288,128]{1,0:T(8,128)(2,1)S(1)} %get-tuple-element.40), channel_id=1, source_target_pairs={{0,28},{4,24},{8,20},{12,16},{16,12},{20,8},{24,4},{28,0},{1,29},{... | collective-permute-start | bytes 221192 | tf_op jit(solution)/shard_map/ppermute | solution.py:560
  19.4 6.2 %collective-permute-start.9 = (bf16[288,128]{1,0:T(8,128)(2,1)S(1)}, bf16[288,128]{1,0:T(8,128)(2,1)S(1)}, u32[]{:S(2)}, u32[]{:S(2)}) collective-permute-start(bf16[288,128]{1,0:T(8,128)(2,1)S(1)} %get-tuple-element.41), channel_id=1, source_target_pairs={{0,16},{4,20},{8,24},{12,28},{16,0},{20,4},{24,8},{28,12},{1,17},{... | collective-permute-start | bytes 221192 | tf_op jit(solution)/shard_map/ppermute | solution.py:560
  20.9 5.3 %collective-permute-start.10 = (bf16[288,128]{1,0:T(8,128)(2,1)S(1)}, bf16[288,128]{1,0:T(8,128)(2,1)S(1)}, u32[]{:S(2)}, u32[]{:S(2)}) collective-permute-start(bf16[288,128]{1,0:T(8,128)(2,1)S(1)} %get-tuple-element.45), channel_id=1, source_target_pairs={{0,8},{4,12},{8,0},{12,4},{16,24},{20,28},{24,16},{28,20},{1,9},{5... | collective-permute-start | bytes 221192 | tf_op jit(solution)/shard_map/ppermute | solution.py:560
  21.5 5.1 %collective-permute-start.11 = (bf16[288,128]{1,0:T(8,128)(2,1)S(1)}, bf16[288,128]{1,0:T(8,128)(2,1)S(1)}, u32[]{:S(2)}, u32[]{:S(2)}) collective-permute-start(bf16[288,128]{1,0:T(8,128)(2,1)S(1)} %get-tuple-element.46), channel_id=1, source_target_pairs={{0,12},{4,8},{8,4},{12,0},{16,28},{20,24},{24,20},{28,16},{1,13},{... | collective-permute-start | bytes 221192 | tf_op jit(solution)/shard_map/ppermute | solution.py:560
  22.7 4.1 %collective-permute-start.12 = (bf16[288,128]{1,0:T(8,128)(2,1)S(1)}, bf16[288,128]{1,0:T(8,128)(2,1)S(1)}, u32[]{:S(2)}, u32[]{:S(2)}) collective-permute-start(bf16[288,128]{1,0:T(8,128)(2,1)S(1)} %get-tuple-element.47), channel_id=1, source_target_pairs={{0,20},{4,16},{8,28},{12,24},{16,4},{20,0},{24,12},{28,8},{1,21},{... | collective-permute-start | bytes 221192 | tf_op jit(solution)/shard_map/ppermute | solution.py:560
  24.1 2.7 %collective-permute-start.13 = (bf16[288,128]{1,0:T(8,128)(2,1)S(1)}, bf16[288,128]{1,0:T(8,128)(2,1)S(1)}, u32[]{:S(2)}, u32[]{:S(2)}) collective-permute-start(bf16[288,128]{1,0:T(8,128)(2,1)S(1)} %get-tuple-element.48), channel_id=1, source_target_pairs={{0,4},{4,0},{8,12},{12,8},{16,20},{20,16},{24,28},{28,24},{1,5},{5... | collective-permute-start | bytes 221192 | tf_op jit(solution)/shard_map/ppermute | solution.py:560

commit v3 on v2

--- a/solution.py
+++ b/solution.py
@@ -174,12 +174,10 @@
 @functools.cache
 def block_tables(rows):
     bins = np.pi * (np.arange(rows) + 0.5)[:, None] / rows
-    lag = np.arange(-rows, rows)[None, :]
-    window = np.concatenate([np.cos(bins * lag), -np.sin(bins * lag)], axis=0)
-    window_hi, window_lo = split_bf16(window)
-    doubled = np.concatenate([window_hi[:, rows:], window_lo[:, rows:]], axis=1)
-    inv_hi, inv_lo = split_bf16(window[:, rows:].T / rows)
-    return (window_hi, window_lo, doubled, inv_hi, inv_lo)
+    lag = np.arange(rows)[None, :]
+    forward = np.concatenate([np.cos(bins * lag), -np.sin(bins * lag)], axis=0)
+    forward_hi, forward_lo = split_bf16(forward)
+    return (forward_hi, forward_lo, split_bf16(forward.T / rows)[0])
 
 
 def round_up(count, unit):
@@ -271,13 +269,15 @@
         copy.wait()
 
 
-def gather_heads(order, in_refs, edges, firsts, rows):
+def gather(order, in_refs, edges, firsts, pairs, rows):
     me = lax.axis_index("context")
     for mask, in_ref in zip(order, in_refs):
         block = me ^ mask
         edges[block] = in_ref[pl.ds(2 * rows, edges.shape[1]), :].astype(jnp.float32)
-        firsts[block, 0] = in_ref[pl.ds(0, 16), :].astype(jnp.float32)[:8]
-        firsts[block, 1] = in_ref[pl.ds(rows, 16), :].astype(jnp.float32)[:8]
+        for which in range(2):
+            values = in_ref[pl.ds(which * rows, rows), :]
+            firsts[block, which] = values[:16].astype(jnp.float32)[:8]
+            pairs[block, :, pl.ds(which * LANES, LANES)] = values
 
 
 def repair_heads(taps_ref, edges, firsts, joined, heads):
@@ -306,45 +306,48 @@
         heads[block, 5] = cotangent * filtered[0]
 
 
-def to_spectra(order, in_refs, heads, doubled, spec_x, spec_g, rows, halo):
-    me = lax.axis_index("context")
-    for mask, in_ref in zip(order, in_refs):
-        block = me ^ mask
-        parts = []
-        for first, place in ((0, 4), (rows, 5)):
-            head = in_ref[pl.ds(first, 16), :].astype(jnp.float32)
-            head = head_rows(heads[block, place], head, halo).astype(jnp.bfloat16)
-            parts.append(jnp.concatenate([head, in_ref[pl.ds(first + 16, rows - 16), :]], axis=0))
-        pair = jnp.concatenate(parts, axis=1)
-        spectrum = jnp.dot(
-            doubled, jnp.concatenate([pair, pair], axis=0), preferred_element_type=jnp.float32
-        )
-        spec_x[block] = spectrum[:, :LANES]
-        spec_g[block] = spectrum[:, LANES:]
-
-
-def filter_kernel(parcel_ref, h_ref, window_hi, window_lo, out_ref):
+def to_spectra(heads, pairs, forward, spec_x, spec_g, halo):
+    blocks, rows, width = pairs.shape
+    merged = blocks // spec_x.shape[0]
+    for block in range(blocks):
+        fresh = jnp.concatenate([heads[block, 4], heads[block, 5]], axis=1)
+        head = head_rows(fresh, pairs[block, pl.ds(0, 16), :].astype(jnp.float32), halo)
+        pairs[block, pl.ds(0, 16), :] = head.astype(jnp.bfloat16)
+    for index in range(spec_x.shape[0]):
+        signals = pairs[pl.ds(index * merged, merged)].reshape(merged * rows, width)
+        spectrum = jnp.dot(forward, signals, preferred_element_type=jnp.float32)
+        spec_x[index] = spectrum[:, :LANES]
+        spec_g[index] = spectrum[:, LANES:]
+
+
+def filter_kernel(parcel_ref, h_ref, forward_hi, forward_lo, out_ref):
     del parcel_ref
     blocks, two_rows, _ = out_ref.shape
     rows = two_rows // 2
+    sign = jnp.where(lax.broadcasted_iota(jnp.int32, (rows, LANES), 0) % 2 == 0, 1.0, -1.0)
+
+    def product(table, values):
+        return lax.dot_general(
+            table, values, (((1,), (1,)), ((), ())), preferred_element_type=jnp.float32
+        )
+
+    before = None
     for block in range(blocks):
-        here = h_ref[:, pl.ds(block * rows, rows)]
-        if block > 0:
-            before = h_ref[:, pl.ds((block - 1) * rows, rows)]
-        else:
-            before = jnp.zeros_like(here)
-        signal = jnp.concatenate([before, here], axis=1)
+        signal = h_ref[:, pl.ds(block * rows, rows)]
         high = signal.astype(jnp.bfloat16)
         low = (signal - high.astype(jnp.float32)).astype(jnp.bfloat16)
-
-        def product(table, values):
-            return lax.dot_general(
-                table, values, (((1,), (1,)), ((), ())), preferred_element_type=jnp.float32
-            )
-
-        out_ref[block] = (
-            product(window_hi[...], high) + product(window_lo[...], high) + product(window_hi[...], low)
+        spectrum = (
+            product(forward_hi[...], high)
+            + product(forward_lo[...], high)
+            + product(forward_hi[...], low)
         )
+        real, imag = spectrum[:rows], spectrum[rows:]
+        if before is None:
+            out_ref[block] = spectrum
+        else:
+            out_ref[block, pl.ds(0, rows), :] = real - sign * before[1]
+            out_ref[block, pl.ds(rows, rows), :] = imag + sign * before[0]
+        before = (real, imag)
 
 
 def load_tile(ref, count, tile, bins):
@@ -370,12 +373,6 @@
     return results
 
 
-def back_to_rows(spectrum, inv_hi, inv_lo):
-    return jnp.dot(inv_hi, spectrum, preferred_element_type=jnp.float32) + jnp.dot(
-        inv_lo, spectrum, preferred_element_type=jnp.float32
-    )
-
-
 def store_tiles(ref, first_lane, tiles, pair, bins):
     lanes = pl.ds(first_lane, LANES)
     for index, parts in enumerate(zip(*tiles)):
@@ -384,74 +381,80 @@
             ref[index, rows, lanes] = jnp.concatenate(values, axis=0).astype(ref.dtype)
 
 
-def convolve_kernel(order, taps_ref, spec_h, doubled, inv_hi, inv_lo, *refs):
+def convolve_kernel(order, taps_ref, spec_h, forward, inverse, *refs):
     count = len(order)
     in_refs, out_refs = refs[:count], refs[count : 2 * count]
-    spec_x, spec_g, edges, firsts, joined, heads, spec_y, extra = refs[2 * count :]
+    spec_x, spec_g, edges, firsts, joined, heads, pairs, spec_y, extra = refs[2 * count :]
     me = lax.axis_index("context")
-    rows = inv_hi.shape[0]
+    rows = pairs.shape[1]
     halo = taps_ref.shape[1] - 1
-    gather_heads(order, in_refs, edges, firsts, rows)
+    bins = inverse.shape[0]
+    wide = spec_h.shape[0]
+    gather(order, in_refs, edges, firsts, pairs, rows)
     repair_heads(taps_ref, edges, firsts, joined, heads)
-    to_spectra(order, in_refs, heads, doubled[...], spec_x, spec_g, rows, halo)
+    to_spectra(heads, pairs, forward[...], spec_x, spec_g, halo)
 
     def body(pair, carry):
         longs, backs = [], []
         for tile in (2 * pair, 2 * pair + 1):
-            filt = load_tile(spec_h, count, tile, rows)
-            sums = [[(i - j, j) for j in range(i + 1)] for i in range(count)]
-            longs.append(mixed_products(filt, load_tile(spec_x, count, tile, rows), sums, False))
-            sums = [[(j - i, j) for j in range(i, count)] for i in range(count)]
-            backs.append(mixed_products(filt, load_tile(spec_g, count, tile, rows), sums, True))
-        store_tiles(spec_y, 0, longs, pair, rows)
-        store_tiles(spec_y, LANES, backs, pair, rows)
+            filt = load_tile(spec_h, wide, tile, bins)
+            sums = [[(i - j, j) for j in range(i + 1)] for i in range(wide)]
+            longs.append(mixed_products(filt, load_tile(spec_x, wide, tile, bins), sums, False))
+            sums = [[(j - i, j) for j in range(i, wide)] for i in range(wide)]
+            backs.append(mixed_products(filt, load_tile(spec_g, wide, tile, bins), sums, True))
+        store_tiles(spec_y, 0, longs, pair, bins)
+        store_tiles(spec_y, LANES, backs, pair, bins)
         return carry
 
-    lax.fori_loop(0, rows // 16, body, 0)
+    lax.fori_loop(0, bins // 16, body, 0)
     extra[...] = jnp.zeros(extra.shape, jnp.float32)
+    for index in range(wide):
+        both = jnp.dot(inverse[...], spec_y[index], preferred_element_type=jnp.float32).astype(jnp.bfloat16)
+        for part in range(count // wide):
+            block = index * (count // wide) + part
+            here = both[part * rows : (part + 1) * rows]
+            query_f, key_f, value_f, cotangent = [heads[block, which] for which in range(4)]
+            head = here[:16].astype(jnp.float32)
+            long_head, back_head = head[:8, :LANES], head[:8, LANES:]
+            grad_key, grad_value = back_head * value_f, back_head * key_f
+            back = head_rows(grad_key, head[:, LANES:], halo).astype(jnp.bfloat16)
+            pairs[block, :, pl.ds(0, LANES)] = here[:, :LANES]
+            pairs[block, :, pl.ds(LANES, LANES)] = jnp.concatenate([back, here[16:, LANES:]], axis=0)
+            own = (query_f * long_head, grad_value)
+            following = (cotangent * long_head, grad_key, grad_value)
+            for place, value in enumerate(own):
+                extra[block + 1, pl.ds(place * halo, halo), :] = value[:halo]
+            for place, value in enumerate(following):
+                extra[block, pl.ds((2 + place) * halo, halo), :] = value[:halo]
     for mask, out_ref in zip(order, out_refs):
         block = me ^ mask
-        query_f, key_f, value_f, cotangent = [heads[block, which] for which in range(4)]
-        both = back_to_rows(spec_y[block], inv_hi[...], inv_lo[...]).astype(jnp.bfloat16)
-        out_ref[pl.ds(0, rows), :] = both[:, :LANES]
-        head = both[:16].astype(jnp.float32)
-        long_head, back_head = head[:8, :LANES], head[:8, LANES:]
-        grad_key, grad_value = back_head * value_f, back_head * key_f
-        back = head_rows(grad_key, head[:, LANES:], halo).astype(jnp.bfloat16)
-        out_ref[pl.ds(rows, rows), :] = jnp.concatenate([back, both[16:, LANES:]], axis=0)
-        own = (query_f * long_head, grad_value)
-        following = (cotangent * long_head, grad_key, grad_value)
-        for place, value in enumerate(own):
-            extra[block + 1, pl.ds(place * halo, halo), :] = value[:halo]
-        for place, value in enumerate(following):
-            extra[block, pl.ds((2 + place) * halo, halo), :] = value[:halo]
-    for mask, out_ref in zip(order, out_refs):
-        block = me ^ mask
+        for which in range(2):
+            out_ref[pl.ds(which * rows, rows), :] = pairs[block, :, pl.ds(which * LANES, LANES)]
         out_ref[pl.ds(2 * rows, extra.shape[1]), :] = extra[block + 1].astype(jnp.bfloat16)
 
 
-def correlate_kernel(scale, spec_x, spec_g, inv_hi, inv_lo, out_ref, spec_y):
-    count = spec_x.shape[0]
-    rows = inv_hi.shape[0]
+def correlate_kernel(scale, spec_x, spec_g, inverse, out_ref, spec_y):
+    wide = spec_x.shape[0]
+    bins = inverse.shape[0]
 
     def body(pair, carry):
         row = lax.broadcasted_iota(jnp.int32, (8, LANES), 0)
         sign = jnp.where(row % 2 == 0, 1.0, -1.0)
         tiles = []
         for tile in (2 * pair, 2 * pair + 1):
-            real, imag = load_tile(spec_x, count, tile, rows)
-            window_re = [real[0]] + [real[i] - sign * imag[i - 1] for i in range(1, count)]
-            window_im = [imag[0]] + [imag[i] + sign * real[i - 1] for i in range(1, count)]
-            sums = [[(j - lag, j) for j in range(lag, count)] for lag in range(count)]
-            grad = load_tile(spec_g, count, tile, rows)
+            real, imag = load_tile(spec_x, wide, tile, bins)
+            window_re = [real[0]] + [real[i] - sign * imag[i - 1] for i in range(1, wide)]
+            window_im = [imag[0]] + [imag[i] + sign * real[i - 1] for i in range(1, wide)]
+            sums = [[(j - lag, j) for j in range(lag, wide)] for lag in range(wide)]
+            grad = load_tile(spec_g, wide, tile, bins)
             tiles.append(mixed_products((window_re, window_im), grad, sums, True))
-        store_tiles(spec_y, 0, tiles, pair, rows)
+        store_tiles(spec_y, 0, tiles, pair, bins)
         return carry
 
-    lax.fori_loop(0, rows // 16, body, 0)
-    for block in range(count):
-        result = back_to_rows(spec_y[block], inv_hi[...], inv_lo[...])
-        out_ref[:, pl.ds(block * rows, rows)] = result.T * scale
+    lax.fori_loop(0, bins // 16, body, 0)
+    for index in range(wide):
+        result = jnp.dot(inverse[...], spec_y[index], preferred_element_type=jnp.float32)
+        out_ref[:, pl.ds(index * bins, bins)] = result.T * scale
 
 
 def finish_channels(order, places, in_refs, g_ref, taps_ref, filtered_ref, padded, extra, results, leave):
@@ -487,48 +490,41 @@
             leave(index, which)
 
 
-def early_kernel(order, places, g_ref, taps_ref, filtered_ref, *refs):
-    *in_refs, results, padded, extra = refs
+def receive_kernel(order, places, g_ref, taps_ref, filtered_ref, filter_ref, *refs):
+    in_refs = refs[: len(places)]
+    mixed_ref, grads_ref, filter_out, padded, extra, results, sems, filter_sem = refs[-8:]
+    me = lax.axis_index("context")
+    copies = []
+    if filter_ref is not None:
+        copies.append(pltpu.make_async_copy(filter_ref, filter_out.at[0], filter_sem))
+        copies[-1].start()
+
+    def leave(index, which):
+        lanes = pl.ds(pl.multiple_of((me ^ order[places[index]]) * LANES, LANES), LANES)
+        target = mixed_ref.at[:, lanes] if which == 3 else grads_ref.at[which, :, lanes]
+        copies.append(pltpu.make_async_copy(results.at[index, which], target, sems.at[index, which]))
+        copies[-1].start()
+
     finish_channels(
-        order, places, in_refs, g_ref, taps_ref, filtered_ref, padded, extra, results, lambda *_: None
-    )
-
-
-def last_kernel(order, early, places, g_ref, taps_ref, filtered_ref, early_ref, filter_ref, *refs):
-    in_refs = refs[: len(places)]
-    mixed_ref, grads_ref, filter_out, padded, extra, results, early_sems, sems, filter_sem = refs[
-        len(places) :
-    ]
-    me = lax.axis_index("context")
-    copies = [pltpu.make_async_copy(filter_ref, filter_out.at[0], filter_sem)]
-    copies[0].start()
-
-    def leave_from(source, members, semaphores):
-        def leave(index, which):
-            lanes = pl.ds(pl.multiple_of((me ^ order[members[index]]) * LANES, LANES), LANES)
-            target = mixed_ref.at[:, lanes] if which == 3 else grads_ref.at[which, :, lanes]
-            copies.append(
-                pltpu.make_async_copy(source.at[index, which], target, semaphores.at[index, which])
-            )
-            copies[-1].start()
-
-        return leave
-
-    leave = leave_from(early_ref, early, early_sems)
-    for index in range(len(early)):
-        for which in range(4):
-            leave(index, which)
-    finish_channels(
-        order, places, in_refs, g_ref, taps_ref, filtered_ref, padded, extra, results,
-        leave_from(results, places, sems),
+        order, places, in_refs, g_ref, taps_ref, filtered_ref, padded, extra, results, leave
     )
     for copy in copies:
         copy.wait()
 
 
-def on_device(kernel, out_shape, scratch, args, in_hbm=0, pin=True):
+def last_kernel(order, places, g_ref, taps_ref, filtered_ref, *refs):
+    in_refs, refs = refs[: len(places)], refs[len(places) + 2 :]
+    mixed_ref, grads_ref, padded, extra, results, sems = refs
+    receive_kernel(
+        order, places, g_ref, taps_ref, filtered_ref, None, *in_refs,
+        mixed_ref, grads_ref, None, padded, extra, results, sems, None,
+    )
+
+
+def on_device(kernel, out_shape, scratch, args, in_hbm=0, pin=True, updated=0):
     whole = pl.BlockSpec(memory_space=pltpu.VMEM)
     outside = pl.BlockSpec(memory_space=pltpu.HBM if pin else pl.ANY)
+    last = len(args) - updated
     args = [
         pltpu.with_memory_space_constraint(arg, pltpu.HBM) if pin and place < in_hbm else arg
         for place, arg in enumerate(args)
@@ -536,10 +532,11 @@
     return pl.pallas_call(
         kernel,
         out_shape=out_shape,
-        in_specs=[outside if place < in_hbm else whole for place in range(len(args))],
+        in_specs=[outside if place < in_hbm or place >= last else whole for place in range(len(args))],
         out_specs=jax.tree.map(
             lambda out: whole if isinstance(out, jax.ShapeDtypeStruct) else outside, out_shape
         ),
+        input_output_aliases={last + place: place for place in range(updated)},
         scratch_shapes=[
             pltpu.VMEM(shape, jnp.float32) if isinstance(shape, tuple) else shape for shape in scratch
         ],
@@ -567,13 +564,15 @@
     blocks = lax.axis_size("context")
     halo = short_taps.shape[1] - 1
     seq_len = rows * blocks
-    window_hi, window_lo, doubled, inv_hi, inv_lo = [jnp.asarray(t) for t in block_tables(rows)]
+    merged = 2
+    wide = merged * rows
+    forward_hi, forward_lo, inverse = [jnp.asarray(table) for table in block_tables(wide)]
     edge_rows = round_up(5 * halo, 16)
     order = exchange_order(blocks)
     parcels = [jax.ShapeDtypeStruct((2 * rows + edge_rows, LANES), jnp.bfloat16)] * blocks
-    spectra = (blocks, 2 * rows, LANES)
+    spectra = (blocks // merged, 2 * wide, LANES)
     own_taps = (*short_taps.shape[:2], LANES)
-    kept = (long_filter[0], window_hi, window_lo)
+    kept = (long_filter[0], forward_hi, forward_lo)
 
     *sent, filtered, own, filter_here, hi_here, lo_here = on_device(
         functools.partial(send_kernel, order),
@@ -611,43 +610,48 @@
             (blocks, 2, 8, LANES),
             (3, blocks, 24, LANES),
             (blocks, 6, 8, LANES),
-            pltpu.VMEM((blocks, 2 * rows, 2 * LANES), jnp.bfloat16),
+            pltpu.VMEM((blocks, rows, 2 * LANES), jnp.bfloat16),
+            pltpu.VMEM((*spectra[:2], 2 * LANES), jnp.bfloat16),
             (blocks + 1, edge_rows, LANES),
         ],
-        (own, spec_h, doubled, inv_hi, inv_lo, *arrived),
+        (own, spec_h, hi_here, inverse, *arrived),
     )
     returned = exchange(order, results)
     filter_grad = on_device(
         functools.partial(correlate_kernel, 1.0 / math.sqrt(seq_len)),
         jax.ShapeDtypeStruct(long_filter.shape[1:], jnp.float32),
         [pltpu.VMEM(spectra, jnp.bfloat16)],
-        (spec_x, spec_g, inv_hi, inv_lo),
+        (spec_x, spec_g, inverse),
     )
     late = list(range(blocks // 2 - 1, blocks - 1))
     early = [place for place in range(blocks) if place not in late]
-    padded = [(2, 3, rows + 16, LANES), (2, edge_rows + 8, LANES)]
+    outputs = (
+        pltpu.HBM((rows, channels), jnp.bfloat16),
+        pltpu.HBM((3, rows, channels), jnp.bfloat16),
+        pltpu.HBM(long_filter.shape, jnp.float32),
+    )
+
+    def working(places):
+        return [
+            (2, 3, rows + 16, LANES),
+            (2, edge_rows + 8, LANES),
+            pltpu.VMEM((len(places), 4, rows, LANES), jnp.bfloat16),
+            pltpu.SemaphoreType.DMA((len(places), 4)),
+        ]
+
     common = (grad_mixed, short_taps, filtered)
-    early_results = on_device(
-        functools.partial(early_kernel, order, early),
-        jax.ShapeDtypeStruct((len(early), 4, rows, LANES), jnp.bfloat16),
-        padded,
-        (*common, *(returned[place] for place in early)),
-    )
-    mixed_out, input_grads, filter_grad = on_device(
-        functools.partial(last_kernel, order, early, late),
-        (
-            pltpu.HBM((rows, channels), jnp.bfloat16),
-            pltpu.HBM((3, rows, channels), jnp.bfloat16),
-            pltpu.HBM(long_filter.shape, jnp.float32),
-        ),
-        padded
-        + [
-            pltpu.VMEM((len(late), 4, rows, LANES), jnp.bfloat16),
-            pltpu.SemaphoreType.DMA((len(early), 4)),
-            pltpu.SemaphoreType.DMA((len(late), 4)),
-            pltpu.SemaphoreType.DMA(()),
-        ],
-        (*common, early_results, filter_grad, *(returned[place] for place in late)),
+    *begun, filter_grad = on_device(
+        functools.partial(receive_kernel, order, early),
+        outputs,
+        [*working(early), pltpu.SemaphoreType.DMA(())],
+        (*common, filter_grad, *(returned[place] for place in early)),
+    )
+    mixed_out, input_grads = on_device(
+        functools.partial(last_kernel, order, late),
+        outputs[:2],
+        working(late),
+        (*common, *(returned[place] for place in late), *begun),
+        updated=2,
     )
     return (mixed_out, input_grads, filter_grad)
 
@@ -657,7 +661,7 @@
     halo = short_taps.shape[1] - 1
     blocks = lax.axis_size("context")
     power_of_two = blocks & (blocks - 1) == 0
-    fits = power_of_two and channels == blocks * LANES and rows % 128 == 0 and halo <= 8
+    fits = power_of_two and blocks > 1 and channels == blocks * LANES and rows % 128 == 0 and halo <= 8
     chosen = block_shards if fits else general_shards
     return chosen(query_proj, key_proj, value_proj, short_taps, long_filter, grad_mixed)
 

time: 28.5 us -> 28.1 us (0.986)
  transfers between devices with their start and end apart: 14 -> 14, of which waited for: 7 -> 6; matrix products, arithmetic and copies ran while one was open for 0% -> 0% of each run, Pallas kernels for 10% -> 12%
where the time goes in v3:
time: 28.1 us; the launch traced here: 27.9 us
  starting transfers between devices  14 us (50%)
  Pallas kernels  8.91 us (32%)
  waiting for transfers between devices  4.28 us (15%)
  between operations  0.73 us (3%)
    ppermute x14, starting transfers between devices, exchange(): lax.ppermute(parcel, 'context', [(i, i ^ mask) for i in range(count)])  14 us
    pallas_call x6, Pallas kernels, on_device(): pl.pallas_call(kernel, out_shape=out_shape, in_specs=[outside if place <...  8.91 us
    ppermute x14, waiting for transfers between devices, exchange(): lax.ppermute(parcel, 'context', [(i, i ^ mask) for i in range(count)])  4.28 us
  transfers between devices with their start and end apart: 14, of which 6 were waited for; matrix products, arithmetic and copies ran while one was open for 0% of the time, Pallas kernels for 12%

profile of v3, /device:TPU:0, one launch (start us, length us, event | category | flops | bytes accessed | tf_op | source)
XLA Modules:
  0.0 27.9 jit_solution(10517809991344187568)
XLA Ops:
  0.6 2.2 %shard_map.112 = (bf16[288,128]{1,0:T(8,128)(2,1)S(1)}, bf16[288,128]{1,0:T(8,128)(2,1)S(1)}, bf16[288,128]{1,0:T(8,128)(2,1)S(1)}, bf16[288,128]{1,0:T(8,128)(2...) custom-call(bf16[128,1024]{1,0:T(8,128)(2,1)} %q_ref.1, ...), custom_call_target="tpu_custom_call" | custom-call | tf_op jit(solution)/shard_map/pallas_call | solution.py:532
  2.9 0.0 copy-start.1
  2.9 4.0 %collective-permute-start = (bf16[288,128]{1,0:T(8,128)(2,1)S(1)}, bf16[288,128]{1,0:T(8,128)(2,1)S(1)}, u32[]{:S(2)}, u32[]{:S(2)}) collective-permute-start(bf16[288,128]{1,0:T(8,128)(2,1)S(1)} %get-tuple-element.33), channel_id=1, source_target_pairs={{0,24},{4,28},{8,16},{12,20},{16,8},{20,12},{24,0},{28,4},{1,25},{... | collective-permute-start | bytes 221192 | tf_op jit(solution)/shard_map/ppermute | solution.py:557
  6.9 0.0 collective-permute-start.1
  6.9 1.2 %collective-permute-start.2 = (bf16[288,128]{1,0:T(8,128)(2,1)S(1)}, bf16[288,128]{1,0:T(8,128)(2,1)S(1)}, u32[]{:S(2)}, u32[]{:S(2)}) collective-permute-start(bf16[288,128]{1,0:T(8,128)(2,1)S(1)} %get-tuple-element.38), channel_id=1, source_target_pairs={{0,16},{4,20},{8,24},{12,28},{16,0},{20,4},{24,8},{28,12},{1,17},{... | collective-permute-start | bytes 221192 | tf_op jit(solution)/shard_map/ppermute | solution.py:557
  8.0 1.5 %collective-permute-start.3 = (bf16[288,128]{1,0:T(8,128)(2,1)S(1)}, bf16[288,128]{1,0:T(8,128)(2,1)S(1)}, u32[]{:S(2)}, u32[]{:S(2)}) collective-permute-start(bf16[288,128]{1,0:T(8,128)(2,1)S(1)} %get-tuple-element.39), channel_id=1, source_target_pairs={{0,8},{4,12},{8,0},{12,4},{16,24},{20,28},{24,16},{28,20},{1,9},{5... | collective-permute-start | bytes 221192 | tf_op jit(solution)/shard_map/ppermute | solution.py:557
  9.5 0.6 %collective-permute-start.4 = (bf16[288,128]{1,0:T(8,128)(2,1)S(1)}, bf16[288,128]{1,0:T(8,128)(2,1)S(1)}, u32[]{:S(2)}, u32[]{:S(2)}) collective-permute-start(bf16[288,128]{1,0:T(8,128)(2,1)S(1)} %get-tuple-element.40), channel_id=1, source_target_pairs={{0,12},{4,8},{8,4},{12,0},{16,28},{20,24},{24,20},{28,16},{1,13},{... | collective-permute-start | bytes 221192 | tf_op jit(solution)/shard_map/ppermute | solution.py:557
  10.1 0.0 collective-permute-done.parcel_ref.refs_0_
  10.1 0.6 %collective-permute-start.5 = (bf16[288,128]{1,0:T(8,128)(2,1)S(1)}, bf16[288,128]{1,0:T(8,128)(2,1)S(1)}, u32[]{:S(2)}, u32[]{:S(2)}) collective-permute-start(bf16[288,128]{1,0:T(8,128)(2,1)S(1)} %get-tuple-element.41), channel_id=1, source_target_pairs={{0,20},{4,16},{8,28},{12,24},{16,4},{20,0},{24,12},{28,8},{1,21},{... | collective-permute-start | bytes 221192 | tf_op jit(solution)/shard_map/ppermute | solution.py:557
  10.6 1.7 %collective-permute-done.1.refs_1_ = bf16[288,128]{1,0:T(8,128)(2,1)S(1)} collective-permute-done((bf16[288,128]{1,0:T(8,128)(2,1)S(1)}, bf16[288,128]{1,0:T(8,128)(2,1)S(1)}, u32[]{:S(2)}, u32[]{:S(2)}) %collective-permute-start.1) | collective-permute-done | bytes 73760 | tf_op jit(solution)/shard_map/ppermute | solution.py:557
  12.3 0.0 collective-permute-start.6
  12.3 1.0 %shard_map.113.spec_h = f32[4,512,128]{2,1,0:T(8,128)S(1)} custom-call(bf16[288,128]{1,0:T(8,128)(2,1)S(1)} %collective-permute-done.parcel_ref.refs_0_, f32[128,1024]{1,0:T(8,128)S(1)} %get-tuple-element.34.h_ref, bf16[512,256]{1,0:T(8,128)(2,1)S(1)} %get-tuple-element.35.forward_hi.forward, bf16[512,256]{1,0:T(8,128)(2,1)S(1)} %get-tuple-element.36.forward_lo), custom_call_target="tpu_custom_call" | custom-call | tf_op jit(solution)/shard_map/pallas_call | solution.py:532
  13.3 0.0 collective-permute-done.2.refs_2_
  13.3 0.0 collective-permute-done.3.refs_3_
  13.3 0.8 %collective-permute-done.4.refs_4_ = bf16[288,128]{1,0:T(8,128)(2,1)S(1)} collective-permute-done((bf16[288,128]{1,0:T(8,128)(2,1)S(1)}, bf16[288,128]{1,0:T(8,128)(2,1)S(1)}, u32[]{:S(2)}, u32[]{:S(2)}) %collective-permute-start.4) | collective-permute-done | bytes 73760 | tf_op jit(solution)/shard_map/ppermute | solution.py:557
  14.1 0.3 collective-permute-done.5.refs_5_
  14.4 0.0 collective-permute-done.6.refs_6_
  14.4 0.0 copy-done.1
  14.4 2.0 %shard_map.114 = (bf16[288,128]{1,0:T(8,128)(2,1)S(1)}, bf16[288,128]{1,0:T(8,128)(2,1)S(1)}, bf16[288,128]{1,0:T(8,128)(2,1)S(1)}, bf16[288,128]{1,0:T(8,128)(2...) custom-call(f32[3,7,128]{2,1,0:T(8,128)S(1)} %get-tuple-element.32.t, ...), custom_call_target="tpu_custom_call" | custom-call | tf_op jit(solution)/shard_map/pallas_call | solution.py:532
  16.4 0.0 copy-start
  16.4 0.0 copy-start.2
  16.4 2.2 %collective-permute-start.11 = (bf16[288,128]{1,0:T(8,128)(2,1)S(1)}, bf16[288,128]{1,0:T(8,128)(2,1)S(1)}, u32[]{:S(2)}, u32[]{:S(2)}) collective-permute-start(bf16[288,128]{1,0:T(8,128)(2,1)S(1)} %get-tuple-element.50), channel_id=1, source_target_pairs={{0,24},{4,28},{8,16},{12,20},{16,8},{20,12},{24,0},{28,4},{1,25},{... | collective-permute-start | bytes 221192 | tf_op jit(solution)/shard_map/ppermute | solution.py:557
  18.6 0.3 collective-permute-start.12
  18.9 1.5 %collective-permute-start.7 = (bf16[288,128]{1,0:T(8,128)(2,1)S(1)}, bf16[288,128]{1,0:T(8,128)(2,1)S(1)}, u32[]{:S(2)}, u32[]{:S(2)}) collective-permute-start(bf16[288,128]{1,0:T(8,128)(2,1)S(1)} %get-tuple-element.44), channel_id=1, source_target_pairs={{0,8},{4,12},{8,0},{12,4},{16,24},{20,28},{24,16},{28,20},{1,9},{5... | collective-permute-start | bytes 221192 | tf_op jit(solution)/shard_map/ppermute | solution.py:557
  20.4 0.6 %collective-permute-start.13 = (bf16[288,128]{1,0:T(8,128)(2,1)S(1)}, bf16[288,128]{1,0:T(8,128)(2,1)S(1)}, u32[]{:S(2)}, u32[]{:S(2)}) collective-permute-start(bf16[288,128]{1,0:T(8,128)(2,1)S(1)} %get-tuple-element.52), channel_id=1, source_target_pairs={{0,16},{4,20},{8,24},{12,28},{16,0},{20,4},{24,8},{28,12},{1,17},{... | collective-permute-start | bytes 221192 | tf_op jit(solution)/shard_map/ppermute | solution.py:557
  21.0 1.2 %collective-permute-start.8 = (bf16[288,128]{1,0:T(8,128)(2,1)S(1)}, bf16[288,128]{1,0:T(8,128)(2,1)S(1)}, u32[]{:S(2)}, u32[]{:S(2)}) collective-permute-start(bf16[288,128]{1,0:T(8,128)(2,1)S(1)} %get-tuple-element.45), channel_id=1, source_target_pairs={{0,12},{4,8},{8,4},{12,0},{16,28},{20,24},{24,20},{28,16},{1,13},{... | collective-permute-start | bytes 221192 | tf_op jit(solution)/shard_map/ppermute | solution.py:557
  22.2 0.0 collective-permute-done.11.refs_0_
  22.2 0.5 %collective-permute-start.9 = (bf16[288,128]{1,0:T(8,128)(2,1)S(1)}, bf16[288,128]{1,0:T(8,128)(2,1)S(1)}, u32[]{:S(2)}, u32[]{:S(2)}) collective-permute-start(bf16[288,128]{1,0:T(8,128)(2,1)S(1)} %get-tuple-element.46), channel_id=1, source_target_pairs={{0,20},{4,16},{8,28},{12,24},{16,4},{20,0},{24,12},{28,8},{1,21},{... | collective-permute-start | bytes 221192 | tf_op jit(solution)/shard_map/ppermute | solution.py:557
  22.7 0.9 %collective-permute-done.12.refs_1_ = bf16[288,128]{1,0:T(8,128)(2,1)S(1)} collective-permute-done((bf16[288,128]{1,0:T(8,128)(2,1)S(1)}, bf16[288,128]{1,0:T(8,128)(2,1)S(1)}, u32[]{:S(2)}, u32[]{:S(2)}) %collective-permute-start.12) | collective-permute-done | bytes 73760 | tf_op jit(solution)/shard_map/ppermute | solution.py:557
  23.6 0.0 collective-permute-start.10
  23.6 1.0 %shard_map.115.filter_ref = f32[128,1024]{1,0:T(8,128)S(1)} custom-call(f32[4,512,128]{2,1,0:T(8,128)S(1)} %get-tuple-element.48.spec_x, f32[4,512,128]{2,1,0:T(8,128)S(1)} %get-tuple-element.49.spec_g, bf16[256,512]{1,0:T(8,128)(2,1)S(1)} %copy-done.1), custom_call_target="tpu_custom_call" | custom-call | tf_op jit(solution)/shard_map/pallas_call | solution.py:532
  24.6 0.5 %collective-permute-done.13.refs_2_ = bf16[288,128]{1,0:T(8,128)(2,1)S(1)} collective-permute-done((bf16[288,128]{1,0:T(8,128)(2,1)S(1)}, bf16[288,128]{1,0:T(8,128)(2,1)S(1)}, u32[]{:S(2)}, u32[]{:S(2)}) %collective-permute-start.13) | collective-permute-done | bytes 73760 | tf_op jit(solution)/shard_map/ppermute | solution.py:557
  25.1 0.0 copy-done
  25.1 0.0 copy-done.2
  25.1 1.4 %shard_map.116 = (bf16[128,1024]{1,0:T(8,128)(2,1)}, bf16[3,128,1024]{2,1,0:T(8,128)(2,1)}, f32[1,128,1024]{2,1,0:T(8,128)}) custom-call(bf16[128,1024]{1,0:T(8,128)(2,1)S(1)} %copy-done, f32[3,7,1024]{2,1,0:T(8,128)S(1)} %copy-done.2, f32[3,8,128,128]{3,2,1,0:T(8,128)S(1)} %get-tuple-element.31.filtered_ref, f32[128,1024]{1,0:T(8,128)S(1)} %shard_map.115.filter_ref, ...), custom_call_target="tpu_custom_call" | custom-call | tf_op jit(solution)/shard_map/pallas_call | solution.py:532
  26.5 0.0 collective-permute-done.7.refs_0_
  26.5 0.1 collective-permute-done.8.refs_1_
  26.6 0.0 collective-permute-done.9.refs_2_
  26.6 0.0 collective-permute-done.10.refs_3_
  26.6 1.3 %shard_map.117 = (bf16[128,1024]{1,0:T(8,128)(2,1)}, bf16[3,128,1024]{2,1,0:T(8,128)(2,1)}) custom-call(bf16[128,1024]{1,0:T(8,128)(2,1)S(1)} %copy-done, f32[3,7,1024]{2,1,0:T(8,128)S(1)} %copy-done.2, f32[3,8,128,128]{3,2,1,0:T(8,128)S(1)} %get-tuple-element.31.filtered_ref, ...), custom_call_target="tpu_custom_call", output_to_operand_aliasing={{0}: (7, {}), {1}: (8, {})} | custom-call | tf_op jit(solution)/shard_map/pallas_call | solution.py:532
Async XLA Ops:
  2.9 11.5 %copy-start.1 = (bf16[256,512]{1,0:T(8,128)(2,1)S(1)}, bf16[256,512]{1,0:T(8,128)(2,1)}, u32[]{:S(2)}) copy-start(bf16[256,512]{1,0:T(8,128)(2,1)} %constant.8.clone.inverse) | copy-start | bytes 786436
  2.9 7.2 %collective-permute-start = (bf16[288,128]{1,0:T(8,128)(2,1)S(1)}, bf16[288,128]{1,0:T(8,128)(2,1)S(1)}, u32[]{:S(2)}, u32[]{:S(2)}) collective-permute-start(bf16[288,128]{1,0:T(8,128)(2,1)S(1)} %get-tuple-element.33), channel_id=1, source_target_pairs={{0,24},{4,28},{8,16},{12,20},{16,8},{20,12},{24,0},{28,4},{1,25},{... | collective-permute-start | bytes 221192 | tf_op jit(solution)/shard_map/ppermute | solution.py:557
  6.9 5.5 %collective-permute-start.1 = (bf16[288,128]{1,0:T(8,128)(2,1)S(1)}, bf16[288,128]{1,0:T(8,128)(2,1)S(1)}, u32[]{:S(2)}, u32[]{:S(2)}) collective-permute-start(bf16[288,128]{1,0:T(8,128)(2,1)S(1)} %get-tuple-element.37), channel_id=1, source_target_pairs={{0,28},{4,24},{8,20},{12,16},{16,12},{20,8},{24,4},{28,0},{1,29},{... | collective-permute-start | bytes 221192 | tf_op jit(solution)/shard_map/ppermute | solution.py:557
  6.9 6.4 %collective-permute-start.2 = (bf16[288,128]{1,0:T(8,128)(2,1)S(1)}, bf16[288,128]{1,0:T(8,128)(2,1)S(1)}, u32[]{:S(2)}, u32[]{:S(2)}) collective-permute-start(bf16[288,128]{1,0:T(8,128)(2,1)S(1)} %get-tuple-element.38), channel_id=1, source_target_pairs={{0,16},{4,20},{8,24},{12,28},{16,0},{20,4},{24,8},{28,12},{1,17},{... | collective-permute-start | bytes 221192 | tf_op jit(solution)/shard_map/ppermute | solution.py:557
  8.0 5.3 %collective-permute-start.3 = (bf16[288,128]{1,0:T(8,128)(2,1)S(1)}, bf16[288,128]{1,0:T(8,128)(2,1)S(1)}, u32[]{:S(2)}, u32[]{:S(2)}) collective-permute-start(bf16[288,128]{1,0:T(8,128)(2,1)S(1)} %get-tuple-element.39), channel_id=1, source_target_pairs={{0,8},{4,12},{8,0},{12,4},{16,24},{20,28},{24,16},{28,20},{1,9},{5... | collective-permute-start | bytes 221192 | tf_op jit(solution)/shard_map/ppermute | solution.py:557
  9.5 4.6 %collective-permute-start.4 = (bf16[288,128]{1,0:T(8,128)(2,1)S(1)}, bf16[288,128]{1,0:T(8,128)(2,1)S(1)}, u32[]{:S(2)}, u32[]{:S(2)}) collective-permute-start(bf16[288,128]{1,0:T(8,128)(2,1)S(1)} %get-tuple-element.40), channel_id=1, source_target_pairs={{0,12},{4,8},{8,4},{12,0},{16,28},{20,24},{24,20},{28,16},{1,13},{... | collective-permute-start | bytes 221192 | tf_op jit(solution)/shard_map/ppermute | solution.py:557
  10.1 4.3 %collective-permute-start.5 = (bf16[288,128]{1,0:T(8,128)(2,1)S(1)}, bf16[288,128]{1,0:T(8,128)(2,1)S(1)}, u32[]{:S(2)}, u32[]{:S(2)}) collective-permute-start(bf16[288,128]{1,0:T(8,128)(2,1)S(1)} %get-tuple-element.41), channel_id=1, source_target_pairs={{0,20},{4,16},{8,28},{12,24},{16,4},{20,0},{24,12},{28,8},{1,21},{... | collective-permute-start | bytes 221192 | tf_op jit(solution)/shard_map/ppermute | solution.py:557
  12.3 2.1 %collective-permute-start.6 = (bf16[288,128]{1,0:T(8,128)(2,1)S(1)}, bf16[288,128]{1,0:T(8,128)(2,1)S(1)}, u32[]{:S(2)}, u32[]{:S(2)}) collective-permute-start(bf16[288,128]{1,0:T(8,128)(2,1)S(1)} %get-tuple-element.42), channel_id=1, source_target_pairs={{0,4},{4,0},{8,12},{12,8},{16,20},{20,16},{24,28},{28,24},{1,5},{5... | collective-permute-start | bytes 221192 | tf_op jit(solution)/shard_map/ppermute | solution.py:557
  16.4 8.7 %copy-start = (bf16[128,1024]{1,0:T(8,128)(2,1)S(1)}, bf16[128,1024]{1,0:T(8,128)(2,1)}, u32[]{:S(2)}) copy-start(bf16[128,1024]{1,0:T(8,128)(2,1)} %g_ref.5) | copy-start | bytes 786436
  16.4 8.7 %copy-start.2 = (f32[3,7,1024]{2,1,0:T(8,128)S(1)}, f32[3,7,1024]{2,1,0:T(8,128)}, u32[]{:S(2)}) copy-start(f32[3,7,1024]{2,1,0:T(8,128)} %taps_ref.5) | copy-start | bytes 258052
  16.4 5.7 %collective-permute-start.11 = (bf16[288,128]{1,0:T(8,128)(2,1)S(1)}, bf16[288,128]{1,0:T(8,128)(2,1)S(1)}, u32[]{:S(2)}, u32[]{:S(2)}) collective-permute-start(bf16[288,128]{1,0:T(8,128)(2,1)S(1)} %get-tuple-element.50), channel_id=1, source_target_pairs={{0,24},{4,28},{8,16},{12,20},{16,8},{20,12},{24,0},{28,4},{1,25},{... | collective-permute-start | bytes 221192 | tf_op jit(solution)/shard_map/ppermute | solution.py:557
  18.6 5.0 %collective-permute-start.12 = (bf16[288,128]{1,0:T(8,128)(2,1)S(1)}, bf16[288,128]{1,0:T(8,128)(2,1)S(1)}, u32[]{:S(2)}, u32[]{:S(2)}) collective-permute-start(bf16[288,128]{1,0:T(8,128)(2,1)S(1)} %get-tuple-element.51), channel_id=1, source_target_pairs={{0,28},{4,24},{8,20},{12,16},{16,12},{20,8},{24,4},{28,0},{1,29},{... | collective-permute-start | bytes 221192 | tf_op jit(solution)/shard_map/ppermute | solution.py:557
  18.9 7.6 %collective-permute-start.7 = (bf16[288,128]{1,0:T(8,128)(2,1)S(1)}, bf16[288,128]{1,0:T(8,128)(2,1)S(1)}, u32[]{:S(2)}, u32[]{:S(2)}) collective-permute-start(bf16[288,128]{1,0:T(8,128)(2,1)S(1)} %get-tuple-element.44), channel_id=1, source_target_pairs={{0,8},{4,12},{8,0},{12,4},{16,24},{20,28},{24,16},{28,20},{1,9},{5... | collective-permute-start | bytes 221192 | tf_op jit(solution)/shard_map/ppermute | solution.py:557
  20.4 4.7 %collective-permute-start.13 = (bf16[288,128]{1,0:T(8,128)(2,1)S(1)}, bf16[288,128]{1,0:T(8,128)(2,1)S(1)}, u32[]{:S(2)}, u32[]{:S(2)}) collective-permute-start(bf16[288,128]{1,0:T(8,128)(2,1)S(1)} %get-tuple-element.52), channel_id=1, source_target_pairs={{0,16},{4,20},{8,24},{12,28},{16,0},{20,4},{24,8},{28,12},{1,17},{... | collective-permute-start | bytes 221192 | tf_op jit(solution)/shard_map/ppermute | solution.py:557
  21.0 5.6 %collective-permute-start.8 = (bf16[288,128]{1,0:T(8,128)(2,1)S(1)}, bf16[288,128]{1,0:T(8,128)(2,1)S(1)}, u32[]{:S(2)}, u32[]{:S(2)}) collective-permute-start(bf16[288,128]{1,0:T(8,128)(2,1)S(1)} %get-tuple-element.45), channel_id=1, source_target_pairs={{0,12},{4,8},{8,4},{12,0},{16,28},{20,24},{24,20},{28,16},{1,13},{... | collective-permute-start | bytes 221192 | tf_op jit(solution)/shard_map/ppermute | solution.py:557
  22.2 4.4 %collective-permute-start.9 = (bf16[288,128]{1,0:T(8,128)(2,1)S(1)}, bf16[288,128]{1,0:T(8,128)(2,1)S(1)}, u32[]{:S(2)}, u32[]{:S(2)}) collective-permute-start(bf16[288,128]{1,0:T(8,128)(2,1)S(1)} %get-tuple-element.46), channel_id=1, source_target_pairs={{0,20},{4,16},{8,28},{12,24},{16,4},{20,0},{24,12},{28,8},{1,21},{... | collective-permute-start | bytes 221192 | tf_op jit(solution)/shard_map/ppermute | solution.py:557
  23.6 3.0 %collective-permute-start.10 = (bf16[288,128]{1,0:T(8,128)(2,1)S(1)}, bf16[288,128]{1,0:T(8,128)(2,1)S(1)}, u32[]{:S(2)}, u32[]{:S(2)}) collective-permute-start(bf16[288,128]{1,0:T(8,128)(2,1)S(1)} %get-tuple-element.47), channel_id=1, source_target_pairs={{0,4},{4,0},{8,12},{12,8},{16,20},{20,16},{24,28},{28,24},{1,5},{5... | collective-permute-start | bytes 221192 | tf_op jit(solution)/shard_map/ppermute | solution.py:557

commit v4 on v3

--- a/solution.py
+++ b/solution.py
@@ -200,62 +200,55 @@
     return running
 
 
-def send_kernel(order, q_ref, k_ref, v_ref, g_ref, taps_ref, h_ref, hi_ref, lo_ref, *refs):
-    count = len(order)
-    outs = refs[:count]
-    filtered_ref, own_ref, h_here, hi_here, lo_here = refs[count : count + 5]
-    landed, taps, padded, extra, arrivals, kept = refs[count + 5 :]
+def send_kernel(order, places, extras, q_ref, k_ref, v_ref, g_ref, taps_ref, *refs):
+    sources, refs = refs[:extras], refs[extras:]
+    outs, refs = refs[: len(places)], refs[len(places) :]
+    landed, taps, padded, extra, arrivals, kept = refs[-6:]
+    filtered_ref, *brought = refs[:-6]
     me = lax.axis_index("context")
     rows = q_ref.shape[0]
     halo = taps_ref.shape[1] - 1
 
-    def lanes_of(place):
-        return pl.ds(pl.multiple_of((me ^ order[place]) * LANES, LANES), LANES)
-
-    def fetches(place):
-        lanes = lanes_of(place)
+    def fetches(index):
+        lanes = pl.ds(pl.multiple_of((me ^ order[places[index]]) * LANES, LANES), LANES)
         copies = [
-            pltpu.make_async_copy(
-                taps_ref.at[:, :, lanes], taps.at[place], arrivals.at[place, 4]
-            )
+            pltpu.make_async_copy(taps_ref.at[:, :, lanes], taps.at[index], arrivals.at[index, 4])
         ]
         for which, ref in enumerate((q_ref, k_ref, v_ref, g_ref)):
             copies.append(
                 pltpu.make_async_copy(
-                    ref.at[:, lanes], landed.at[place, which], arrivals.at[place, which]
+                    ref.at[:, lanes], landed.at[index, which], arrivals.at[index, which]
                 )
             )
         return copies
 
     keeps = [
         pltpu.make_async_copy(source, target, kept.at[index])
-        for index, (source, target) in enumerate(
-            ((h_ref, h_here), (hi_ref, hi_here), (lo_ref, lo_here))
-        )
+        for index, (source, target) in enumerate(zip(sources, brought))
     ]
-    for place in range(count):
-        for copy in fetches(place):
+    for index in range(len(places)):
+        for copy in fetches(index):
             copy.start()
     for copy in keeps:
         copy.start()
-    for place in range(count):
-        slot = place % padded.shape[0]
-        out_ref = outs[place]
+    for index in range(len(places)):
+        slot = index % padded.shape[0]
+        out_ref = outs[index]
         padded[slot, :, pl.ds(0, 8), :] = jnp.zeros((3, 8, LANES), jnp.float32)
         extra[slot, pl.ds(5 * halo, extra.shape[1] - 5 * halo), :] = jnp.zeros(
             (extra.shape[1] - 5 * halo, LANES), jnp.float32
         )
-        for copy in fetches(place):
+        for copy in fetches(index):
             copy.wait()
         filtered = []
         for which in range(3):
-            padded[slot, which, pl.ds(8, rows), :] = landed[place, which].astype(jnp.float32)
-            weights = tap_rows(taps.at[place], which, pl.ds(0, LANES))
+            padded[slot, which, pl.ds(8, rows), :] = landed[index, which].astype(jnp.float32)
+            weights = tap_rows(taps.at[index], which, pl.ds(0, LANES))
             result = short_filter(padded.at[slot, which], rows, weights)
-            filtered_ref[which, place] = result
+            filtered_ref[which, index] = result
             filtered.append(result)
         query_f, key_f, value_f = filtered
-        cotangent = landed[place, 3].astype(jnp.float32)
+        cotangent = landed[index, 3].astype(jnp.float32)
         gated = head_rows(padded[slot, 1, pl.ds(8, 8), :], key_f * value_f, halo)
         grad_long = head_rows(cotangent[:8], cotangent * query_f, halo)
         out_ref[pl.ds(0, rows), :] = gated.astype(jnp.bfloat16)
@@ -264,7 +257,8 @@
         for position, (which, first) in enumerate(pieces):
             extra[slot, pl.ds(position * halo, halo), :] = padded[slot, which, pl.ds(8 + first, halo), :]
         out_ref[pl.ds(2 * rows, extra.shape[1]), :] = extra[slot].astype(jnp.bfloat16)
-    own_ref[...] = taps[order.index(0)]
+    if order[places[-1]] == 0:
+        brought[-1][...] = taps[len(places) - 1]
     for copy in keeps:
         copy.wait()
 
@@ -320,8 +314,7 @@
         spec_g[index] = spectrum[:, LANES:]
 
 
-def filter_kernel(parcel_ref, h_ref, forward_hi, forward_lo, out_ref):
-    del parcel_ref
+def filter_kernel(h_ref, forward_hi, forward_lo, out_ref):
     blocks, two_rows, _ = out_ref.shape
     rows = two_rows // 2
     sign = jnp.where(lax.broadcasted_iota(jnp.int32, (rows, LANES), 0) % 2 == 0, 1.0, -1.0)
@@ -457,7 +450,9 @@
         out_ref[:, pl.ds(index * bins, bins)] = result.T * scale
 
 
-def finish_channels(order, places, in_refs, g_ref, taps_ref, filtered_ref, padded, extra, results, leave):
+def finish_channels(
+    order, places, in_refs, g_ref, taps_ref, far_ref, near_ref, padded, extra, results, leave
+):
     me = lax.axis_index("context")
     rows = g_ref.shape[0]
     span = taps_ref.shape[1]
@@ -466,7 +461,9 @@
         lanes = pl.ds(pl.multiple_of((me ^ order[place]) * LANES, LANES), LANES)
         slot = index % padded.shape[0]
         edge_rows = in_ref.shape[0] - 2 * rows
-        query_f, key_f, value_f = [filtered_ref[which, place] for which in range(3)]
+        far_count = far_ref.shape[1]
+        held, spot = (far_ref, place) if place < far_count else (near_ref, place - far_count)
+        query_f, key_f, value_f = [held[which, spot] for which in range(3)]
         cotangent = g_ref[:, lanes].astype(jnp.float32)
         long_conv = in_ref[pl.ds(0, rows), :].astype(jnp.float32)
         back = in_ref[pl.ds(rows, rows), :].astype(jnp.float32)
@@ -490,7 +487,7 @@
             leave(index, which)
 
 
-def receive_kernel(order, places, g_ref, taps_ref, filtered_ref, filter_ref, *refs):
+def receive_kernel(order, places, g_ref, taps_ref, far_ref, near_ref, filter_ref, *refs):
     in_refs = refs[: len(places)]
     mixed_ref, grads_ref, filter_out, padded, extra, results, sems, filter_sem = refs[-8:]
     me = lax.axis_index("context")
@@ -506,42 +503,41 @@
         copies[-1].start()
 
     finish_channels(
-        order, places, in_refs, g_ref, taps_ref, filtered_ref, padded, extra, results, leave
+        order, places, in_refs, g_ref, taps_ref, far_ref, near_ref, padded, extra, results, leave
     )
     for copy in copies:
         copy.wait()
 
 
-def last_kernel(order, places, g_ref, taps_ref, filtered_ref, *refs):
+def last_kernel(order, places, g_ref, taps_ref, far_ref, near_ref, *refs):
     in_refs, refs = refs[: len(places)], refs[len(places) + 2 :]
     mixed_ref, grads_ref, padded, extra, results, sems = refs
     receive_kernel(
-        order, places, g_ref, taps_ref, filtered_ref, None, *in_refs,
+        order, places, g_ref, taps_ref, far_ref, near_ref, None, *in_refs,
         mixed_ref, grads_ref, None, padded, extra, results, sems, None,
     )
 
 
-def on_device(kernel, out_shape, scratch, args, in_hbm=0, pin=True, updated=0):
+def on_device(kernel, out_shape, scratch, args, in_hbm=(), unread=None, updates=()):
     whole = pl.BlockSpec(memory_space=pltpu.VMEM)
-    outside = pl.BlockSpec(memory_space=pltpu.HBM if pin else pl.ANY)
-    last = len(args) - updated
-    args = [
-        pltpu.with_memory_space_constraint(arg, pltpu.HBM) if pin and place < in_hbm else arg
-        for place, arg in enumerate(args)
-    ]
+    hbm = pl.BlockSpec(memory_space=pltpu.HBM)
+    anywhere = pl.BlockSpec(memory_space=pl.ANY)
+    fixed = [pltpu.with_memory_space_constraint(arg, pltpu.HBM) for arg in in_hbm]
+    before = [] if unread is None else [unread]
+    first_update = len(before) + len(fixed) + len(args)
     return pl.pallas_call(
-        kernel,
+        kernel if unread is None else lambda _, *refs: kernel(*refs),
         out_shape=out_shape,
-        in_specs=[outside if place < in_hbm or place >= last else whole for place in range(len(args))],
+        in_specs=[anywhere] * len(before) + [hbm] * len(fixed) + [whole] * len(args) + [hbm] * len(updates),
         out_specs=jax.tree.map(
-            lambda out: whole if isinstance(out, jax.ShapeDtypeStruct) else outside, out_shape
+            lambda out: whole if isinstance(out, jax.ShapeDtypeStruct) else hbm, out_shape
         ),
-        input_output_aliases={last + place: place for place in range(updated)},
+        input_output_aliases={first_update + place: place for place in range(len(updates))},
         scratch_shapes=[
             pltpu.VMEM(shape, jnp.float32) if isinstance(shape, tuple) else shape for shape in scratch
         ],
         compiler_params=pltpu.CompilerParams(vmem_limit_bytes=VMEM_BYTES),
-    )(*args)
+    )(*before, *fixed, *args, *updates)
 
 
 def exchange_order(count):
@@ -551,12 +547,9 @@
     )
 
 
-def exchange(order, parcels):
+def exchange(parcel, mask):
     count = lax.axis_size("context")
-    return [
-        parcel if mask == 0 else lax.ppermute(parcel, "context", [(i, i ^ mask) for i in range(count)])
-        for mask, parcel in zip(order, parcels)
-    ]
+    return lax.ppermute(parcel, "context", [(i, i ^ mask) for i in range(count)])
 
 
 def block_shards(query_proj, key_proj, value_proj, short_taps, long_filter, grad_mixed):
@@ -572,35 +565,42 @@
     parcels = [jax.ShapeDtypeStruct((2 * rows + edge_rows, LANES), jnp.bfloat16)] * blocks
     spectra = (blocks // merged, 2 * wide, LANES)
     own_taps = (*short_taps.shape[:2], LANES)
-    kept = (long_filter[0], forward_hi, forward_lo)
-
-    *sent, filtered, own, filter_here, hi_here, lo_here = on_device(
-        functools.partial(send_kernel, order),
-        parcels
-        + [
-            jax.ShapeDtypeStruct((3, blocks, rows, LANES), jnp.float32),
-            jax.ShapeDtypeStruct(own_taps, jnp.float32),
-        ]
-        + [jax.ShapeDtypeStruct(value.shape, value.dtype) for value in kept],
-        [
-            pltpu.VMEM((blocks, 4, rows, LANES), jnp.bfloat16),
-            (blocks, *own_taps),
-            (2, 3, rows + 8, LANES),
-            (2, edge_rows, LANES),
-            pltpu.SemaphoreType.DMA((blocks, 5)),
-            pltpu.SemaphoreType.DMA((len(kept),)),
-        ],
-        (query_proj, key_proj, value_proj, grad_mixed, short_taps, *kept),
-        in_hbm=8,
-    )
-    arrived = exchange(order, sent)
+    far = [place for place in range(blocks) if order[place] > 1]
+    near = [place for place in range(blocks) if order[place] <= 1]
+
+    def send(places, sources=(), unread=None):
+        return on_device(
+            functools.partial(send_kernel, order, places, len(sources)),
+            [parcels[place] for place in places]
+            + [
+                jax.ShapeDtypeStruct((3, len(places), rows, LANES), jnp.float32),
+            ]
+            + [jax.ShapeDtypeStruct(value.shape, value.dtype) for value in sources]
+            + [jax.ShapeDtypeStruct(own_taps, jnp.float32)] * (order[places[-1]] == 0),
+            [
+                pltpu.VMEM((len(places), 4, rows, LANES), jnp.bfloat16),
+                (len(places), *own_taps),
+                (2, 3, rows + 8, LANES),
+                (2, edge_rows, LANES),
+                pltpu.SemaphoreType.DMA((len(places), 5)),
+                pltpu.SemaphoreType.DMA((max(1, len(sources)),)),
+            ],
+            (),
+            in_hbm=(query_proj, key_proj, value_proj, grad_mixed, short_taps, *sources),
+            unread=unread,
+        )
+
+    *sent, far_filtered = send(far)
+    arrived = [exchange(parcel, order[place]) for place, parcel in zip(far, sent)]
+    *sent, near_filtered, filter_here, hi_here, lo_here, own = send(
+        near, (long_filter[0], forward_hi, forward_lo), arrived[0]
+    )
+    arrived += [exchange(sent[0], order[near[0]]), sent[1]]
     spec_h = on_device(
         filter_kernel,
         jax.ShapeDtypeStruct(spectra, jnp.float32),
         [],
-        (arrived[0], filter_here, hi_here, lo_here),
-        in_hbm=1,
-        pin=False,
+        (filter_here, hi_here, lo_here),
     )
     *results, spec_x, spec_g = on_device(
         functools.partial(convolve_kernel, order),
@@ -616,14 +616,14 @@
         ],
         (own, spec_h, hi_here, inverse, *arrived),
     )
-    returned = exchange(order, results)
+    returned = [exchange(parcel, mask) if mask else parcel for mask, parcel in zip(order, results)]
     filter_grad = on_device(
         functools.partial(correlate_kernel, 1.0 / math.sqrt(seq_len)),
         jax.ShapeDtypeStruct(long_filter.shape[1:], jnp.float32),
         [pltpu.VMEM(spectra, jnp.bfloat16)],
         (spec_x, spec_g, inverse),
     )
-    late = list(range(blocks // 2 - 1, blocks - 1))
+    late = far[len(far) // 2 :] + near[:-1]
     early = [place for place in range(blocks) if place not in late]
     outputs = (
         pltpu.HBM((rows, channels), jnp.bfloat16),
@@ -639,7 +639,7 @@
             pltpu.SemaphoreType.DMA((len(places), 4)),
         ]
 
-    common = (grad_mixed, short_taps, filtered)
+    common = (grad_mixed, short_taps, far_filtered, near_filtered)
     *begun, filter_grad = on_device(
         functools.partial(receive_kernel, order, early),
         outputs,
@@ -650,8 +650,8 @@
         functools.partial(last_kernel, order, late),
         outputs[:2],
         working(late),
-        (*common, *(returned[place] for place in late), *begun),
-        updated=2,
+        (*common, *(returned[place] for place in late)),
+        updates=begun,
     )
     return (mixed_out, input_grads, filter_grad)
 

time: 28.1 us -> 27.7 us (0.986)
  waiting for transfers between devices: 4.28 us -> 2.16 us
  Pallas kernels: 8.91 us -> 10 us
  starting transfers between devices: 14 us -> 14.5 us
    ppermute x14, waiting for transfers between devices: 4.28 us -> 2.16 us  [exchange(): lax.ppermute(parcel, 'context', [(i, i ^ mask) for i in range(count)])]
    pallas_call x6 -> x7, Pallas kernels: 8.91 us -> 10 us  [on_device(): pl.pallas_call(kernel if unread is None else lambda _, *refs: kernel(*ref...]
    ppermute x14, starting transfers between devices: 14 us -> 14.5 us  [exchange(): lax.ppermute(parcel, 'context', [(i, i ^ mask) for i in range(count)])]
  transfers between devices with their start and end apart: 14 -> 14, of which waited for: 6 -> 5; matrix products, arithmetic and copies ran while one was open for 0% -> 0% of each run, Pallas kernels for 12% -> 18%
where the time goes in v4:
time: 27.7 us; the launch traced here: 27.4 us
  starting transfers between devices  14.5 us (52%)
  Pallas kernels  10 us (36%)
  waiting for transfers between devices  2.16 us (8%)
  between operations  0.72 us (3%)
    ppermute x14, starting transfers between devices, exchange(): lax.ppermute(parcel, 'context', [(i, i ^ mask) for i in range(count)])  14.5 us
    pallas_call x7, Pallas kernels, on_device(): pl.pallas_call(kernel if unread is None else lambda _, *refs: kernel(*ref...  10 us
    ppermute x14, waiting for transfers between devices, exchange(): lax.ppermute(parcel, 'context', [(i, i ^ mask) for i in range(count)])  2.16 us
  transfers between devices with their start and end apart: 14, of which 5 were waited for; matrix products, arithmetic and copies ran while one was open for 0% of the time, Pallas kernels for 18%

profile of v4, /device:TPU:0, one launch (start us, length us, event | category | flops | bytes accessed | tf_op | source)
XLA Modules:
  0.0 27.4 jit_solution(2791208165568994632)
XLA Ops:
  0.6 1.9 %shard_map.112 = (bf16[288,128]{1,0:T(8,128)(2,1)S(1)}, bf16[288,128]{1,0:T(8,128)(2,1)S(1)}, bf16[288,128]{1,0:T(8,128)(2,1)S(1)}, bf16[288,128]{1,0:T(8,128)(2...) custom-call(bf16[128,1024]{1,0:T(8,128)(2,1)} %refs_0_.1, ...), custom_call_target="tpu_custom_call" | custom-call | tf_op jit(solution)/shard_map/pallas_call | solution.py:528
  2.5 4.0 %collective-permute-start = (bf16[288,128]{1,0:T(8,128)(2,1)S(1)}, bf16[288,128]{1,0:T(8,128)(2,1)S(1)}, u32[]{:S(2)}, u32[]{:S(2)}) collective-permute-start(bf16[288,128]{1,0:T(8,128)(2,1)S(1)} %get-tuple-element.33), channel_id=1, source_target_pairs={{0,24},{4,28},{8,16},{12,20},{16,8},{20,12},{24,0},{28,4},{1,25},{... | collective-permute-start | bytes 221192 | tf_op jit(solution)/shard_map/ppermute | solution.py:552
  6.5 0.0 collective-permute-start.1
  6.5 1.2 %collective-permute-start.2 = (bf16[288,128]{1,0:T(8,128)(2,1)S(1)}, bf16[288,128]{1,0:T(8,128)(2,1)S(1)}, u32[]{:S(2)}, u32[]{:S(2)}) collective-permute-start(bf16[288,128]{1,0:T(8,128)(2,1)S(1)} %get-tuple-element.40), channel_id=1, source_target_pairs={{0,16},{4,20},{8,24},{12,28},{16,0},{20,4},{24,8},{28,12},{1,17},{... | collective-permute-start | bytes 221192 | tf_op jit(solution)/shard_map/ppermute | solution.py:552
  7.6 1.5 %collective-permute-start.3 = (bf16[288,128]{1,0:T(8,128)(2,1)S(1)}, bf16[288,128]{1,0:T(8,128)(2,1)S(1)}, u32[]{:S(2)}, u32[]{:S(2)}) collective-permute-start(bf16[288,128]{1,0:T(8,128)(2,1)S(1)} %get-tuple-element.41), channel_id=1, source_target_pairs={{0,8},{4,12},{8,0},{12,4},{16,24},{20,28},{24,16},{28,20},{1,9},{5... | collective-permute-start | bytes 221192 | tf_op jit(solution)/shard_map/ppermute | solution.py:552
  9.1 0.6 %collective-permute-start.4 = (bf16[288,128]{1,0:T(8,128)(2,1)S(1)}, bf16[288,128]{1,0:T(8,128)(2,1)S(1)}, u32[]{:S(2)}, u32[]{:S(2)}) collective-permute-start(bf16[288,128]{1,0:T(8,128)(2,1)S(1)} %get-tuple-element.42), channel_id=1, source_target_pairs={{0,12},{4,8},{8,4},{12,0},{16,28},{20,24},{24,20},{28,16},{1,13},{... | collective-permute-start | bytes 221192 | tf_op jit(solution)/shard_map/ppermute | solution.py:552
  9.7 0.0 collective-permute-done._.refs_0_
  9.7 0.6 %collective-permute-start.5 = (bf16[288,128]{1,0:T(8,128)(2,1)S(1)}, bf16[288,128]{1,0:T(8,128)(2,1)S(1)}, u32[]{:S(2)}, u32[]{:S(2)}) collective-permute-start(bf16[288,128]{1,0:T(8,128)(2,1)S(1)} %get-tuple-element.43), channel_id=1, source_target_pairs={{0,20},{4,16},{8,28},{12,24},{16,4},{20,0},{24,12},{28,8},{1,21},{... | collective-permute-start | bytes 221192 | tf_op jit(solution)/shard_map/ppermute | solution.py:552
  10.3 1.5 %shard_map.113 = (bf16[288,128]{1,0:T(8,128)(2,1)S(1)}, bf16[288,128]{1,0:T(8,128)(2,1)S(1)}, f32[3,2,128,128]{3,2,1,0:T(8,128)S(1)}, f32[128,1024]{1,0:T(8,128)...) custom-call(bf16[288,128]{1,0:T(8,128)(2,1)S(1)} %collective-permute-done._.refs_0_, ...), custom_call_target="tpu_custom_call" | custom-call | tf_op jit(solution)/shard_map/pallas_call | solution.py:528
  11.7 0.0 copy-start.2
  11.7 0.2 collective-permute-done.1.refs_1_
  11.9 0.6 %collective-permute-start.6 = (bf16[288,128]{1,0:T(8,128)(2,1)S(1)}, bf16[288,128]{1,0:T(8,128)(2,1)S(1)}, u32[]{:S(2)}, u32[]{:S(2)}) collective-permute-start(bf16[288,128]{1,0:T(8,128)(2,1)S(1)} %get-tuple-element.44), channel_id=1, source_target_pairs={{0,4},{4,0},{8,12},{12,8},{16,20},{20,16},{24,28},{28,24},{1,5},{5... | collective-permute-start | bytes 221192 | tf_op jit(solution)/shard_map/ppermute | solution.py:552
  12.5 1.0 %shard_map.114.spec_h = f32[4,512,128]{2,1,0:T(8,128)S(1)} custom-call(f32[128,1024]{1,0:T(8,128)S(1)} %get-tuple-element.36.h_ref, bf16[512,256]{1,0:T(8,128)(2,1)S(1)} %get-tuple-element.37.forward_hi.forward, bf16[512,256]{1,0:T(8,128)(2,1)S(1)} %get-tuple-element.38.forward_lo), custom_call_target="tpu_custom_call" | custom-call | tf_op jit(solution)/shard_map/pallas_call | solution.py:528
  13.5 0.0 collective-permute-done.2.refs_2_
  13.5 0.0 collective-permute-done.3.refs_3_
  13.5 0.2 collective-permute-done.4.refs_4_
  13.7 0.3 collective-permute-done.5.refs_5_
  14.0 0.0 collective-permute-done.6.refs_6_
  14.0 0.0 copy-done.2
  14.0 2.0 %shard_map.115 = (bf16[288,128]{1,0:T(8,128)(2,1)S(1)}, bf16[288,128]{1,0:T(8,128)(2,1)S(1)}, bf16[288,128]{1,0:T(8,128)(2,1)S(1)}, bf16[288,128]{1,0:T(8,128)(2...) custom-call(f32[3,7,128]{2,1,0:T(8,128)S(1)} %get-tuple-element.35.t, ...), custom_call_target="tpu_custom_call" | custom-call | tf_op jit(solution)/shard_map/pallas_call | solution.py:528
  16.0 2.2 %collective-permute-start.11 = (bf16[288,128]{1,0:T(8,128)(2,1)S(1)}, bf16[288,128]{1,0:T(8,128)(2,1)S(1)}, u32[]{:S(2)}, u32[]{:S(2)}) collective-permute-start(bf16[288,128]{1,0:T(8,128)(2,1)S(1)} %get-tuple-element.52), channel_id=1, source_target_pairs={{0,24},{4,28},{8,16},{12,20},{16,8},{20,12},{24,0},{28,4},{1,25},{... | collective-permute-start | bytes 221192 | tf_op jit(solution)/shard_map/ppermute | solution.py:552
  18.2 0.3 collective-permute-start.12
  18.5 1.6 %collective-permute-start.7 = (bf16[288,128]{1,0:T(8,128)(2,1)S(1)}, bf16[288,128]{1,0:T(8,128)(2,1)S(1)}, u32[]{:S(2)}, u32[]{:S(2)}) collective-permute-start(bf16[288,128]{1,0:T(8,128)(2,1)S(1)} %get-tuple-element.46), channel_id=1, source_target_pairs={{0,8},{4,12},{8,0},{12,4},{16,24},{20,28},{24,16},{28,20},{1,9},{5... | collective-permute-start | bytes 221192 | tf_op jit(solution)/shard_map/ppermute | solution.py:552
  20.0 0.5 %collective-permute-start.13 = (bf16[288,128]{1,0:T(8,128)(2,1)S(1)}, bf16[288,128]{1,0:T(8,128)(2,1)S(1)}, u32[]{:S(2)}, u32[]{:S(2)}) collective-permute-start(bf16[288,128]{1,0:T(8,128)(2,1)S(1)} %get-tuple-element.54), channel_id=1, source_target_pairs={{0,16},{4,20},{8,24},{12,28},{16,0},{20,4},{24,8},{28,12},{1,17},{... | collective-permute-start | bytes 221192 | tf_op jit(solution)/shard_map/ppermute | solution.py:552
  20.5 1.2 %collective-permute-start.8 = (bf16[288,128]{1,0:T(8,128)(2,1)S(1)}, bf16[288,128]{1,0:T(8,128)(2,1)S(1)}, u32[]{:S(2)}, u32[]{:S(2)}) collective-permute-start(bf16[288,128]{1,0:T(8,128)(2,1)S(1)} %get-tuple-element.47), channel_id=1, source_target_pairs={{0,12},{4,8},{8,4},{12,0},{16,28},{20,24},{24,20},{28,16},{1,13},{... | collective-permute-start | bytes 221192 | tf_op jit(solution)/shard_map/ppermute | solution.py:552
  21.8 0.0 collective-permute-done.11.refs_0_
  21.8 0.5 %collective-permute-start.9 = (bf16[288,128]{1,0:T(8,128)(2,1)S(1)}, bf16[288,128]{1,0:T(8,128)(2,1)S(1)}, u32[]{:S(2)}, u32[]{:S(2)}) collective-permute-start(bf16[288,128]{1,0:T(8,128)(2,1)S(1)} %get-tuple-element.48), channel_id=1, source_target_pairs={{0,20},{4,16},{8,28},{12,24},{16,4},{20,0},{24,12},{28,8},{1,21},{... | collective-permute-start | bytes 221192 | tf_op jit(solution)/shard_map/ppermute | solution.py:552
  22.3 0.9 %collective-permute-done.12.refs_1_ = bf16[288,128]{1,0:T(8,128)(2,1)S(1)} collective-permute-done((bf16[288,128]{1,0:T(8,128)(2,1)S(1)}, bf16[288,128]{1,0:T(8,128)(2,1)S(1)}, u32[]{:S(2)}, u32[]{:S(2)}) %collective-permute-start.12) | collective-permute-done | bytes 73760 | tf_op jit(solution)/shard_map/ppermute | solution.py:552
  23.2 0.0 collective-permute-start.10
  23.2 0.0 copy-start
  23.2 0.0 copy-start.1
  23.2 1.0 %shard_map.116.filter_ref = f32[128,1024]{1,0:T(8,128)S(1)} custom-call(f32[4,512,128]{2,1,0:T(8,128)S(1)} %get-tuple-element.50.spec_x, f32[4,512,128]{2,1,0:T(8,128)S(1)} %get-tuple-element.51.spec_g, bf16[256,512]{1,0:T(8,128)(2,1)S(1)} %copy-done.2), custom_call_target="tpu_custom_call" | custom-call | tf_op jit(solution)/shard_map/pallas_call | solution.py:528
  24.2 0.5 %collective-permute-done.13.refs_2_ = bf16[288,128]{1,0:T(8,128)(2,1)S(1)} collective-permute-done((bf16[288,128]{1,0:T(8,128)(2,1)S(1)}, bf16[288,128]{1,0:T(8,128)(2,1)S(1)}, u32[]{:S(2)}, u32[]{:S(2)}) %collective-permute-start.13) | collective-permute-done | bytes 73760 | tf_op jit(solution)/shard_map/ppermute | solution.py:552
  24.7 0.0 copy-done
  24.7 0.0 copy-done.1
  24.7 1.4 %shard_map.117 = (bf16[128,1024]{1,0:T(8,128)(2,1)}, bf16[3,128,1024]{2,1,0:T(8,128)(2,1)}, f32[1,128,1024]{2,1,0:T(8,128)}) custom-call(bf16[128,1024]{1,0:T(8,128)(2,1)S(1)} %copy-done, f32[3,7,1024]{2,1,0:T(8,128)S(1)} %copy-done.1, f32[3,6,128,128]{3,2,1,0:T(8,128)S(1)} %get-tuple-element.32.far_ref, f32[3,2,128,128]{3,2,1,0:T(8,128)S(1)} %get-tuple-element.34.near_ref, ...), custom_call_target="tpu_custom_call" | custom-call | tf_op jit(solution)/shard_map/pallas_call | solution.py:528
  26.1 0.0 collective-permute-done.7.refs_0_
  26.1 0.0 collective-permute-done.8.refs_1_
  26.1 0.0 collective-permute-done.9.refs_2_
  26.1 0.0 collective-permute-done.10.refs_3_
  26.1 1.3 %shard_map.118 = (bf16[128,1024]{1,0:T(8,128)(2,1)}, bf16[3,128,1024]{2,1,0:T(8,128)(2,1)}) custom-call(bf16[128,1024]{1,0:T(8,128)(2,1)S(1)} %copy-done, f32[3,7,1024]{2,1,0:T(8,128)S(1)} %copy-done.1, f32[3,6,128,128]{3,2,1,0:T(8,128)S(1)} %get-tuple-element.32.far_ref, ...), custom_call_target="tpu_custom_call", output_to_operand_aliasing={{0}: (8, {}), {1}: (9, {})} | custom-call | tf_op jit(solution)/shard_map/pallas_call | solution.py:528
Async XLA Ops:
  2.5 7.2 %collective-permute-start = (bf16[288,128]{1,0:T(8,128)(2,1)S(1)}, bf16[288,128]{1,0:T(8,128)(2,1)S(1)}, u32[]{:S(2)}, u32[]{:S(2)}) collective-permute-start(bf16[288,128]{1,0:T(8,128)(2,1)S(1)} %get-tuple-element.33), channel_id=1, source_target_pairs={{0,24},{4,28},{8,16},{12,20},{16,8},{20,12},{24,0},{28,4},{1,25},{... | collective-permute-start | bytes 221192 | tf_op jit(solution)/shard_map/ppermute | solution.py:552
  6.5 5.5 %collective-permute-start.1 = (bf16[288,128]{1,0:T(8,128)(2,1)S(1)}, bf16[288,128]{1,0:T(8,128)(2,1)S(1)}, u32[]{:S(2)}, u32[]{:S(2)}) collective-permute-start(bf16[288,128]{1,0:T(8,128)(2,1)S(1)} %get-tuple-element.39), channel_id=1, source_target_pairs={{0,28},{4,24},{8,20},{12,16},{16,12},{20,8},{24,4},{28,0},{1,29},{... | collective-permute-start | bytes 221192 | tf_op jit(solution)/shard_map/ppermute | solution.py:552
  6.5 7.0 %collective-permute-start.2 = (bf16[288,128]{1,0:T(8,128)(2,1)S(1)}, bf16[288,128]{1,0:T(8,128)(2,1)S(1)}, u32[]{:S(2)}, u32[]{:S(2)}) collective-permute-start(bf16[288,128]{1,0:T(8,128)(2,1)S(1)} %get-tuple-element.40), channel_id=1, source_target_pairs={{0,16},{4,20},{8,24},{12,28},{16,0},{20,4},{24,8},{28,12},{1,17},{... | collective-permute-start | bytes 221192 | tf_op jit(solution)/shard_map/ppermute | solution.py:552
  7.6 5.9 %collective-permute-start.3 = (bf16[288,128]{1,0:T(8,128)(2,1)S(1)}, bf16[288,128]{1,0:T(8,128)(2,1)S(1)}, u32[]{:S(2)}, u32[]{:S(2)}) collective-permute-start(bf16[288,128]{1,0:T(8,128)(2,1)S(1)} %get-tuple-element.41), channel_id=1, source_target_pairs={{0,8},{4,12},{8,0},{12,4},{16,24},{20,28},{24,16},{28,20},{1,9},{5... | collective-permute-start | bytes 221192 | tf_op jit(solution)/shard_map/ppermute | solution.py:552
  9.1 4.6 %collective-permute-start.4 = (bf16[288,128]{1,0:T(8,128)(2,1)S(1)}, bf16[288,128]{1,0:T(8,128)(2,1)S(1)}, u32[]{:S(2)}, u32[]{:S(2)}) collective-permute-start(bf16[288,128]{1,0:T(8,128)(2,1)S(1)} %get-tuple-element.42), channel_id=1, source_target_pairs={{0,12},{4,8},{8,4},{12,0},{16,28},{20,24},{24,20},{28,16},{1,13},{... | collective-permute-start | bytes 221192 | tf_op jit(solution)/shard_map/ppermute | solution.py:552
  9.7 4.3 %collective-permute-start.5 = (bf16[288,128]{1,0:T(8,128)(2,1)S(1)}, bf16[288,128]{1,0:T(8,128)(2,1)S(1)}, u32[]{:S(2)}, u32[]{:S(2)}) collective-permute-start(bf16[288,128]{1,0:T(8,128)(2,1)S(1)} %get-tuple-element.43), channel_id=1, source_target_pairs={{0,20},{4,16},{8,28},{12,24},{16,4},{20,0},{24,12},{28,8},{1,21},{... | collective-permute-start | bytes 221192 | tf_op jit(solution)/shard_map/ppermute | solution.py:552
  11.7 2.3 %copy-start.2 = (bf16[256,512]{1,0:T(8,128)(2,1)S(1)}, bf16[256,512]{1,0:T(8,128)(2,1)}, u32[]{:S(2)}) copy-start(bf16[256,512]{1,0:T(8,128)(2,1)} %constant.8.clone.inverse) | copy-start | bytes 786436
  11.9 2.1 %collective-permute-start.6 = (bf16[288,128]{1,0:T(8,128)(2,1)S(1)}, bf16[288,128]{1,0:T(8,128)(2,1)S(1)}, u32[]{:S(2)}, u32[]{:S(2)}) collective-permute-start(bf16[288,128]{1,0:T(8,128)(2,1)S(1)} %get-tuple-element.44), channel_id=1, source_target_pairs={{0,4},{4,0},{8,12},{12,8},{16,20},{20,16},{24,28},{28,24},{1,5},{5... | collective-permute-start | bytes 221192 | tf_op jit(solution)/shard_map/ppermute | solution.py:552
  16.0 5.7 %collective-permute-start.11 = (bf16[288,128]{1,0:T(8,128)(2,1)S(1)}, bf16[288,128]{1,0:T(8,128)(2,1)S(1)}, u32[]{:S(2)}, u32[]{:S(2)}) collective-permute-start(bf16[288,128]{1,0:T(8,128)(2,1)S(1)} %get-tuple-element.52), channel_id=1, source_target_pairs={{0,24},{4,28},{8,16},{12,20},{16,8},{20,12},{24,0},{28,4},{1,25},{... | collective-permute-start | bytes 221192 | tf_op jit(solution)/shard_map/ppermute | solution.py:552
  18.2 5.0 %collective-permute-start.12 = (bf16[288,128]{1,0:T(8,128)(2,1)S(1)}, bf16[288,128]{1,0:T(8,128)(2,1)S(1)}, u32[]{:S(2)}, u32[]{:S(2)}) collective-permute-start(bf16[288,128]{1,0:T(8,128)(2,1)S(1)} %get-tuple-element.53), channel_id=1, source_target_pairs={{0,28},{4,24},{8,20},{12,16},{16,12},{20,8},{24,4},{28,0},{1,29},{... | collective-permute-start | bytes 221192 | tf_op jit(solution)/shard_map/ppermute | solution.py:552
  18.5 7.6 %collective-permute-start.7 = (bf16[288,128]{1,0:T(8,128)(2,1)S(1)}, bf16[288,128]{1,0:T(8,128)(2,1)S(1)}, u32[]{:S(2)}, u32[]{:S(2)}) collective-permute-start(bf16[288,128]{1,0:T(8,128)(2,1)S(1)} %get-tuple-element.46), channel_id=1, source_target_pairs={{0,8},{4,12},{8,0},{12,4},{16,24},{20,28},{24,16},{28,20},{1,9},{5... | collective-permute-start | bytes 221192 | tf_op jit(solution)/shard_map/ppermute | solution.py:552
  20.0 4.6 %collective-permute-start.13 = (bf16[288,128]{1,0:T(8,128)(2,1)S(1)}, bf16[288,128]{1,0:T(8,128)(2,1)S(1)}, u32[]{:S(2)}, u32[]{:S(2)}) collective-permute-start(bf16[288,128]{1,0:T(8,128)(2,1)S(1)} %get-tuple-element.54), channel_id=1, source_target_pairs={{0,16},{4,20},{8,24},{12,28},{16,0},{20,4},{24,8},{28,12},{1,17},{... | collective-permute-start | bytes 221192 | tf_op jit(solution)/shard_map/ppermute | solution.py:552
  20.5 5.6 %collective-permute-start.8 = (bf16[288,128]{1,0:T(8,128)(2,1)S(1)}, bf16[288,128]{1,0:T(8,128)(2,1)S(1)}, u32[]{:S(2)}, u32[]{:S(2)}) collective-permute-start(bf16[288,128]{1,0:T(8,128)(2,1)S(1)} %get-tuple-element.47), channel_id=1, source_target_pairs={{0,12},{4,8},{8,4},{12,0},{16,28},{20,24},{24,20},{28,16},{1,13},{... | collective-permute-start | bytes 221192 | tf_op jit(solution)/shard_map/ppermute | solution.py:552
  21.8 4.3 %collective-permute-start.9 = (bf16[288,128]{1,0:T(8,128)(2,1)S(1)}, bf16[288,128]{1,0:T(8,128)(2,1)S(1)}, u32[]{:S(2)}, u32[]{:S(2)}) collective-permute-start(bf16[288,128]{1,0:T(8,128)(2,1)S(1)} %get-tuple-element.48), channel_id=1, source_target_pairs={{0,20},{4,16},{8,28},{12,24},{16,4},{20,0},{24,12},{28,8},{1,21},{... | collective-permute-start | bytes 221192 | tf_op jit(solution)/shard_map/ppermute | solution.py:552
  23.2 2.9 %collective-permute-start.10 = (bf16[288,128]{1,0:T(8,128)(2,1)S(1)}, bf16[288,128]{1,0:T(8,128)(2,1)S(1)}, u32[]{:S(2)}, u32[]{:S(2)}) collective-permute-start(bf16[288,128]{1,0:T(8,128)(2,1)S(1)} %get-tuple-element.49), channel_id=1, source_target_pairs={{0,4},{4,0},{8,12},{12,8},{16,20},{20,16},{24,28},{28,24},{1,5},{5... | collective-permute-start | bytes 221192 | tf_op jit(solution)/shard_map/ppermute | solution.py:552
  23.2 1.5 %copy-start = (bf16[128,1024]{1,0:T(8,128)(2,1)S(1)}, bf16[128,1024]{1,0:T(8,128)(2,1)}, u32[]{:S(2)}) copy-start(bf16[128,1024]{1,0:T(8,128)(2,1)} %g_ref.5) | copy-start | bytes 786436
  23.2 1.5 %copy-start.1 = (f32[3,7,1024]{2,1,0:T(8,128)S(1)}, f32[3,7,1024]{2,1,0:T(8,128)}, u32[]{:S(2)}) copy-start(f32[3,7,1024]{2,1,0:T(8,128)} %taps_ref.5) | copy-start | bytes 258052

commit v5 on v4

--- a/solution.py
+++ b/solution.py
@@ -163,6 +163,7 @@
 
 LANES = 128
 VMEM_BYTES = 48 * 1024 * 1024
+COVER = pl.CostEstimate(flops=10**10, bytes_accessed=10**8, transcendentals=0)
 
 
 def split_bf16(table):
@@ -200,67 +201,86 @@
     return running
 
 
-def send_kernel(order, places, extras, q_ref, k_ref, v_ref, g_ref, taps_ref, *refs):
+def make_parcel(slot, source, taps, padded, extra, filtered_ref, out_ref):
+    rows = source.shape[1]
+    halo = taps.shape[1] - 1
+    padded[slot, :, pl.ds(0, 8), :] = jnp.zeros((3, 8, LANES), jnp.float32)
+    extra[slot, pl.ds(5 * halo, extra.shape[1] - 5 * halo), :] = jnp.zeros(
+        (extra.shape[1] - 5 * halo, LANES), jnp.float32
+    )
+    filtered = []
+    for which in range(3):
+        padded[slot, which, pl.ds(8, rows), :] = source[which].astype(jnp.float32)
+        weights = tap_rows(taps, which, pl.ds(0, LANES))
+        result = short_filter(padded.at[slot, which], rows, weights)
+        filtered_ref[which] = result
+        filtered.append(result)
+    query_f, key_f, value_f = filtered
+    cotangent = source[3].astype(jnp.float32)
+    gated = head_rows(padded[slot, 1, pl.ds(8, 8), :], key_f * value_f, halo)
+    grad_long = head_rows(cotangent[:8], cotangent * query_f, halo)
+    out_ref[pl.ds(0, rows), :] = gated.astype(jnp.bfloat16)
+    out_ref[pl.ds(rows, rows), :] = grad_long.astype(jnp.bfloat16)
+    pieces = ((1, rows - halo), (2, 0), (2, rows - halo), (0, 0), (0, rows - halo))
+    for position, (which, first) in enumerate(pieces):
+        extra[slot, pl.ds(position * halo, halo), :] = padded[slot, which, pl.ds(8 + first, halo), :]
+    out_ref[pl.ds(2 * rows, extra.shape[1]), :] = extra[slot].astype(jnp.bfloat16)
+
+
+def fetches(order, places, inputs, taps_ref, landed, taps, arrivals):
+    me = lax.axis_index("context")
+    result = []
+    for index, place in enumerate(places):
+        lanes = pl.ds(pl.multiple_of((me ^ order[place]) * LANES, LANES), LANES)
+        sources = [taps_ref.at[:, :, lanes]] + [ref.at[:, lanes] for ref in inputs]
+        targets = [taps.at[index]] + [landed.at[index, which] for which in range(len(inputs))]
+        result.append(
+            [
+                pltpu.make_async_copy(source, target, arrivals.at[index, number])
+                for number, (source, target) in enumerate(zip(sources, targets))
+            ]
+        )
+    return result
+
+
+def send_kernel(order, places, ahead, extras, q_ref, k_ref, v_ref, g_ref, taps_ref, *refs):
+    inputs = (q_ref, k_ref, v_ref, g_ref)
     sources, refs = refs[:extras], refs[extras:]
-    outs, refs = refs[: len(places)], refs[len(places) :]
-    landed, taps, padded, extra, arrivals, kept = refs[-6:]
-    filtered_ref, *brought = refs[:-6]
-    me = lax.axis_index("context")
-    rows = q_ref.shape[0]
-    halo = taps_ref.shape[1] - 1
-
-    def fetches(index):
-        lanes = pl.ds(pl.multiple_of((me ^ order[places[index]]) * LANES, LANES), LANES)
-        copies = [
-            pltpu.make_async_copy(taps_ref.at[:, :, lanes], taps.at[index], arrivals.at[index, 4])
-        ]
-        for which, ref in enumerate((q_ref, k_ref, v_ref, g_ref)):
-            copies.append(
-                pltpu.make_async_copy(
-                    ref.at[:, lanes], landed.at[index, which], arrivals.at[index, which]
-                )
-            )
-        return copies
-
-    keeps = [
+    first_ref, *outs = refs[: len(places) - 1]
+    size = first_ref.shape[0] // 2
+    outs = [first_ref.at[pl.ds(0, size)], first_ref.at[pl.ds(size, size)], *outs]
+    filtered_ref, *brought = refs[len(places) - 1 : -7]
+    landed, taps, padded, extra, arrivals, later, kept = refs[-7:]
+    own = fetches(order, places, inputs, taps_ref, landed, taps, arrivals)
+    others = [
         pltpu.make_async_copy(source, target, kept.at[index])
         for index, (source, target) in enumerate(zip(sources, brought))
     ]
-    for index in range(len(places)):
-        for copy in fetches(index):
+    for copies in fetches(order, ahead, inputs, taps_ref, *brought[-2:], later):
+        others += copies
+    for copies in own:
+        for copy in copies:
             copy.start()
-    for copy in keeps:
+    for copy in others:
         copy.start()
-    for index in range(len(places)):
-        slot = index % padded.shape[0]
-        out_ref = outs[index]
-        padded[slot, :, pl.ds(0, 8), :] = jnp.zeros((3, 8, LANES), jnp.float32)
-        extra[slot, pl.ds(5 * halo, extra.shape[1] - 5 * halo), :] = jnp.zeros(
-            (extra.shape[1] - 5 * halo, LANES), jnp.float32
+    for index, copies in enumerate(own):
+        for copy in copies:
+            copy.wait()
+        make_parcel(
+            index % 2, landed.at[index], taps.at[index], padded, extra, filtered_ref.at[index], outs[index]
         )
-        for copy in fetches(index):
-            copy.wait()
-        filtered = []
-        for which in range(3):
-            padded[slot, which, pl.ds(8, rows), :] = landed[index, which].astype(jnp.float32)
-            weights = tap_rows(taps.at[index], which, pl.ds(0, LANES))
-            result = short_filter(padded.at[slot, which], rows, weights)
-            filtered_ref[which, index] = result
-            filtered.append(result)
-        query_f, key_f, value_f = filtered
-        cotangent = landed[index, 3].astype(jnp.float32)
-        gated = head_rows(padded[slot, 1, pl.ds(8, 8), :], key_f * value_f, halo)
-        grad_long = head_rows(cotangent[:8], cotangent * query_f, halo)
-        out_ref[pl.ds(0, rows), :] = gated.astype(jnp.bfloat16)
-        out_ref[pl.ds(rows, rows), :] = grad_long.astype(jnp.bfloat16)
-        pieces = ((1, rows - halo), (2, 0), (2, rows - halo), (0, 0), (0, rows - halo))
-        for position, (which, first) in enumerate(pieces):
-            extra[slot, pl.ds(position * halo, halo), :] = padded[slot, which, pl.ds(8 + first, halo), :]
-        out_ref[pl.ds(2 * rows, extra.shape[1]), :] = extra[slot].astype(jnp.bfloat16)
-    if order[places[-1]] == 0:
-        brought[-1][...] = taps[len(places) - 1]
-    for copy in keeps:
+    for copy in others:
         copy.wait()
+
+
+def near_kernel(landed, taps, first_ref, shared_ref, own_ref, filtered_ref, own_taps, padded, extra):
+    rows = own_ref.shape[0]
+    shared_ref[pl.ds(rows, rows), :] = first_ref[pl.ds(rows, rows), :]
+    for index, out_ref in enumerate((shared_ref.at[pl.ds(0, rows)], own_ref)):
+        make_parcel(
+            index, landed.at[index], taps.at[index], padded, extra, filtered_ref.at[index], out_ref
+        )
+    own_taps[...] = taps[1]
 
 
 def gather(order, in_refs, edges, firsts, pairs, rows):
@@ -376,8 +396,12 @@
 
 def convolve_kernel(order, taps_ref, spec_h, forward, inverse, *refs):
     count = len(order)
-    in_refs, out_refs = refs[:count], refs[count : 2 * count]
-    spec_x, spec_g, edges, firsts, joined, heads, pairs, spec_y, extra = refs[2 * count :]
+    first_ref, *others, shared_ref, own_ref = refs[: count - 1]
+    size = own_ref.shape[0]
+    in_refs = [first_ref.at[pl.ds(0, size)], shared_ref.at[pl.ds(size, size)], *others]
+    in_refs += [shared_ref.at[pl.ds(0, size)], own_ref]
+    out_refs, refs = refs[count - 1 : 2 * count - 1], refs[2 * count - 1 :]
+    spec_x, spec_g, edges, firsts, joined, heads, pairs, spec_y, extra = refs
     me = lax.axis_index("context")
     rows = pairs.shape[1]
     halo = taps_ref.shape[1] - 1
@@ -399,7 +423,7 @@
         store_tiles(spec_y, LANES, backs, pair, bins)
         return carry
 
-    lax.fori_loop(0, bins // 16, body, 0)
+    lax.fori_loop(0, bins // 16, body, 0, unroll=2)
     extra[...] = jnp.zeros(extra.shape, jnp.float32)
     for index in range(wide):
         both = jnp.dot(inverse[...], spec_y[index], preferred_element_type=jnp.float32).astype(jnp.bfloat16)
@@ -426,7 +450,8 @@
         out_ref[pl.ds(2 * rows, extra.shape[1]), :] = extra[block + 1].astype(jnp.bfloat16)
 
 
-def correlate_kernel(scale, spec_x, spec_g, inverse, out_ref, spec_y):
+def correlate_kernel(scale, spec_x, spec_g, inverse, parcel_ref, out_ref, parcel_out, spec_y):
+    parcel_out[...] = parcel_ref[...]
     wide = spec_x.shape[0]
     bins = inverse.shape[0]
 
@@ -444,26 +469,25 @@
         store_tiles(spec_y, 0, tiles, pair, bins)
         return carry
 
-    lax.fori_loop(0, bins // 16, body, 0)
+    lax.fori_loop(0, bins // 16, body, 0, unroll=2)
     for index in range(wide):
         result = jnp.dot(inverse[...], spec_y[index], preferred_element_type=jnp.float32)
         out_ref[:, pl.ds(index * bins, bins)] = result.T * scale
 
 
 def finish_channels(
-    order, places, in_refs, g_ref, taps_ref, far_ref, near_ref, padded, extra, results, leave
+    order, places, in_refs, g_ref, taps_ref, held, padded, extra, results, leave
 ):
     me = lax.axis_index("context")
     rows = g_ref.shape[0]
     span = taps_ref.shape[1]
     halo = span - 1
+    held = [ref.at[index] for ref in held for index in range(ref.shape[0])]
     for index, (place, in_ref) in enumerate(zip(places, in_refs)):
         lanes = pl.ds(pl.multiple_of((me ^ order[place]) * LANES, LANES), LANES)
         slot = index % padded.shape[0]
         edge_rows = in_ref.shape[0] - 2 * rows
-        far_count = far_ref.shape[1]
-        held, spot = (far_ref, place) if place < far_count else (near_ref, place - far_count)
-        query_f, key_f, value_f = [held[which, spot] for which in range(3)]
+        query_f, key_f, value_f = [held[place][which] for which in range(3)]
         cotangent = g_ref[:, lanes].astype(jnp.float32)
         long_conv = in_ref[pl.ds(0, rows), :].astype(jnp.float32)
         back = in_ref[pl.ds(rows, rows), :].astype(jnp.float32)
@@ -502,8 +526,9 @@
         copies.append(pltpu.make_async_copy(results.at[index, which], target, sems.at[index, which]))
         copies[-1].start()
 
+    held = (far_ref, near_ref)
     finish_channels(
-        order, places, in_refs, g_ref, taps_ref, far_ref, near_ref, padded, extra, results, leave
+        order, places, in_refs, g_ref, taps_ref, held, padded, extra, results, leave
     )
     for copy in copies:
         copy.wait()
@@ -518,7 +543,7 @@
     )
 
 
-def on_device(kernel, out_shape, scratch, args, in_hbm=(), unread=None, updates=()):
+def on_device(kernel, out_shape, scratch, args, in_hbm=(), unread=None, updates=(), cover=False):
     whole = pl.BlockSpec(memory_space=pltpu.VMEM)
     hbm = pl.BlockSpec(memory_space=pltpu.HBM)
     anywhere = pl.BlockSpec(memory_space=pl.ANY)
@@ -537,6 +562,7 @@
             pltpu.VMEM(shape, jnp.float32) if isinstance(shape, tuple) else shape for shape in scratch
         ],
         compiler_params=pltpu.CompilerParams(vmem_limit_bytes=VMEM_BYTES),
+        cost_estimate=COVER if cover else None,
     )(*before, *fixed, *args, *updates)
 
 
@@ -568,39 +594,50 @@
     far = [place for place in range(blocks) if order[place] > 1]
     near = [place for place in range(blocks) if order[place] <= 1]
 
-    def send(places, sources=(), unread=None):
-        return on_device(
-            functools.partial(send_kernel, order, places, len(sources)),
-            [parcels[place] for place in places]
-            + [
-                jax.ShapeDtypeStruct((3, len(places), rows, LANES), jnp.float32),
-            ]
-            + [jax.ShapeDtypeStruct(value.shape, value.dtype) for value in sources]
-            + [jax.ShapeDtypeStruct(own_taps, jnp.float32)] * (order[places[-1]] == 0),
-            [
-                pltpu.VMEM((len(places), 4, rows, LANES), jnp.bfloat16),
-                (len(places), *own_taps),
-                (2, 3, rows + 8, LANES),
-                (2, edge_rows, LANES),
-                pltpu.SemaphoreType.DMA((len(places), 5)),
-                pltpu.SemaphoreType.DMA((max(1, len(sources)),)),
-            ],
-            (),
-            in_hbm=(query_proj, key_proj, value_proj, grad_mixed, short_taps, *sources),
-            unread=unread,
-        )
-
-    *sent, far_filtered = send(far)
-    arrived = [exchange(parcel, order[place]) for place, parcel in zip(far, sent)]
-    *sent, near_filtered, filter_here, hi_here, lo_here, own = send(
-        near, (long_filter[0], forward_hi, forward_lo), arrived[0]
-    )
-    arrived += [exchange(sent[0], order[near[0]]), sent[1]]
+    parcel = parcels[0]
+    double = jax.ShapeDtypeStruct((2 * parcel.shape[0], LANES), jnp.bfloat16)
+    made = [(2, 3, rows + 8, LANES), (2, edge_rows, LANES)]
+    inputs = (4, rows, LANES)
+    sources = (long_filter[0], forward_hi, forward_lo)
+
+    def floats(*shape):
+        return jax.ShapeDtypeStruct(shape, jnp.float32)
+
+    first, *sent, far_filtered, filter_here, hi_here, lo_here, landed, taps = on_device(
+        functools.partial(send_kernel, order, far, near, len(sources)),
+        [double, *parcels[: len(far) - 2], floats(len(far), 3, rows, LANES)]
+        + [jax.ShapeDtypeStruct(value.shape, value.dtype) for value in sources]
+        + [
+            jax.ShapeDtypeStruct((len(near), *inputs), jnp.bfloat16),
+            floats(len(near), *own_taps),
+        ],
+        [
+            pltpu.VMEM((len(far), *inputs), jnp.bfloat16),
+            (len(far), *own_taps),
+            *made,
+            pltpu.SemaphoreType.DMA((len(far), 5)),
+            pltpu.SemaphoreType.DMA((len(near), 5)),
+            pltpu.SemaphoreType.DMA((len(sources),)),
+        ],
+        (),
+        in_hbm=(query_proj, key_proj, value_proj, grad_mixed, short_taps, *sources),
+    )
+    first = exchange(first, order[0])
+    others = [exchange(value, order[place]) for place, value in zip(far[2:], sent)]
+    shared, kept_here, near_filtered, own = on_device(
+        near_kernel,
+        [double, parcel, floats(len(near), 3, rows, LANES), floats(*own_taps)],
+        made,
+        (landed, taps, first),
+        cover=True,
+    )
+    arrived = (first, *others, exchange(shared, 1), kept_here)
     spec_h = on_device(
         filter_kernel,
         jax.ShapeDtypeStruct(spectra, jnp.float32),
         [],
         (filter_here, hi_here, lo_here),
+        cover=True,
     )
     *results, spec_x, spec_g = on_device(
         functools.partial(convolve_kernel, order),
@@ -616,14 +653,16 @@
         ],
         (own, spec_h, hi_here, inverse, *arrived),
     )
-    returned = [exchange(parcel, mask) if mask else parcel for mask, parcel in zip(order, results)]
-    filter_grad = on_device(
+    returned = [exchange(results[place], order[place]) for place in far]
+    filter_grad, parcel = on_device(
         functools.partial(correlate_kernel, 1.0 / math.sqrt(seq_len)),
-        jax.ShapeDtypeStruct(long_filter.shape[1:], jnp.float32),
+        [jax.ShapeDtypeStruct(long_filter.shape[1:], jnp.float32), parcels[0]],
         [pltpu.VMEM(spectra, jnp.bfloat16)],
-        (spec_x, spec_g, inverse),
-    )
-    late = far[len(far) // 2 :] + near[:-1]
+        (spec_x, spec_g, inverse, results[near[0]]),
+        unread=returned[0],
+    )
+    returned += [exchange(parcel, order[near[0]]), results[near[1]]]
+    late = far[len(far) // 2 - 1 :] + near[:-1]
     early = [place for place in range(blocks) if place not in late]
     outputs = (
         pltpu.HBM((rows, channels), jnp.bfloat16),

time: 27.7 us -> 27.2 us (0.982)
  Pallas kernels: 10 us -> 8.85 us
  waiting for transfers between devices: 2.16 us -> 2.93 us
    pallas_call x7, Pallas kernels: 10 us -> 8.85 us  [on_device(): pl.pallas_call(kernel if unread is None else lambda _, *refs: kernel(*ref...]
    ppermute x14 -> x13, waiting for transfers between devices: 2.16 us -> 2.93 us  [exchange(): lax.ppermute(parcel, 'context', [(i, i ^ mask) for i in range(count)])]
    ppermute x14 -> x13, starting transfers between devices: 14.5 us -> 14.5 us  [exchange(): lax.ppermute(parcel, 'context', [(i, i ^ mask) for i in range(count)])]
  transfers between devices with their start and end apart: 14 -> 13, of which waited for: 5 -> 4; matrix products, arithmetic and copies ran while one was open for 0% -> 0% of each run, Pallas kernels for 18% -> 12%
where the time goes in v5:
time: 27.2 us; the launch traced here: 27.1 us
  starting transfers between devices  14.5 us (53%)
  Pallas kernels  8.85 us (33%)
  waiting for transfers between devices  2.93 us (11%)
  between operations  0.73 us (3%)
    ppermute x13, starting transfers between devices, exchange(): lax.ppermute(parcel, 'context', [(i, i ^ mask) for i in range(count)])  14.5 us
    pallas_call x7, Pallas kernels, on_device(): pl.pallas_call(kernel if unread is None else lambda _, *refs: kernel(*ref...  8.85 us
    ppermute x13, waiting for transfers between devices, exchange(): lax.ppermute(parcel, 'context', [(i, i ^ mask) for i in range(count)])  2.93 us
  transfers between devices with their start and end apart: 13, of which 4 were waited for; matrix products, arithmetic and copies ran while one was open for 0% of the time, Pallas kernels for 12%

profile of v5, /device:TPU:0, one launch (start us, length us, event | category | flops | bytes accessed | tf_op | source)
XLA Modules:
  0.0 27.1 jit_solution(18365071124789057241)
XLA Ops:
  0.6 2.0 %shard_map.112 = (bf16[576,128]{1,0:T(8,128)(2,1)S(1)}, bf16[288,128]{1,0:T(8,128)(2,1)S(1)}, bf16[288,128]{1,0:T(8,128)(2,1)S(1)}, bf16[288,128]{1,0:T(8,128)(2...) custom-call(bf16[128,1024]{1,0:T(8,128)(2,1)} %q_ref.1, ...), custom_call_target="tpu_custom_call" | custom-call | tf_op jit(solution)/shard_map/pallas_call | solution.py:553
  2.7 4.0 %collective-permute-start = (bf16[576,128]{1,0:T(8,128)(2,1)S(1)}, bf16[576,128]{1,0:T(8,128)(2,1)S(1)}, u32[]{:S(2)}, u32[]{:S(2)}) collective-permute-start(bf16[576,128]{1,0:T(8,128)(2,1)S(1)} %get-tuple-element.38), channel_id=1, source_target_pairs={{0,24},{4,28},{8,16},{12,20},{16,8},{20,12},{24,0},{28,4},{1,25},{... | collective-permute-start | bytes 442376 | tf_op jit(solution)/shard_map/ppermute | solution.py:578
  6.6 0.5 %collective-permute-start.1 = (bf16[288,128]{1,0:T(8,128)(2,1)S(1)}, bf16[288,128]{1,0:T(8,128)(2,1)S(1)}, u32[]{:S(2)}, u32[]{:S(2)}) collective-permute-start(bf16[288,128]{1,0:T(8,128)(2,1)S(1)} %get-tuple-element.44), channel_id=1, source_target_pairs={{0,16},{4,20},{8,24},{12,28},{16,0},{20,4},{24,8},{28,12},{1,17},{... | collective-permute-start | bytes 221192 | tf_op jit(solution)/shard_map/ppermute | solution.py:578
  7.1 0.1 collective-permute-start.2
  7.3 0.5 %collective-permute-start.3 = (bf16[288,128]{1,0:T(8,128)(2,1)S(1)}, bf16[288,128]{1,0:T(8,128)(2,1)S(1)}, u32[]{:S(2)}, u32[]{:S(2)}) collective-permute-start(bf16[288,128]{1,0:T(8,128)(2,1)S(1)} %get-tuple-element.46), channel_id=1, source_target_pairs={{0,12},{4,8},{8,4},{12,0},{16,28},{20,24},{24,20},{28,16},{1,13},{... | collective-permute-start | bytes 221192 | tf_op jit(solution)/shard_map/ppermute | solution.py:578
  7.8 2.6 %collective-permute-start.4 = (bf16[288,128]{1,0:T(8,128)(2,1)S(1)}, bf16[288,128]{1,0:T(8,128)(2,1)S(1)}, u32[]{:S(2)}, u32[]{:S(2)}) collective-permute-start(bf16[288,128]{1,0:T(8,128)(2,1)S(1)} %get-tuple-element.47), channel_id=1, source_target_pairs={{0,20},{4,16},{8,28},{12,24},{16,4},{20,0},{24,12},{28,8},{1,21},{... | collective-permute-start | bytes 221192 | tf_op jit(solution)/shard_map/ppermute | solution.py:578
  10.4 0.5 %collective-permute-done.first_ref.refs_0_ = bf16[576,128]{1,0:T(8,128)(2,1)S(1)} collective-permute-done((bf16[576,128]{1,0:T(8,128)(2,1)S(1)}, bf16[576,128]{1,0:T(8,128)(2,1)S(1)}, u32[]{:S(2)}, u32[]{:S(2)}) %collective-permute-start) | collective-permute-done | bytes 147488 | tf_op jit(solution)/shard_map/ppermute | solution.py:578
  10.9 0.2 shard_map.113
  11.2 0.1 collective-permute-start.5
  11.3 0.0 copy-start.1
  11.3 1.0 %shard_map.114.spec_h = f32[4,512,128]{2,1,0:T(8,128)S(1)} custom-call(f32[128,1024]{1,0:T(8,128)S(1)} %get-tuple-element.41.h_ref, bf16[512,256]{1,0:T(8,128)(2,1)S(1)} %get-tuple-element.42.forward_hi.forward, bf16[512,256]{1,0:T(8,128)(2,1)S(1)} %get-tuple-element.43.forward_lo), custom_call_target="tpu_custom_call" | custom-call | flops 10000000000 | bytes 100000000 | tf_op jit(solution)/shard_map/pallas_call | solution.py:553
  12.3 0.0 collective-permute-done.1.refs_1_
  12.3 0.9 %collective-permute-done.2.refs_2_ = bf16[288,128]{1,0:T(8,128)(2,1)S(1)} collective-permute-done((bf16[288,128]{1,0:T(8,128)(2,1)S(1)}, bf16[288,128]{1,0:T(8,128)(2,1)S(1)}, u32[]{:S(2)}, u32[]{:S(2)}) %collective-permute-start.2) | collective-permute-done | bytes 73760 | tf_op jit(solution)/shard_map/ppermute | solution.py:578
  13.1 0.0 collective-permute-done.3.refs_3_
  13.1 0.0 collective-permute-done.4.refs_4_
  13.2 0.0 collective-permute-done.5.refs_5_
  13.2 0.0 copy-done.1
  13.2 2.0 %shard_map.115 = (bf16[288,128]{1,0:T(8,128)(2,1)S(1)}, bf16[288,128]{1,0:T(8,128)(2,1)S(1)}, bf16[288,128]{1,0:T(8,128)(2,1)S(1)}, bf16[288,128]{1,0:T(8,128)(2...) custom-call(f32[3,7,128]{2,1,0:T(8,128)S(1)} %get-tuple-element.40.t, ...), custom_call_target="tpu_custom_call" | custom-call | tf_op jit(solution)/shard_map/pallas_call | solution.py:553
  15.2 2.9 %collective-permute-start.10 = (bf16[288,128]{1,0:T(8,128)(2,1)S(1)}, bf16[288,128]{1,0:T(8,128)(2,1)S(1)}, u32[]{:S(2)}, u32[]{:S(2)}) collective-permute-start(bf16[288,128]{1,0:T(8,128)(2,1)S(1)} %get-tuple-element.54), channel_id=1, source_target_pairs={{0,24},{4,28},{8,16},{12,20},{16,8},{20,12},{24,0},{28,4},{1,25},{... | collective-permute-start | bytes 221192 | tf_op jit(solution)/shard_map/ppermute | solution.py:578
  18.0 0.0 collective-permute-start.12
  18.1 1.5 %collective-permute-start.6 = (bf16[288,128]{1,0:T(8,128)(2,1)S(1)}, bf16[288,128]{1,0:T(8,128)(2,1)S(1)}, u32[]{:S(2)}, u32[]{:S(2)}) collective-permute-start(bf16[288,128]{1,0:T(8,128)(2,1)S(1)} %get-tuple-element.50), channel_id=1, source_target_pairs={{0,16},{4,20},{8,24},{12,28},{16,0},{20,4},{24,8},{28,12},{1,17},{... | collective-permute-start | bytes 221192 | tf_op jit(solution)/shard_map/ppermute | solution.py:578
  19.5 1.5 %collective-permute-start.7 = (bf16[288,128]{1,0:T(8,128)(2,1)S(1)}, bf16[288,128]{1,0:T(8,128)(2,1)S(1)}, u32[]{:S(2)}, u32[]{:S(2)}) collective-permute-start(bf16[288,128]{1,0:T(8,128)(2,1)S(1)} %get-tuple-element.51), channel_id=1, source_target_pairs={{0,8},{4,12},{8,0},{12,4},{16,24},{20,28},{24,16},{28,20},{1,9},{5... | collective-permute-start | bytes 221192 | tf_op jit(solution)/shard_map/ppermute | solution.py:578
  21.0 0.2 collective-permute-start.8
  21.2 0.0 collective-permute-done.10._.refs_0_
  21.2 0.6 %collective-permute-start.9 = (bf16[288,128]{1,0:T(8,128)(2,1)S(1)}, bf16[288,128]{1,0:T(8,128)(2,1)S(1)}, u32[]{:S(2)}, u32[]{:S(2)}) collective-permute-start(bf16[288,128]{1,0:T(8,128)(2,1)S(1)} %get-tuple-element.53), channel_id=1, source_target_pairs={{0,20},{4,16},{8,28},{12,24},{16,4},{20,0},{24,12},{28,8},{1,21},{... | collective-permute-start | bytes 221192 | tf_op jit(solution)/shard_map/ppermute | solution.py:578
  21.8 0.0 copy-start
  21.8 0.0 copy-start.2
  21.8 0.9 %shard_map.116 = (f32[128,1024]{1,0:T(8,128)S(1)}, bf16[288,128]{1,0:T(8,128)(2,1)S(1)}) custom-call(bf16[288,128]{1,0:T(8,128)(2,1)S(1)} %collective-permute-done.10._.refs_0_, f32[4,512,128]{2,1,0:T(8,128)S(1)} %get-tuple-element.55.refs_0_, f32[4,512,128]{2,1,0:T(8,128)S(1)} %get-tuple-element.56.refs_1_, bf16[256,512]{1,0:T(8,128)(2,1)S(1)} %copy-done.1, ...), custom_call_target="tpu_custom_call" | custom-call | tf_op jit(solution)/shard_map/pallas_call | solution.py:553
  22.8 0.7 %collective-permute-done.12.refs_1_ = bf16[288,128]{1,0:T(8,128)(2,1)S(1)} collective-permute-done((bf16[288,128]{1,0:T(8,128)(2,1)S(1)}, bf16[288,128]{1,0:T(8,128)(2,1)S(1)}, u32[]{:S(2)}, u32[]{:S(2)}) %collective-permute-start.12) | collective-permute-done | bytes 73760 | tf_op jit(solution)/shard_map/ppermute | solution.py:578
  23.5 0.1 collective-permute-start.11
  23.5 0.0 copy-done
  23.5 0.0 copy-done.2
  23.5 1.2 %shard_map.117 = (bf16[128,1024]{1,0:T(8,128)(2,1)}, bf16[3,128,1024]{2,1,0:T(8,128)(2,1)}, f32[1,128,1024]{2,1,0:T(8,128)}) custom-call(bf16[128,1024]{1,0:T(8,128)(2,1)S(1)} %copy-done, f32[3,7,1024]{2,1,0:T(8,128)S(1)} %copy-done.2, f32[6,3,128,128]{3,2,1,0:T(8,128)S(1)} %get-tuple-element.35.far_ref, f32[2,3,128,128]{3,2,1,0:T(8,128)S(1)} %get-tuple-element.39.near_ref, ...), custom_call_target="tpu_custom_call" | custom-call | tf_op jit(solution)/shard_map/pallas_call | solution.py:553
  24.8 0.0 collective-permute-done.6.refs_0_
  24.8 0.0 collective-permute-done.7.refs_1_
  24.8 0.8 %collective-permute-done.8.refs_2_ = bf16[288,128]{1,0:T(8,128)(2,1)S(1)} collective-permute-done((bf16[288,128]{1,0:T(8,128)(2,1)S(1)}, bf16[288,128]{1,0:T(8,128)(2,1)S(1)}, u32[]{:S(2)}, u32[]{:S(2)}) %collective-permute-start.8) | collective-permute-done | bytes 73760 | tf_op jit(solution)/shard_map/ppermute | solution.py:578
  25.6 0.0 collective-permute-done.9.refs_3_
  25.6 0.0 collective-permute-done.11.refs_4_
  25.6 1.5 %shard_map.118 = (bf16[128,1024]{1,0:T(8,128)(2,1)}, bf16[3,128,1024]{2,1,0:T(8,128)(2,1)}) custom-call(bf16[128,1024]{1,0:T(8,128)(2,1)S(1)} %copy-done, f32[3,7,1024]{2,1,0:T(8,128)S(1)} %copy-done.2, f32[6,3,128,128]{3,2,1,0:T(8,128)S(1)} %get-tuple-element.35.far_ref, ...), custom_call_target="tpu_custom_call", output_to_operand_aliasing={{0}: (9, {}), {1}: (10, {})} | custom-call | tf_op jit(solution)/shard_map/pallas_call | solution.py:553
Async XLA Ops:
  2.7 8.3 %collective-permute-start = (bf16[576,128]{1,0:T(8,128)(2,1)S(1)}, bf16[576,128]{1,0:T(8,128)(2,1)S(1)}, u32[]{:S(2)}, u32[]{:S(2)}) collective-permute-start(bf16[576,128]{1,0:T(8,128)(2,1)S(1)} %get-tuple-element.38), channel_id=1, source_target_pairs={{0,24},{4,28},{8,16},{12,20},{16,8},{20,12},{24,0},{28,4},{1,25},{... | collective-permute-start | bytes 442376 | tf_op jit(solution)/shard_map/ppermute | solution.py:578
  6.6 5.6 %collective-permute-start.1 = (bf16[288,128]{1,0:T(8,128)(2,1)S(1)}, bf16[288,128]{1,0:T(8,128)(2,1)S(1)}, u32[]{:S(2)}, u32[]{:S(2)}) collective-permute-start(bf16[288,128]{1,0:T(8,128)(2,1)S(1)} %get-tuple-element.44), channel_id=1, source_target_pairs={{0,16},{4,20},{8,24},{12,28},{16,0},{20,4},{24,8},{28,12},{1,17},{... | collective-permute-start | bytes 221192 | tf_op jit(solution)/shard_map/ppermute | solution.py:578
  7.1 6.0 %collective-permute-start.2 = (bf16[288,128]{1,0:T(8,128)(2,1)S(1)}, bf16[288,128]{1,0:T(8,128)(2,1)S(1)}, u32[]{:S(2)}, u32[]{:S(2)}) collective-permute-start(bf16[288,128]{1,0:T(8,128)(2,1)S(1)} %get-tuple-element.45), channel_id=1, source_target_pairs={{0,8},{4,12},{8,0},{12,4},{16,24},{20,28},{24,16},{28,20},{1,9},{5... | collective-permute-start | bytes 221192 | tf_op jit(solution)/shard_map/ppermute | solution.py:578
  7.3 5.9 %collective-permute-start.3 = (bf16[288,128]{1,0:T(8,128)(2,1)S(1)}, bf16[288,128]{1,0:T(8,128)(2,1)S(1)}, u32[]{:S(2)}, u32[]{:S(2)}) collective-permute-start(bf16[288,128]{1,0:T(8,128)(2,1)S(1)} %get-tuple-element.46), channel_id=1, source_target_pairs={{0,12},{4,8},{8,4},{12,0},{16,28},{20,24},{24,20},{28,16},{1,13},{... | collective-permute-start | bytes 221192 | tf_op jit(solution)/shard_map/ppermute | solution.py:578
  7.8 5.4 %collective-permute-start.4 = (bf16[288,128]{1,0:T(8,128)(2,1)S(1)}, bf16[288,128]{1,0:T(8,128)(2,1)S(1)}, u32[]{:S(2)}, u32[]{:S(2)}) collective-permute-start(bf16[288,128]{1,0:T(8,128)(2,1)S(1)} %get-tuple-element.47), channel_id=1, source_target_pairs={{0,20},{4,16},{8,28},{12,24},{16,4},{20,0},{24,12},{28,8},{1,21},{... | collective-permute-start | bytes 221192 | tf_op jit(solution)/shard_map/ppermute | solution.py:578
  11.2 2.0 %collective-permute-start.5 = (bf16[576,128]{1,0:T(8,128)(2,1)S(1)}, bf16[576,128]{1,0:T(8,128)(2,1)S(1)}, u32[]{:S(2)}, u32[]{:S(2)}) collective-permute-start(bf16[576,128]{1,0:T(8,128)(2,1)S(1)} %get-tuple-element.48), channel_id=1, source_target_pairs={{0,4},{4,0},{8,12},{12,8},{16,20},{20,16},{24,28},{28,24},{1,5},{5... | collective-permute-start | bytes 442376 | tf_op jit(solution)/shard_map/ppermute | solution.py:578
  11.3 1.9 %copy-start.1 = (bf16[256,512]{1,0:T(8,128)(2,1)S(1)}, bf16[256,512]{1,0:T(8,128)(2,1)}, u32[]{:S(2)}) copy-start(bf16[256,512]{1,0:T(8,128)(2,1)} %constant.8.clone.inverse.refs_2_) | copy-start | bytes 786436
  15.2 6.1 %collective-permute-start.10 = (bf16[288,128]{1,0:T(8,128)(2,1)S(1)}, bf16[288,128]{1,0:T(8,128)(2,1)S(1)}, u32[]{:S(2)}, u32[]{:S(2)}) collective-permute-start(bf16[288,128]{1,0:T(8,128)(2,1)S(1)} %get-tuple-element.54), channel_id=1, source_target_pairs={{0,24},{4,28},{8,16},{12,20},{16,8},{20,12},{24,0},{28,4},{1,25},{... | collective-permute-start | bytes 221192 | tf_op jit(solution)/shard_map/ppermute | solution.py:578
  18.0 5.5 %collective-permute-start.12 = (bf16[288,128]{1,0:T(8,128)(2,1)S(1)}, bf16[288,128]{1,0:T(8,128)(2,1)S(1)}, u32[]{:S(2)}, u32[]{:S(2)}) collective-permute-start(bf16[288,128]{1,0:T(8,128)(2,1)S(1)} %get-tuple-element.60), channel_id=1, source_target_pairs={{0,28},{4,24},{8,20},{12,16},{16,12},{20,8},{24,4},{28,0},{1,29},{... | collective-permute-start | bytes 221192 | tf_op jit(solution)/shard_map/ppermute | solution.py:578
  18.1 6.7 %collective-permute-start.6 = (bf16[288,128]{1,0:T(8,128)(2,1)S(1)}, bf16[288,128]{1,0:T(8,128)(2,1)S(1)}, u32[]{:S(2)}, u32[]{:S(2)}) collective-permute-start(bf16[288,128]{1,0:T(8,128)(2,1)S(1)} %get-tuple-element.50), channel_id=1, source_target_pairs={{0,16},{4,20},{8,24},{12,28},{16,0},{20,4},{24,8},{28,12},{1,17},{... | collective-permute-start | bytes 221192 | tf_op jit(solution)/shard_map/ppermute | solution.py:578
  19.5 5.2 %collective-permute-start.7 = (bf16[288,128]{1,0:T(8,128)(2,1)S(1)}, bf16[288,128]{1,0:T(8,128)(2,1)S(1)}, u32[]{:S(2)}, u32[]{:S(2)}) collective-permute-start(bf16[288,128]{1,0:T(8,128)(2,1)S(1)} %get-tuple-element.51), channel_id=1, source_target_pairs={{0,8},{4,12},{8,0},{12,4},{16,24},{20,28},{24,16},{28,20},{1,9},{5... | collective-permute-start | bytes 221192 | tf_op jit(solution)/shard_map/ppermute | solution.py:578
  21.0 4.6 %collective-permute-start.8 = (bf16[288,128]{1,0:T(8,128)(2,1)S(1)}, bf16[288,128]{1,0:T(8,128)(2,1)S(1)}, u32[]{:S(2)}, u32[]{:S(2)}) collective-permute-start(bf16[288,128]{1,0:T(8,128)(2,1)S(1)} %get-tuple-element.52), channel_id=1, source_target_pairs={{0,12},{4,8},{8,4},{12,0},{16,28},{20,24},{24,20},{28,16},{1,13},{... | collective-permute-start | bytes 221192 | tf_op jit(solution)/shard_map/ppermute | solution.py:578
  21.2 4.3 %collective-permute-start.9 = (bf16[288,128]{1,0:T(8,128)(2,1)S(1)}, bf16[288,128]{1,0:T(8,128)(2,1)S(1)}, u32[]{:S(2)}, u32[]{:S(2)}) collective-permute-start(bf16[288,128]{1,0:T(8,128)(2,1)S(1)} %get-tuple-element.53), channel_id=1, source_target_pairs={{0,20},{4,16},{8,28},{12,24},{16,4},{20,0},{24,12},{28,8},{1,21},{... | collective-permute-start | bytes 221192 | tf_op jit(solution)/shard_map/ppermute | solution.py:578
  21.8 1.7 %copy-start = (bf16[128,1024]{1,0:T(8,128)(2,1)S(1)}, bf16[128,1024]{1,0:T(8,128)(2,1)}, u32[]{:S(2)}) copy-start(bf16[128,1024]{1,0:T(8,128)(2,1)} %g_ref.5) | copy-start | bytes 786436
  21.8 1.7 %copy-start.2 = (f32[3,7,1024]{2,1,0:T(8,128)S(1)}, f32[3,7,1024]{2,1,0:T(8,128)}, u32[]{:S(2)}) copy-start(f32[3,7,1024]{2,1,0:T(8,128)} %taps_ref.5) | copy-start | bytes 258052
  23.5 2.1 %collective-permute-start.11 = (bf16[288,128]{1,0:T(8,128)(2,1)S(1)}, bf16[288,128]{1,0:T(8,128)(2,1)S(1)}, u32[]{:S(2)}, u32[]{:S(2)}) collective-permute-start(bf16[288,128]{1,0:T(8,128)(2,1)S(1)} %get-tuple-element.58), channel_id=1, source_target_pairs={{0,4},{4,0},{8,12},{12,8},{16,20},{20,16},{24,28},{28,24},{1,5},{5... | collective-permute-start | bytes 221192 | tf_op jit(solution)/shard_map/ppermute | solution.py:578

commit v6 on v5

--- a/solution.py
+++ b/solution.py
@@ -217,6 +217,7 @@
         filtered.append(result)
     query_f, key_f, value_f = filtered
     cotangent = source[3].astype(jnp.float32)
+    filtered_ref[3] = cotangent
     gated = head_rows(padded[slot, 1, pl.ds(8, 8), :], key_f * value_f, halo)
     grad_long = head_rows(cotangent[:8], cotangent * query_f, halo)
     out_ref[pl.ds(0, rows), :] = gated.astype(jnp.bfloat16)
@@ -400,7 +401,9 @@
     size = own_ref.shape[0]
     in_refs = [first_ref.at[pl.ds(0, size)], shared_ref.at[pl.ds(size, size)], *others]
     in_refs += [shared_ref.at[pl.ds(0, size)], own_ref]
-    out_refs, refs = refs[count - 1 : 2 * count - 1], refs[2 * count - 1 :]
+    first_out, *out_refs = refs[count - 1 : 2 * count - 2]
+    out_refs = [first_out.at[pl.ds(0, size)], first_out.at[pl.ds(size, size)], *out_refs]
+    refs = refs[2 * count - 2 :]
     spec_x, spec_g, edges, firsts, joined, heads, pairs, spec_y, extra = refs
     me = lax.axis_index("context")
     rows = pairs.shape[1]
@@ -423,7 +426,7 @@
         store_tiles(spec_y, LANES, backs, pair, bins)
         return carry
 
-    lax.fori_loop(0, bins // 16, body, 0, unroll=2)
+    lax.fori_loop(0, bins // 16, body, 0, unroll=8)
     extra[...] = jnp.zeros(extra.shape, jnp.float32)
     for index in range(wide):
         both = jnp.dot(inverse[...], spec_y[index], preferred_element_type=jnp.float32).astype(jnp.bfloat16)
@@ -450,8 +453,13 @@
         out_ref[pl.ds(2 * rows, extra.shape[1]), :] = extra[block + 1].astype(jnp.bfloat16)
 
 
-def correlate_kernel(scale, spec_x, spec_g, inverse, parcel_ref, out_ref, parcel_out, spec_y):
-    parcel_out[...] = parcel_ref[...]
+def share_kernel(filter_ref, parcel_ref, first_ref, shared_ref):
+    rows = parcel_ref.shape[0]
+    shared_ref[pl.ds(0, rows), :] = parcel_ref[...]
+    shared_ref[pl.ds(rows, rows), :] = first_ref[pl.ds(rows, rows), :]
+
+
+def correlate_kernel(scale, spec_x, spec_g, inverse, out_ref, spec_y):
     wide = spec_x.shape[0]
     bins = inverse.shape[0]
 
@@ -469,17 +477,17 @@
         store_tiles(spec_y, 0, tiles, pair, bins)
         return carry
 
-    lax.fori_loop(0, bins // 16, body, 0, unroll=2)
+    lax.fori_loop(0, bins // 16, body, 0, unroll=8)
     for index in range(wide):
         result = jnp.dot(inverse[...], spec_y[index], preferred_element_type=jnp.float32)
         out_ref[:, pl.ds(index * bins, bins)] = result.T * scale
 
 
 def finish_channels(
-    order, places, in_refs, g_ref, taps_ref, held, padded, extra, results, leave
+    order, places, in_refs, taps_ref, held, padded, extra, results, leave
 ):
     me = lax.axis_index("context")
-    rows = g_ref.shape[0]
+    rows = held[0].shape[2]
     span = taps_ref.shape[1]
     halo = span - 1
     held = [ref.at[index] for ref in held for index in range(ref.shape[0])]
@@ -488,7 +496,7 @@
         slot = index % padded.shape[0]
         edge_rows = in_ref.shape[0] - 2 * rows
         query_f, key_f, value_f = [held[place][which] for which in range(3)]
-        cotangent = g_ref[:, lanes].astype(jnp.float32)
+        cotangent = held[place][3]
         long_conv = in_ref[pl.ds(0, rows), :].astype(jnp.float32)
         back = in_ref[pl.ds(rows, rows), :].astype(jnp.float32)
         extra[slot, pl.ds(0, edge_rows), :] = in_ref[pl.ds(2 * rows, edge_rows), :].astype(jnp.float32)
@@ -511,8 +519,9 @@
             leave(index, which)
 
 
-def receive_kernel(order, places, g_ref, taps_ref, far_ref, near_ref, filter_ref, *refs):
-    in_refs = refs[: len(places)]
+def receive_kernel(order, places, taps_ref, far_ref, near_ref, filter_ref, *refs):
+    size = 2 * far_ref.shape[2] + round_up(5 * (taps_ref.shape[1] - 1), 16)
+    in_refs = [ref.at[pl.ds((place == 1) * size, size)] for place, ref in zip(places, refs)]
     mixed_ref, grads_ref, filter_out, padded, extra, results, sems, filter_sem = refs[-8:]
     me = lax.axis_index("context")
     copies = []
@@ -528,17 +537,17 @@
 
     held = (far_ref, near_ref)
     finish_channels(
-        order, places, in_refs, g_ref, taps_ref, held, padded, extra, results, leave
+        order, places, in_refs, taps_ref, held, padded, extra, results, leave
     )
     for copy in copies:
         copy.wait()
 
 
-def last_kernel(order, places, g_ref, taps_ref, far_ref, near_ref, *refs):
+def last_kernel(order, places, taps_ref, far_ref, near_ref, *refs):
     in_refs, refs = refs[: len(places)], refs[len(places) + 2 :]
     mixed_ref, grads_ref, padded, extra, results, sems = refs
     receive_kernel(
-        order, places, g_ref, taps_ref, far_ref, near_ref, None, *in_refs,
+        order, places, taps_ref, far_ref, near_ref, None, *in_refs,
         mixed_ref, grads_ref, None, padded, extra, results, sems, None,
     )
 
@@ -605,7 +614,7 @@
 
     first, *sent, far_filtered, filter_here, hi_here, lo_here, landed, taps = on_device(
         functools.partial(send_kernel, order, far, near, len(sources)),
-        [double, *parcels[: len(far) - 2], floats(len(far), 3, rows, LANES)]
+        [double, *parcels[: len(far) - 2], floats(len(far), 4, rows, LANES)]
         + [jax.ShapeDtypeStruct(value.shape, value.dtype) for value in sources]
         + [
             jax.ShapeDtypeStruct((len(near), *inputs), jnp.bfloat16),
@@ -626,7 +635,7 @@
     others = [exchange(value, order[place]) for place, value in zip(far[2:], sent)]
     shared, kept_here, near_filtered, own = on_device(
         near_kernel,
-        [double, parcel, floats(len(near), 3, rows, LANES), floats(*own_taps)],
+        [double, parcel, floats(len(near), 4, rows, LANES), floats(*own_taps)],
         made,
         (landed, taps, first),
         cover=True,
@@ -641,7 +650,7 @@
     )
     *results, spec_x, spec_g = on_device(
         functools.partial(convolve_kernel, order),
-        parcels + [jax.ShapeDtypeStruct(spectra, jnp.float32)] * 2,
+        [double, *parcels[2:], floats(*spectra), floats(*spectra)],
         [
             (blocks, edge_rows, LANES),
             (blocks, 2, 8, LANES),
@@ -653,17 +662,20 @@
         ],
         (own, spec_h, hi_here, inverse, *arrived),
     )
-    returned = [exchange(results[place], order[place]) for place in far]
-    filter_grad, parcel = on_device(
+    first, *sent = results
+    first = exchange(first, order[0])
+    others = [exchange(value, order[place]) for place, value in zip(far[2:], sent)]
+    (filter_grad,) = on_device(
         functools.partial(correlate_kernel, 1.0 / math.sqrt(seq_len)),
-        [jax.ShapeDtypeStruct(long_filter.shape[1:], jnp.float32), parcels[0]],
+        [floats(*long_filter.shape[1:])],
         [pltpu.VMEM(spectra, jnp.bfloat16)],
-        (spec_x, spec_g, inverse, results[near[0]]),
-        unread=returned[0],
-    )
-    returned += [exchange(parcel, order[near[0]]), results[near[1]]]
-    late = far[len(far) // 2 - 1 :] + near[:-1]
-    early = [place for place in range(blocks) if place not in late]
+        (spec_x, spec_g, inverse),
+    )
+    (shared,) = on_device(share_kernel, [double], [], (filter_grad, sent[-2], first))
+    shared = exchange(shared, 1)
+    returned = [first, shared, *others, shared, sent[-1]]
+    early = [0, *far[2:3], near[-1]]
+    late = [place for place in range(blocks) if place not in early]
     outputs = (
         pltpu.HBM((rows, channels), jnp.bfloat16),
         pltpu.HBM((3, rows, channels), jnp.bfloat16),
@@ -678,12 +690,13 @@
             pltpu.SemaphoreType.DMA((len(places), 4)),
         ]
 
-    common = (grad_mixed, short_taps, far_filtered, near_filtered)
+    common = (short_taps, far_filtered, near_filtered)
     *begun, filter_grad = on_device(
         functools.partial(receive_kernel, order, early),
         outputs,
         [*working(early), pltpu.SemaphoreType.DMA(())],
         (*common, filter_grad, *(returned[place] for place in early)),
+        cover=True,
     )
     mixed_out, input_grads = on_device(
         functools.partial(last_kernel, order, late),
@@ -700,7 +713,7 @@
     halo = short_taps.shape[1] - 1
     blocks = lax.axis_size("context")
     power_of_two = blocks & (blocks - 1) == 0
-    fits = power_of_two and blocks > 1 and channels == blocks * LANES and rows % 128 == 0 and halo <= 8
+    fits = power_of_two and blocks > 2 and channels == blocks * LANES and rows % 128 == 0 and halo <= 8
     chosen = block_shards if fits else general_shards
     return chosen(query_proj, key_proj, value_proj, short_taps, long_filter, grad_mixed)
 

time: 27.2 us -> 27 us (level)
    pallas_call x7 -> x8, Pallas kernels: 8.85 us -> 8.69 us  [on_device(): pl.pallas_call(kernel if unread is None else lambda _, *refs: kernel(*ref...]
    ppermute x13 -> x12, starting transfers between devices: 14.5 us -> 14.5 us  [exchange(): lax.ppermute(parcel, 'context', [(i, i ^ mask) for i in range(count)])]
    ppermute x13 -> x12, waiting for transfers between devices: 2.93 us -> 2.94 us  [exchange(): lax.ppermute(parcel, 'context', [(i, i ^ mask) for i in range(count)])]
  transfers between devices with their start and end apart: 13 -> 12, of which waited for: 4 -> 5; matrix products, arithmetic and copies ran while one was open for 0% -> 0% of each run, Pallas kernels for 12% -> 12%
where the time goes in v6:
time: 27 us; the launch traced here: 26.9 us
  starting transfers between devices  14.5 us (54%)
  Pallas kernels  8.69 us (32%)
  waiting for transfers between devices  2.94 us (11%)
  between operations  0.74 us (3%)
    ppermute x12, starting transfers between devices, exchange(): lax.ppermute(parcel, 'context', [(i, i ^ mask) for i in range(count)])  14.5 us
    pallas_call x8, Pallas kernels, on_device(): pl.pallas_call(kernel if unread is None else lambda _, *refs: kernel(*ref...  8.69 us
    ppermute x12, waiting for transfers between devices, exchange(): lax.ppermute(parcel, 'context', [(i, i ^ mask) for i in range(count)])  2.94 us
  transfers between devices with their start and end apart: 12, of which 5 were waited for; matrix products, arithmetic and copies ran while one was open for 0% of the time, Pallas kernels for 12%

profile of v6, /device:TPU:0, one launch (start us, length us, event | category | flops | bytes accessed | tf_op | source)
XLA Modules:
  0.0 26.9 jit_solution(1436294095120899084)
XLA Ops:
  0.6 2.0 %shard_map.112 = (bf16[576,128]{1,0:T(8,128)(2,1)S(1)}, bf16[288,128]{1,0:T(8,128)(2,1)S(1)}, bf16[288,128]{1,0:T(8,128)(2,1)S(1)}, bf16[288,128]{1,0:T(8,128)(2...) custom-call(bf16[128,1024]{1,0:T(8,128)(2,1)} %q_ref.1, ...), custom_call_target="tpu_custom_call" | custom-call | tf_op jit(solution)/shard_map/pallas_call | solution.py:562
  2.7 4.0 %collective-permute-start = (bf16[576,128]{1,0:T(8,128)(2,1)S(1)}, bf16[576,128]{1,0:T(8,128)(2,1)S(1)}, u32[]{:S(2)}, u32[]{:S(2)}) collective-permute-start(bf16[576,128]{1,0:T(8,128)(2,1)S(1)} %get-tuple-element.35), channel_id=1, source_target_pairs={{0,24},{4,28},{8,16},{12,20},{16,8},{20,12},{24,0},{28,4},{1,25},{... | collective-permute-start | bytes 442376 | tf_op jit(solution)/shard_map/ppermute | solution.py:587
  6.6 0.5 %collective-permute-start.1 = (bf16[288,128]{1,0:T(8,128)(2,1)S(1)}, bf16[288,128]{1,0:T(8,128)(2,1)S(1)}, u32[]{:S(2)}, u32[]{:S(2)}) collective-permute-start(bf16[288,128]{1,0:T(8,128)(2,1)S(1)} %get-tuple-element.41), channel_id=1, source_target_pairs={{0,16},{4,20},{8,24},{12,28},{16,0},{20,4},{24,8},{28,12},{1,17},{... | collective-permute-start | bytes 221192 | tf_op jit(solution)/shard_map/ppermute | solution.py:587
  7.1 0.1 collective-permute-start.2
  7.3 0.5 %collective-permute-start.3 = (bf16[288,128]{1,0:T(8,128)(2,1)S(1)}, bf16[288,128]{1,0:T(8,128)(2,1)S(1)}, u32[]{:S(2)}, u32[]{:S(2)}) collective-permute-start(bf16[288,128]{1,0:T(8,128)(2,1)S(1)} %get-tuple-element.43), channel_id=1, source_target_pairs={{0,12},{4,8},{8,4},{12,0},{16,28},{20,24},{24,20},{28,16},{1,13},{... | collective-permute-start | bytes 221192 | tf_op jit(solution)/shard_map/ppermute | solution.py:587
  7.8 2.6 %collective-permute-start.4 = (bf16[288,128]{1,0:T(8,128)(2,1)S(1)}, bf16[288,128]{1,0:T(8,128)(2,1)S(1)}, u32[]{:S(2)}, u32[]{:S(2)}) collective-permute-start(bf16[288,128]{1,0:T(8,128)(2,1)S(1)} %get-tuple-element.44), channel_id=1, source_target_pairs={{0,20},{4,16},{8,28},{12,24},{16,4},{20,0},{24,12},{28,8},{1,21},{... | collective-permute-start | bytes 221192 | tf_op jit(solution)/shard_map/ppermute | solution.py:587
  10.4 0.5 %collective-permute-done.first_ref.refs_0_ = bf16[576,128]{1,0:T(8,128)(2,1)S(1)} collective-permute-done((bf16[576,128]{1,0:T(8,128)(2,1)S(1)}, bf16[576,128]{1,0:T(8,128)(2,1)S(1)}, u32[]{:S(2)}, u32[]{:S(2)}) %collective-permute-start) | collective-permute-done | bytes 147488 | tf_op jit(solution)/shard_map/ppermute | solution.py:587
  10.9 0.3 shard_map.113
  11.2 0.1 collective-permute-start.5
  11.3 0.0 copy-start
  11.3 1.0 %shard_map.114.spec_h = f32[4,512,128]{2,1,0:T(8,128)S(1)} custom-call(f32[128,1024]{1,0:T(8,128)S(1)} %get-tuple-element.38.h_ref, bf16[512,256]{1,0:T(8,128)(2,1)S(1)} %get-tuple-element.39.forward_hi.forward, bf16[512,256]{1,0:T(8,128)(2,1)S(1)} %get-tuple-element.40.forward_lo), custom_call_target="tpu_custom_call" | custom-call | flops 10000000000 | bytes 100000000 | tf_op jit(solution)/shard_map/pallas_call | solution.py:562
  12.3 0.0 collective-permute-done.1.refs_1_
  12.3 0.9 %collective-permute-done.2.refs_2_ = bf16[288,128]{1,0:T(8,128)(2,1)S(1)} collective-permute-done((bf16[288,128]{1,0:T(8,128)(2,1)S(1)}, bf16[288,128]{1,0:T(8,128)(2,1)S(1)}, u32[]{:S(2)}, u32[]{:S(2)}) %collective-permute-start.2) | collective-permute-done | bytes 73760 | tf_op jit(solution)/shard_map/ppermute | solution.py:587
  13.1 0.0 collective-permute-done.3.refs_3_
  13.1 0.0 collective-permute-done.4.refs_4_
  13.2 0.0 collective-permute-done.5.refs_5_
  13.2 0.0 copy-done
  13.2 1.9 %shard_map.115 = (bf16[576,128]{1,0:T(8,128)(2,1)S(1)}, bf16[288,128]{1,0:T(8,128)(2,1)S(1)}, bf16[288,128]{1,0:T(8,128)(2,1)S(1)}, bf16[288,128]{1,0:T(8,128)(2...) custom-call(f32[3,7,128]{2,1,0:T(8,128)S(1)} %get-tuple-element.37.t, ...), custom_call_target="tpu_custom_call" | custom-call | tf_op jit(solution)/shard_map/pallas_call | solution.py:562
  15.1 2.9 %collective-permute-start.6 = (bf16[576,128]{1,0:T(8,128)(2,1)S(1)}, bf16[576,128]{1,0:T(8,128)(2,1)S(1)}, u32[]{:S(2)}, u32[]{:S(2)}) collective-permute-start(bf16[576,128]{1,0:T(8,128)(2,1)S(1)} %get-tuple-element.50), channel_id=1, source_target_pairs={{0,24},{4,28},{8,16},{12,20},{16,8},{20,12},{24,0},{28,4},{1,25},{... | collective-permute-start | bytes 442376 | tf_op jit(solution)/shard_map/ppermute | solution.py:587
  17.9 0.7 %collective-permute-start.11 = (bf16[288,128]{1,0:T(8,128)(2,1)S(1)}, bf16[288,128]{1,0:T(8,128)(2,1)S(1)}, u32[]{:S(2)}, u32[]{:S(2)}) collective-permute-start(bf16[288,128]{1,0:T(8,128)(2,1)S(1)} %get-tuple-element.54), channel_id=1, source_target_pairs={{0,16},{4,20},{8,24},{12,28},{16,0},{20,4},{24,8},{28,12},{1,17},{... | collective-permute-start | bytes 221192 | tf_op jit(solution)/shard_map/ppermute | solution.py:587
  18.7 0.0 collective-permute-start.8
  18.7 0.9 %collective-permute-start.9 = (bf16[288,128]{1,0:T(8,128)(2,1)S(1)}, bf16[288,128]{1,0:T(8,128)(2,1)S(1)}, u32[]{:S(2)}, u32[]{:S(2)}) collective-permute-start(bf16[288,128]{1,0:T(8,128)(2,1)S(1)} %get-tuple-element.52), channel_id=1, source_target_pairs={{0,12},{4,8},{8,4},{12,0},{16,28},{20,24},{24,20},{28,16},{1,13},{... | collective-permute-start | bytes 221192 | tf_op jit(solution)/shard_map/ppermute | solution.py:587
  19.6 2.1 %collective-permute-start.10 = (bf16[288,128]{1,0:T(8,128)(2,1)S(1)}, bf16[288,128]{1,0:T(8,128)(2,1)S(1)}, u32[]{:S(2)}, u32[]{:S(2)}) collective-permute-start(bf16[288,128]{1,0:T(8,128)(2,1)S(1)} %get-tuple-element.53), channel_id=1, source_target_pairs={{0,20},{4,16},{8,28},{12,24},{16,4},{20,0},{24,12},{28,8},{1,21},{... | collective-permute-start | bytes 221192 | tf_op jit(solution)/shard_map/ppermute | solution.py:587
  21.7 0.0 copy-start.1
  21.7 0.9 %shard_map.116.filter_ref = f32[128,1024]{1,0:T(8,128)S(1)} custom-call(f32[4,512,128]{2,1,0:T(8,128)S(1)} %get-tuple-element.47.spec_x, f32[4,512,128]{2,1,0:T(8,128)S(1)} %get-tuple-element.48.spec_g, bf16[256,512]{1,0:T(8,128)(2,1)S(1)} %copy-done), custom_call_target="tpu_custom_call" | custom-call | tf_op jit(solution)/shard_map/pallas_call | solution.py:562
  22.6 0.1 collective-permute-done.6.first_ref.refs_0_
  22.7 0.1 collective-permute-start.7
  22.8 1.3 %collective-permute-done.11.refs_1_ = bf16[288,128]{1,0:T(8,128)(2,1)S(1)} collective-permute-done((bf16[288,128]{1,0:T(8,128)(2,1)S(1)}, bf16[288,128]{1,0:T(8,128)(2,1)S(1)}, u32[]{:S(2)}, u32[]{:S(2)}) %collective-permute-start.11) | collective-permute-done | bytes 73760 | tf_op jit(solution)/shard_map/ppermute | solution.py:587
  24.1 0.0 copy-done.1
  24.1 1.2 %shard_map.118 = (bf16[128,1024]{1,0:T(8,128)(2,1)}, bf16[3,128,1024]{2,1,0:T(8,128)(2,1)}, f32[1,128,1024]{2,1,0:T(8,128)}) custom-call(f32[3,7,1024]{2,1,0:T(8,128)S(1)} %copy-done.1, f32[6,4,128,128]{3,2,1,0:T(8,128)S(1)} %get-tuple-element.32.far_ref, f32[2,4,128,128]{3,2,1,0:T(8,128)S(1)} %get-tuple-element.36.near_ref, ...), custom_call_target="tpu_custom_call" | custom-call | flops 10000000000 | bytes 100000000 | tf_op jit(solution)/shard_map/pallas_call | solution.py:562
  25.3 0.0 collective-permute-done.8.refs_1_
  25.3 0.0 collective-permute-done.9.refs_2_
  25.3 0.1 collective-permute-done.10.refs_3_
  25.4 0.0 collective-permute-done.7.refs_0_.refs_4_
  25.4 1.4 %shard_map.119 = (bf16[128,1024]{1,0:T(8,128)(2,1)}, bf16[3,128,1024]{2,1,0:T(8,128)(2,1)}) custom-call(f32[3,7,1024]{2,1,0:T(8,128)S(1)} %copy-done.1, f32[6,4,128,128]{3,2,1,0:T(8,128)S(1)} %get-tuple-element.32.far_ref, f32[2,4,128,128]{3,2,1,0:T(8,128)S(1)} %get-tuple-element.36.near_ref, ...), custom_call_target="tpu_custom_call", output_to_operand_aliasing={{0}: (8, {}), {1}: (9, {})} | custom-call | tf_op jit(solution)/shard_map/pallas_call | solution.py:562
  (1 shorter events, 0.0 us)
Async XLA Ops:
  2.7 8.3 %collective-permute-start = (bf16[576,128]{1,0:T(8,128)(2,1)S(1)}, bf16[576,128]{1,0:T(8,128)(2,1)S(1)}, u32[]{:S(2)}, u32[]{:S(2)}) collective-permute-start(bf16[576,128]{1,0:T(8,128)(2,1)S(1)} %get-tuple-element.35), channel_id=1, source_target_pairs={{0,24},{4,28},{8,16},{12,20},{16,8},{20,12},{24,0},{28,4},{1,25},{... | collective-permute-start | bytes 442376 | tf_op jit(solution)/shard_map/ppermute | solution.py:587
  6.6 5.6 %collective-permute-start.1 = (bf16[288,128]{1,0:T(8,128)(2,1)S(1)}, bf16[288,128]{1,0:T(8,128)(2,1)S(1)}, u32[]{:S(2)}, u32[]{:S(2)}) collective-permute-start(bf16[288,128]{1,0:T(8,128)(2,1)S(1)} %get-tuple-element.41), channel_id=1, source_target_pairs={{0,16},{4,20},{8,24},{12,28},{16,0},{20,4},{24,8},{28,12},{1,17},{... | collective-permute-start | bytes 221192 | tf_op jit(solution)/shard_map/ppermute | solution.py:587
  7.1 6.0 %collective-permute-start.2 = (bf16[288,128]{1,0:T(8,128)(2,1)S(1)}, bf16[288,128]{1,0:T(8,128)(2,1)S(1)}, u32[]{:S(2)}, u32[]{:S(2)}) collective-permute-start(bf16[288,128]{1,0:T(8,128)(2,1)S(1)} %get-tuple-element.42), channel_id=1, source_target_pairs={{0,8},{4,12},{8,0},{12,4},{16,24},{20,28},{24,16},{28,20},{1,9},{5... | collective-permute-start | bytes 221192 | tf_op jit(solution)/shard_map/ppermute | solution.py:587
  7.3 5.9 %collective-permute-start.3 = (bf16[288,128]{1,0:T(8,128)(2,1)S(1)}, bf16[288,128]{1,0:T(8,128)(2,1)S(1)}, u32[]{:S(2)}, u32[]{:S(2)}) collective-permute-start(bf16[288,128]{1,0:T(8,128)(2,1)S(1)} %get-tuple-element.43), channel_id=1, source_target_pairs={{0,12},{4,8},{8,4},{12,0},{16,28},{20,24},{24,20},{28,16},{1,13},{... | collective-permute-start | bytes 221192 | tf_op jit(solution)/shard_map/ppermute | solution.py:587
  7.8 5.4 %collective-permute-start.4 = (bf16[288,128]{1,0:T(8,128)(2,1)S(1)}, bf16[288,128]{1,0:T(8,128)(2,1)S(1)}, u32[]{:S(2)}, u32[]{:S(2)}) collective-permute-start(bf16[288,128]{1,0:T(8,128)(2,1)S(1)} %get-tuple-element.44), channel_id=1, source_target_pairs={{0,20},{4,16},{8,28},{12,24},{16,4},{20,0},{24,12},{28,8},{1,21},{... | collective-permute-start | bytes 221192 | tf_op jit(solution)/shard_map/ppermute | solution.py:587
  11.2 2.0 %collective-permute-start.5 = (bf16[576,128]{1,0:T(8,128)(2,1)S(1)}, bf16[576,128]{1,0:T(8,128)(2,1)S(1)}, u32[]{:S(2)}, u32[]{:S(2)}) collective-permute-start(bf16[576,128]{1,0:T(8,128)(2,1)S(1)} %get-tuple-element.45), channel_id=1, source_target_pairs={{0,4},{4,0},{8,12},{12,8},{16,20},{20,16},{24,28},{28,24},{1,5},{5... | collective-permute-start | bytes 442376 | tf_op jit(solution)/shard_map/ppermute | solution.py:587
  11.3 1.9 %copy-start = (bf16[256,512]{1,0:T(8,128)(2,1)S(1)}, bf16[256,512]{1,0:T(8,128)(2,1)}, u32[]{:S(2)}) copy-start(bf16[256,512]{1,0:T(8,128)(2,1)} %constant.8.clone.inverse) | copy-start | bytes 786436
  15.1 7.6 %collective-permute-start.6 = (bf16[576,128]{1,0:T(8,128)(2,1)S(1)}, bf16[576,128]{1,0:T(8,128)(2,1)S(1)}, u32[]{:S(2)}, u32[]{:S(2)}) collective-permute-start(bf16[576,128]{1,0:T(8,128)(2,1)S(1)} %get-tuple-element.50), channel_id=1, source_target_pairs={{0,24},{4,28},{8,16},{12,20},{16,8},{20,12},{24,0},{28,4},{1,25},{... | collective-permute-start | bytes 442376 | tf_op jit(solution)/shard_map/ppermute | solution.py:587
  17.9 6.1 %collective-permute-start.11 = (bf16[288,128]{1,0:T(8,128)(2,1)S(1)}, bf16[288,128]{1,0:T(8,128)(2,1)S(1)}, u32[]{:S(2)}, u32[]{:S(2)}) collective-permute-start(bf16[288,128]{1,0:T(8,128)(2,1)S(1)} %get-tuple-element.54), channel_id=1, source_target_pairs={{0,16},{4,20},{8,24},{12,28},{16,0},{20,4},{24,8},{28,12},{1,17},{... | collective-permute-start | bytes 221192 | tf_op jit(solution)/shard_map/ppermute | solution.py:587
  18.7 6.6 %collective-permute-start.8 = (bf16[288,128]{1,0:T(8,128)(2,1)S(1)}, bf16[288,128]{1,0:T(8,128)(2,1)S(1)}, u32[]{:S(2)}, u32[]{:S(2)}) collective-permute-start(bf16[288,128]{1,0:T(8,128)(2,1)S(1)} %get-tuple-element.51), channel_id=1, source_target_pairs={{0,8},{4,12},{8,0},{12,4},{16,24},{20,28},{24,16},{28,20},{1,9},{5... | collective-permute-start | bytes 221192 | tf_op jit(solution)/shard_map/ppermute | solution.py:587
  18.7 6.6 %collective-permute-start.9 = (bf16[288,128]{1,0:T(8,128)(2,1)S(1)}, bf16[288,128]{1,0:T(8,128)(2,1)S(1)}, u32[]{:S(2)}, u32[]{:S(2)}) collective-permute-start(bf16[288,128]{1,0:T(8,128)(2,1)S(1)} %get-tuple-element.52), channel_id=1, source_target_pairs={{0,12},{4,8},{8,4},{12,0},{16,28},{20,24},{24,20},{28,16},{1,13},{... | collective-permute-start | bytes 221192 | tf_op jit(solution)/shard_map/ppermute | solution.py:587
  19.6 5.9 %collective-permute-start.10 = (bf16[288,128]{1,0:T(8,128)(2,1)S(1)}, bf16[288,128]{1,0:T(8,128)(2,1)S(1)}, u32[]{:S(2)}, u32[]{:S(2)}) collective-permute-start(bf16[288,128]{1,0:T(8,128)(2,1)S(1)} %get-tuple-element.53), channel_id=1, source_target_pairs={{0,20},{4,16},{8,28},{12,24},{16,4},{20,0},{24,12},{28,8},{1,21},{... | collective-permute-start | bytes 221192 | tf_op jit(solution)/shard_map/ppermute | solution.py:587
  21.7 2.3 %copy-start.1 = (f32[3,7,1024]{2,1,0:T(8,128)S(1)}, f32[3,7,1024]{2,1,0:T(8,128)}, u32[]{:S(2)}) copy-start(f32[3,7,1024]{2,1,0:T(8,128)} %taps_ref.5) | copy-start | bytes 258052
  22.7 2.7 %collective-permute-start.7 = (bf16[576,128]{1,0:T(8,128)(2,1)S(1)}, bf16[576,128]{1,0:T(8,128)(2,1)S(1)}, u32[]{:S(2)}, u32[]{:S(2)}) collective-permute-start(bf16[576,128]{1,0:T(8,128)(2,1)S(1)} %shard_map.117), channel_id=1, source_target_pairs={{0,4},{4,0},{8,12},{12,8},{16,20},{20,16},{24,28},{28,24},{1,5},{5... | collective-permute-start | bytes 442376 | tf_op jit(solution)/shard_map/ppermute | solution.py:587

commit v7 on v6

--- a/solution.py
+++ b/solution.py
@@ -578,7 +578,7 @@
 def exchange_order(count):
     return sorted(
         range(count),
-        key=lambda mask: (mask == 0, -(mask >> 1).bit_count(), mask % 2, mask if mask % 2 else -mask),
+        key=lambda mask: (mask == 0, -(mask >> 1).bit_count(), mask % 2, -mask),
     )
 
 

time: 27 us -> 27 us (level)
  starting transfers between devices: 14.5 us -> 14.1 us
  waiting for transfers between devices: 2.94 us -> 3.3 us
    ppermute x12, starting transfers between devices: 14.5 us -> 14.1 us  [exchange(): lax.ppermute(parcel, 'context', [(i, i ^ mask) for i in range(count)])]
    ppermute x12, waiting for transfers between devices: 2.94 us -> 3.3 us  [exchange(): lax.ppermute(parcel, 'context', [(i, i ^ mask) for i in range(count)])]
  transfers between devices with their start and end apart: 12 -> 12, of which waited for: 5 -> 6; matrix products, arithmetic and copies ran while one was open for 0% -> 0% of each run, Pallas kernels for 12% -> 12%
where the time goes in v7:
time: 27 us; the launch traced here: 26.9 us
  starting transfers between devices  14.1 us (52%)
  Pallas kernels  8.7 us (32%)
  waiting for transfers between devices  3.3 us (12%)
  between operations  0.73 us (3%)
    ppermute x12, starting transfers between devices, exchange(): lax.ppermute(parcel, 'context', [(i, i ^ mask) for i in range(count)])  14.1 us
    pallas_call x8, Pallas kernels, on_device(): pl.pallas_call(kernel if unread is None else lambda _, *refs: kernel(*ref...  8.7 us
    ppermute x12, waiting for transfers between devices, exchange(): lax.ppermute(parcel, 'context', [(i, i ^ mask) for i in range(count)])  3.3 us
  transfers between devices with their start and end apart: 12, of which 6 were waited for; matrix products, arithmetic and copies ran while one was open for 0% of the time, Pallas kernels for 12%

profile of v7, /device:TPU:0, one launch (start us, length us, event | category | flops | bytes accessed | tf_op | source)
XLA Modules:
  0.0 26.9 jit_solution(16799617347491467262)
XLA Ops:
  0.6 2.0 %shard_map.112 = (bf16[576,128]{1,0:T(8,128)(2,1)S(1)}, bf16[288,128]{1,0:T(8,128)(2,1)S(1)}, bf16[288,128]{1,0:T(8,128)(2,1)S(1)}, bf16[288,128]{1,0:T(8,128)(2...) custom-call(bf16[128,1024]{1,0:T(8,128)(2,1)} %q_ref.1, ...), custom_call_target="tpu_custom_call" | custom-call | tf_op jit(solution)/shard_map/pallas_call | solution.py:562
  2.7 4.0 %collective-permute-start = (bf16[576,128]{1,0:T(8,128)(2,1)S(1)}, bf16[576,128]{1,0:T(8,128)(2,1)S(1)}, u32[]{:S(2)}, u32[]{:S(2)}) collective-permute-start(bf16[576,128]{1,0:T(8,128)(2,1)S(1)} %get-tuple-element.35), channel_id=1, source_target_pairs={{0,24},{4,28},{8,16},{12,20},{16,8},{20,12},{24,0},{28,4},{1,25},{... | collective-permute-start | bytes 442376 | tf_op jit(solution)/shard_map/ppermute | solution.py:587
  6.6 0.5 %collective-permute-start.1 = (bf16[288,128]{1,0:T(8,128)(2,1)S(1)}, bf16[288,128]{1,0:T(8,128)(2,1)S(1)}, u32[]{:S(2)}, u32[]{:S(2)}) collective-permute-start(bf16[288,128]{1,0:T(8,128)(2,1)S(1)} %get-tuple-element.41), channel_id=1, source_target_pairs={{0,16},{4,20},{8,24},{12,28},{16,0},{20,4},{24,8},{28,12},{1,17},{... | collective-permute-start | bytes 221192 | tf_op jit(solution)/shard_map/ppermute | solution.py:587
  7.1 0.1 collective-permute-start.2
  7.3 0.5 %collective-permute-start.3 = (bf16[288,128]{1,0:T(8,128)(2,1)S(1)}, bf16[288,128]{1,0:T(8,128)(2,1)S(1)}, u32[]{:S(2)}, u32[]{:S(2)}) collective-permute-start(bf16[288,128]{1,0:T(8,128)(2,1)S(1)} %get-tuple-element.43), channel_id=1, source_target_pairs={{0,20},{4,16},{8,28},{12,24},{16,4},{20,0},{24,12},{28,8},{1,21},{... | collective-permute-start | bytes 221192 | tf_op jit(solution)/shard_map/ppermute | solution.py:587
  7.8 2.6 %collective-permute-start.4 = (bf16[288,128]{1,0:T(8,128)(2,1)S(1)}, bf16[288,128]{1,0:T(8,128)(2,1)S(1)}, u32[]{:S(2)}, u32[]{:S(2)}) collective-permute-start(bf16[288,128]{1,0:T(8,128)(2,1)S(1)} %get-tuple-element.44), channel_id=1, source_target_pairs={{0,12},{4,8},{8,4},{12,0},{16,28},{20,24},{24,20},{28,16},{1,13},{... | collective-permute-start | bytes 221192 | tf_op jit(solution)/shard_map/ppermute | solution.py:587
  10.4 0.5 %collective-permute-done.first_ref.refs_0_ = bf16[576,128]{1,0:T(8,128)(2,1)S(1)} collective-permute-done((bf16[576,128]{1,0:T(8,128)(2,1)S(1)}, bf16[576,128]{1,0:T(8,128)(2,1)S(1)}, u32[]{:S(2)}, u32[]{:S(2)}) %collective-permute-start) | collective-permute-done | bytes 147488 | tf_op jit(solution)/shard_map/ppermute | solution.py:587
  10.9 0.3 shard_map.113
  11.2 0.1 collective-permute-start.5
  11.3 0.0 copy-start
  11.3 1.0 %shard_map.114.spec_h = f32[4,512,128]{2,1,0:T(8,128)S(1)} custom-call(f32[128,1024]{1,0:T(8,128)S(1)} %get-tuple-element.38.h_ref, bf16[512,256]{1,0:T(8,128)(2,1)S(1)} %get-tuple-element.39.forward_hi.forward, bf16[512,256]{1,0:T(8,128)(2,1)S(1)} %get-tuple-element.40.forward_lo), custom_call_target="tpu_custom_call" | custom-call | flops 10000000000 | bytes 100000000 | tf_op jit(solution)/shard_map/pallas_call | solution.py:562
  12.3 0.0 collective-permute-done.1.refs_1_
  12.3 0.7 %collective-permute-done.2.refs_2_ = bf16[288,128]{1,0:T(8,128)(2,1)S(1)} collective-permute-done((bf16[288,128]{1,0:T(8,128)(2,1)S(1)}, bf16[288,128]{1,0:T(8,128)(2,1)S(1)}, u32[]{:S(2)}, u32[]{:S(2)}) %collective-permute-start.2) | collective-permute-done | bytes 73760 | tf_op jit(solution)/shard_map/ppermute | solution.py:587
  13.0 0.6 %collective-permute-done.3.refs_3_ = bf16[288,128]{1,0:T(8,128)(2,1)S(1)} collective-permute-done((bf16[288,128]{1,0:T(8,128)(2,1)S(1)}, bf16[288,128]{1,0:T(8,128)(2,1)S(1)}, u32[]{:S(2)}, u32[]{:S(2)}) %collective-permute-start.3) | collective-permute-done | bytes 73760 | tf_op jit(solution)/shard_map/ppermute | solution.py:587
  13.5 0.0 collective-permute-done.4.refs_4_
  13.5 0.0 collective-permute-done.5.refs_5_
  13.5 0.0 copy-done
  13.6 1.9 %shard_map.115 = (bf16[576,128]{1,0:T(8,128)(2,1)S(1)}, bf16[288,128]{1,0:T(8,128)(2,1)S(1)}, bf16[288,128]{1,0:T(8,128)(2,1)S(1)}, bf16[288,128]{1,0:T(8,128)(2...) custom-call(f32[3,7,128]{2,1,0:T(8,128)S(1)} %get-tuple-element.37.t, ...), custom_call_target="tpu_custom_call" | custom-call | tf_op jit(solution)/shard_map/pallas_call | solution.py:562
  15.5 2.5 %collective-permute-start.6 = (bf16[576,128]{1,0:T(8,128)(2,1)S(1)}, bf16[576,128]{1,0:T(8,128)(2,1)S(1)}, u32[]{:S(2)}, u32[]{:S(2)}) collective-permute-start(bf16[576,128]{1,0:T(8,128)(2,1)S(1)} %get-tuple-element.50), channel_id=1, source_target_pairs={{0,24},{4,28},{8,16},{12,20},{16,8},{20,12},{24,0},{28,4},{1,25},{... | collective-permute-start | bytes 442376 | tf_op jit(solution)/shard_map/ppermute | solution.py:587
  17.9 0.7 %collective-permute-start.11 = (bf16[288,128]{1,0:T(8,128)(2,1)S(1)}, bf16[288,128]{1,0:T(8,128)(2,1)S(1)}, u32[]{:S(2)}, u32[]{:S(2)}) collective-permute-start(bf16[288,128]{1,0:T(8,128)(2,1)S(1)} %get-tuple-element.54), channel_id=1, source_target_pairs={{0,16},{4,20},{8,24},{12,28},{16,0},{20,4},{24,8},{28,12},{1,17},{... | collective-permute-start | bytes 221192 | tf_op jit(solution)/shard_map/ppermute | solution.py:587
  18.7 0.3 %collective-permute-start.8 = (bf16[288,128]{1,0:T(8,128)(2,1)S(1)}, bf16[288,128]{1,0:T(8,128)(2,1)S(1)}, u32[]{:S(2)}, u32[]{:S(2)}) collective-permute-start(bf16[288,128]{1,0:T(8,128)(2,1)S(1)} %get-tuple-element.51), channel_id=1, source_target_pairs={{0,8},{4,12},{8,0},{12,4},{16,24},{20,28},{24,16},{28,20},{1,9},{5... | collective-permute-start | bytes 221192 | tf_op jit(solution)/shard_map/ppermute | solution.py:587
  19.0 0.6 %collective-permute-start.9 = (bf16[288,128]{1,0:T(8,128)(2,1)S(1)}, bf16[288,128]{1,0:T(8,128)(2,1)S(1)}, u32[]{:S(2)}, u32[]{:S(2)}) collective-permute-start(bf16[288,128]{1,0:T(8,128)(2,1)S(1)} %get-tuple-element.52), channel_id=1, source_target_pairs={{0,20},{4,16},{8,28},{12,24},{16,4},{20,0},{24,12},{28,8},{1,21},{... | collective-permute-start | bytes 221192 | tf_op jit(solution)/shard_map/ppermute | solution.py:587
  19.6 2.1 %collective-permute-start.10 = (bf16[288,128]{1,0:T(8,128)(2,1)S(1)}, bf16[288,128]{1,0:T(8,128)(2,1)S(1)}, u32[]{:S(2)}, u32[]{:S(2)}) collective-permute-start(bf16[288,128]{1,0:T(8,128)(2,1)S(1)} %get-tuple-element.53), channel_id=1, source_target_pairs={{0,12},{4,8},{8,4},{12,0},{16,28},{20,24},{24,20},{28,16},{1,13},{... | collective-permute-start | bytes 221192 | tf_op jit(solution)/shard_map/ppermute | solution.py:587
  21.7 0.0 copy-start.1
  21.7 0.9 %shard_map.116.filter_ref = f32[128,1024]{1,0:T(8,128)S(1)} custom-call(f32[4,512,128]{2,1,0:T(8,128)S(1)} %get-tuple-element.47.spec_x, f32[4,512,128]{2,1,0:T(8,128)S(1)} %get-tuple-element.48.spec_g, bf16[256,512]{1,0:T(8,128)(2,1)S(1)} %copy-done), custom_call_target="tpu_custom_call" | custom-call | tf_op jit(solution)/shard_map/pallas_call | solution.py:562
  22.6 0.4 %collective-permute-done.6.first_ref.refs_0_ = bf16[576,128]{1,0:T(8,128)(2,1)S(1)} collective-permute-done((bf16[576,128]{1,0:T(8,128)(2,1)S(1)}, bf16[576,128]{1,0:T(8,128)(2,1)S(1)}, u32[]{:S(2)}, u32[]{:S(2)}) %collective-permute-start.6) | collective-permute-done | bytes 147488 | tf_op jit(solution)/shard_map/ppermute | solution.py:587
  23.0 0.1 collective-permute-start.7
  23.1 0.9 %collective-permute-done.11.refs_1_ = bf16[288,128]{1,0:T(8,128)(2,1)S(1)} collective-permute-done((bf16[288,128]{1,0:T(8,128)(2,1)S(1)}, bf16[288,128]{1,0:T(8,128)(2,1)S(1)}, u32[]{:S(2)}, u32[]{:S(2)}) %collective-permute-start.11) | collective-permute-done | bytes 73760 | tf_op jit(solution)/shard_map/ppermute | solution.py:587
  24.0 0.0 copy-done.1
  24.0 1.2 %shard_map.118 = (bf16[128,1024]{1,0:T(8,128)(2,1)}, bf16[3,128,1024]{2,1,0:T(8,128)(2,1)}, f32[1,128,1024]{2,1,0:T(8,128)}) custom-call(f32[3,7,1024]{2,1,0:T(8,128)S(1)} %copy-done.1, f32[6,4,128,128]{3,2,1,0:T(8,128)S(1)} %get-tuple-element.32.far_ref, f32[2,4,128,128]{3,2,1,0:T(8,128)S(1)} %get-tuple-element.36.near_ref, ...), custom_call_target="tpu_custom_call" | custom-call | flops 10000000000 | bytes 100000000 | tf_op jit(solution)/shard_map/pallas_call | solution.py:562
  25.3 0.0 collective-permute-done.8.refs_1_
  25.3 0.2 collective-permute-done.9.refs_2_
  25.4 0.0 collective-permute-done.10.refs_3_
  25.4 0.0 collective-permute-done.7.refs_0_.refs_4_
  25.4 1.4 %shard_map.119 = (bf16[128,1024]{1,0:T(8,128)(2,1)}, bf16[3,128,1024]{2,1,0:T(8,128)(2,1)}) custom-call(f32[3,7,1024]{2,1,0:T(8,128)S(1)} %copy-done.1, f32[6,4,128,128]{3,2,1,0:T(8,128)S(1)} %get-tuple-element.32.far_ref, f32[2,4,128,128]{3,2,1,0:T(8,128)S(1)} %get-tuple-element.36.near_ref, ...), custom_call_target="tpu_custom_call", output_to_operand_aliasing={{0}: (8, {}), {1}: (9, {})} | custom-call | tf_op jit(solution)/shard_map/pallas_call | solution.py:562
  (1 shorter events, 0.0 us)
Async XLA Ops:
  2.7 8.3 %collective-permute-start = (bf16[576,128]{1,0:T(8,128)(2,1)S(1)}, bf16[576,128]{1,0:T(8,128)(2,1)S(1)}, u32[]{:S(2)}, u32[]{:S(2)}) collective-permute-start(bf16[576,128]{1,0:T(8,128)(2,1)S(1)} %get-tuple-element.35), channel_id=1, source_target_pairs={{0,24},{4,28},{8,16},{12,20},{16,8},{20,12},{24,0},{28,4},{1,25},{... | collective-permute-start | bytes 442376 | tf_op jit(solution)/shard_map/ppermute | solution.py:587
  6.6 5.6 %collective-permute-start.1 = (bf16[288,128]{1,0:T(8,128)(2,1)S(1)}, bf16[288,128]{1,0:T(8,128)(2,1)S(1)}, u32[]{:S(2)}, u32[]{:S(2)}) collective-permute-start(bf16[288,128]{1,0:T(8,128)(2,1)S(1)} %get-tuple-element.41), channel_id=1, source_target_pairs={{0,16},{4,20},{8,24},{12,28},{16,0},{20,4},{24,8},{28,12},{1,17},{... | collective-permute-start | bytes 221192 | tf_op jit(solution)/shard_map/ppermute | solution.py:587
  7.1 5.8 %collective-permute-start.2 = (bf16[288,128]{1,0:T(8,128)(2,1)S(1)}, bf16[288,128]{1,0:T(8,128)(2,1)S(1)}, u32[]{:S(2)}, u32[]{:S(2)}) collective-permute-start(bf16[288,128]{1,0:T(8,128)(2,1)S(1)} %get-tuple-element.42), channel_id=1, source_target_pairs={{0,8},{4,12},{8,0},{12,4},{16,24},{20,28},{24,16},{28,20},{1,9},{5... | collective-permute-start | bytes 221192 | tf_op jit(solution)/shard_map/ppermute | solution.py:587
  7.3 6.3 %collective-permute-start.3 = (bf16[288,128]{1,0:T(8,128)(2,1)S(1)}, bf16[288,128]{1,0:T(8,128)(2,1)S(1)}, u32[]{:S(2)}, u32[]{:S(2)}) collective-permute-start(bf16[288,128]{1,0:T(8,128)(2,1)S(1)} %get-tuple-element.43), channel_id=1, source_target_pairs={{0,20},{4,16},{8,28},{12,24},{16,4},{20,0},{24,12},{28,8},{1,21},{... | collective-permute-start | bytes 221192 | tf_op jit(solution)/shard_map/ppermute | solution.py:587
  7.8 5.7 %collective-permute-start.4 = (bf16[288,128]{1,0:T(8,128)(2,1)S(1)}, bf16[288,128]{1,0:T(8,128)(2,1)S(1)}, u32[]{:S(2)}, u32[]{:S(2)}) collective-permute-start(bf16[288,128]{1,0:T(8,128)(2,1)S(1)} %get-tuple-element.44), channel_id=1, source_target_pairs={{0,12},{4,8},{8,4},{12,0},{16,28},{20,24},{24,20},{28,16},{1,13},{... | collective-permute-start | bytes 221192 | tf_op jit(solution)/shard_map/ppermute | solution.py:587
  11.2 2.4 %collective-permute-start.5 = (bf16[576,128]{1,0:T(8,128)(2,1)S(1)}, bf16[576,128]{1,0:T(8,128)(2,1)S(1)}, u32[]{:S(2)}, u32[]{:S(2)}) collective-permute-start(bf16[576,128]{1,0:T(8,128)(2,1)S(1)} %get-tuple-element.45), channel_id=1, source_target_pairs={{0,4},{4,0},{8,12},{12,8},{16,20},{20,16},{24,28},{28,24},{1,5},{5... | collective-permute-start | bytes 442376 | tf_op jit(solution)/shard_map/ppermute | solution.py:587
  11.3 2.3 %copy-start = (bf16[256,512]{1,0:T(8,128)(2,1)S(1)}, bf16[256,512]{1,0:T(8,128)(2,1)}, u32[]{:S(2)}) copy-start(bf16[256,512]{1,0:T(8,128)(2,1)} %constant.8.clone.inverse) | copy-start | bytes 786436
  15.5 7.6 %collective-permute-start.6 = (bf16[576,128]{1,0:T(8,128)(2,1)S(1)}, bf16[576,128]{1,0:T(8,128)(2,1)S(1)}, u32[]{:S(2)}, u32[]{:S(2)}) collective-permute-start(bf16[576,128]{1,0:T(8,128)(2,1)S(1)} %get-tuple-element.50), channel_id=1, source_target_pairs={{0,24},{4,28},{8,16},{12,20},{16,8},{20,12},{24,0},{28,4},{1,25},{... | collective-permute-start | bytes 442376 | tf_op jit(solution)/shard_map/ppermute | solution.py:587
  17.9 6.1 %collective-permute-start.11 = (bf16[288,128]{1,0:T(8,128)(2,1)S(1)}, bf16[288,128]{1,0:T(8,128)(2,1)S(1)}, u32[]{:S(2)}, u32[]{:S(2)}) collective-permute-start(bf16[288,128]{1,0:T(8,128)(2,1)S(1)} %get-tuple-element.54), channel_id=1, source_target_pairs={{0,16},{4,20},{8,24},{12,28},{16,0},{20,4},{24,8},{28,12},{1,17},{... | collective-permute-start | bytes 221192 | tf_op jit(solution)/shard_map/ppermute | solution.py:587
  18.7 6.6 %collective-permute-start.8 = (bf16[288,128]{1,0:T(8,128)(2,1)S(1)}, bf16[288,128]{1,0:T(8,128)(2,1)S(1)}, u32[]{:S(2)}, u32[]{:S(2)}) collective-permute-start(bf16[288,128]{1,0:T(8,128)(2,1)S(1)} %get-tuple-element.51), channel_id=1, source_target_pairs={{0,8},{4,12},{8,0},{12,4},{16,24},{20,28},{24,16},{28,20},{1,9},{5... | collective-permute-start | bytes 221192 | tf_op jit(solution)/shard_map/ppermute | solution.py:587
  19.0 6.4 %collective-permute-start.9 = (bf16[288,128]{1,0:T(8,128)(2,1)S(1)}, bf16[288,128]{1,0:T(8,128)(2,1)S(1)}, u32[]{:S(2)}, u32[]{:S(2)}) collective-permute-start(bf16[288,128]{1,0:T(8,128)(2,1)S(1)} %get-tuple-element.52), channel_id=1, source_target_pairs={{0,20},{4,16},{8,28},{12,24},{16,4},{20,0},{24,12},{28,8},{1,21},{... | collective-permute-start | bytes 221192 | tf_op jit(solution)/shard_map/ppermute | solution.py:587
  19.6 5.8 %collective-permute-start.10 = (bf16[288,128]{1,0:T(8,128)(2,1)S(1)}, bf16[288,128]{1,0:T(8,128)(2,1)S(1)}, u32[]{:S(2)}, u32[]{:S(2)}) collective-permute-start(bf16[288,128]{1,0:T(8,128)(2,1)S(1)} %get-tuple-element.53), channel_id=1, source_target_pairs={{0,12},{4,8},{8,4},{12,0},{16,28},{20,24},{24,20},{28,16},{1,13},{... | collective-permute-start | bytes 221192 | tf_op jit(solution)/shard_map/ppermute | solution.py:587
  21.7 2.3 %copy-start.1 = (f32[3,7,1024]{2,1,0:T(8,128)S(1)}, f32[3,7,1024]{2,1,0:T(8,128)}, u32[]{:S(2)}) copy-start(f32[3,7,1024]{2,1,0:T(8,128)} %taps_ref.5) | copy-start | bytes 258052
  23.0 2.4 %collective-permute-start.7 = (bf16[576,128]{1,0:T(8,128)(2,1)S(1)}, bf16[576,128]{1,0:T(8,128)(2,1)S(1)}, u32[]{:S(2)}, u32[]{:S(2)}) collective-permute-start(bf16[576,128]{1,0:T(8,128)(2,1)S(1)} %shard_map.117), channel_id=1, source_target_pairs={{0,4},{4,0},{8,12},{12,8},{16,20},{20,16},{24,28},{28,24},{1,5},{5... | collective-permute-start | bytes 442376 | tf_op jit(solution)/shard_map/ppermute | solution.py:587

commit v8 on v7

--- a/solution.py
+++ b/solution.py
@@ -674,7 +674,7 @@
     (shared,) = on_device(share_kernel, [double], [], (filter_grad, sent[-2], first))
     shared = exchange(shared, 1)
     returned = [first, shared, *others, shared, sent[-1]]
-    early = [0, *far[2:3], near[-1]]
+    early = [0, near[-1]]
     late = [place for place in range(blocks) if place not in early]
     outputs = (
         pltpu.HBM((rows, channels), jnp.bfloat16),

time: 27 us -> 27.2 us (level)
  no operation moved by 1% of the time
where the time goes in v8:
time: 27.2 us; the launch traced here: 27 us
  starting transfers between devices  14.1 us (52%)
  Pallas kernels  8.7 us (32%)
  waiting for transfers between devices  3.44 us (13%)
  between operations  0.74 us (3%)
    ppermute x12, starting transfers between devices, exchange(): lax.ppermute(parcel, 'context', [(i, i ^ mask) for i in range(count)])  14.1 us
    pallas_call x8, Pallas kernels, on_device(): pl.pallas_call(kernel if unread is None else lambda _, *refs: kernel(*ref...  8.7 us
    ppermute x12, waiting for transfers between devices, exchange(): lax.ppermute(parcel, 'context', [(i, i ^ mask) for i in range(count)])  3.44 us
  transfers between devices with their start and end apart: 12, of which 6 were waited for; matrix products, arithmetic and copies ran while one was open for 0% of the time, Pallas kernels for 12%

profile of v8, /device:TPU:0, one launch (start us, length us, event | category | flops | bytes accessed | tf_op | source)
XLA Modules:
  0.0 27.0 jit_solution(14753850952510492958)
XLA Ops:
  0.6 2.0 %shard_map.112 = (bf16[576,128]{1,0:T(8,128)(2,1)S(1)}, bf16[288,128]{1,0:T(8,128)(2,1)S(1)}, bf16[288,128]{1,0:T(8,128)(2,1)S(1)}, bf16[288,128]{1,0:T(8,128)(2...) custom-call(bf16[128,1024]{1,0:T(8,128)(2,1)} %q_ref.1, ...), custom_call_target="tpu_custom_call" | custom-call | tf_op jit(solution)/shard_map/pallas_call | solution.py:562
  2.7 4.0 %collective-permute-start = (bf16[576,128]{1,0:T(8,128)(2,1)S(1)}, bf16[576,128]{1,0:T(8,128)(2,1)S(1)}, u32[]{:S(2)}, u32[]{:S(2)}) collective-permute-start(bf16[576,128]{1,0:T(8,128)(2,1)S(1)} %get-tuple-element.35), channel_id=1, source_target_pairs={{0,24},{4,28},{8,16},{12,20},{16,8},{20,12},{24,0},{28,4},{1,25},{... | collective-permute-start | bytes 442376 | tf_op jit(solution)/shard_map/ppermute | solution.py:587
  6.6 0.5 %collective-permute-start.1 = (bf16[288,128]{1,0:T(8,128)(2,1)S(1)}, bf16[288,128]{1,0:T(8,128)(2,1)S(1)}, u32[]{:S(2)}, u32[]{:S(2)}) collective-permute-start(bf16[288,128]{1,0:T(8,128)(2,1)S(1)} %get-tuple-element.41), channel_id=1, source_target_pairs={{0,16},{4,20},{8,24},{12,28},{16,0},{20,4},{24,8},{28,12},{1,17},{... | collective-permute-start | bytes 221192 | tf_op jit(solution)/shard_map/ppermute | solution.py:587
  7.1 0.1 collective-permute-start.2
  7.3 0.5 %collective-permute-start.3 = (bf16[288,128]{1,0:T(8,128)(2,1)S(1)}, bf16[288,128]{1,0:T(8,128)(2,1)S(1)}, u32[]{:S(2)}, u32[]{:S(2)}) collective-permute-start(bf16[288,128]{1,0:T(8,128)(2,1)S(1)} %get-tuple-element.43), channel_id=1, source_target_pairs={{0,20},{4,16},{8,28},{12,24},{16,4},{20,0},{24,12},{28,8},{1,21},{... | collective-permute-start | bytes 221192 | tf_op jit(solution)/shard_map/ppermute | solution.py:587
  7.8 2.6 %collective-permute-start.4 = (bf16[288,128]{1,0:T(8,128)(2,1)S(1)}, bf16[288,128]{1,0:T(8,128)(2,1)S(1)}, u32[]{:S(2)}, u32[]{:S(2)}) collective-permute-start(bf16[288,128]{1,0:T(8,128)(2,1)S(1)} %get-tuple-element.44), channel_id=1, source_target_pairs={{0,12},{4,8},{8,4},{12,0},{16,28},{20,24},{24,20},{28,16},{1,13},{... | collective-permute-start | bytes 221192 | tf_op jit(solution)/shard_map/ppermute | solution.py:587
  10.4 0.5 %collective-permute-done.first_ref.refs_0_ = bf16[576,128]{1,0:T(8,128)(2,1)S(1)} collective-permute-done((bf16[576,128]{1,0:T(8,128)(2,1)S(1)}, bf16[576,128]{1,0:T(8,128)(2,1)S(1)}, u32[]{:S(2)}, u32[]{:S(2)}) %collective-permute-start) | collective-permute-done | bytes 147488 | tf_op jit(solution)/shard_map/ppermute | solution.py:587
  10.9 0.3 shard_map.113
  11.2 0.1 collective-permute-start.5
  11.3 0.0 copy-start
  11.3 1.0 %shard_map.114.spec_h = f32[4,512,128]{2,1,0:T(8,128)S(1)} custom-call(f32[128,1024]{1,0:T(8,128)S(1)} %get-tuple-element.38.h_ref, bf16[512,256]{1,0:T(8,128)(2,1)S(1)} %get-tuple-element.39.forward_hi.forward, bf16[512,256]{1,0:T(8,128)(2,1)S(1)} %get-tuple-element.40.forward_lo), custom_call_target="tpu_custom_call" | custom-call | flops 10000000000 | bytes 100000000 | tf_op jit(solution)/shard_map/pallas_call | solution.py:562
  12.3 0.0 collective-permute-done.1.refs_1_
  12.3 0.7 %collective-permute-done.2.refs_2_ = bf16[288,128]{1,0:T(8,128)(2,1)S(1)} collective-permute-done((bf16[288,128]{1,0:T(8,128)(2,1)S(1)}, bf16[288,128]{1,0:T(8,128)(2,1)S(1)}, u32[]{:S(2)}, u32[]{:S(2)}) %collective-permute-start.2) | collective-permute-done | bytes 73760 | tf_op jit(solution)/shard_map/ppermute | solution.py:587
  13.0 0.6 %collective-permute-done.3.refs_3_ = bf16[288,128]{1,0:T(8,128)(2,1)S(1)} collective-permute-done((bf16[288,128]{1,0:T(8,128)(2,1)S(1)}, bf16[288,128]{1,0:T(8,128)(2,1)S(1)}, u32[]{:S(2)}, u32[]{:S(2)}) %collective-permute-start.3) | collective-permute-done | bytes 73760 | tf_op jit(solution)/shard_map/ppermute | solution.py:587
  13.5 0.0 collective-permute-done.4.refs_4_
  13.5 0.0 collective-permute-done.5.refs_5_
  13.5 0.0 copy-done
  13.6 1.9 %shard_map.115 = (bf16[576,128]{1,0:T(8,128)(2,1)S(1)}, bf16[288,128]{1,0:T(8,128)(2,1)S(1)}, bf16[288,128]{1,0:T(8,128)(2,1)S(1)}, bf16[288,128]{1,0:T(8,128)(2...) custom-call(f32[3,7,128]{2,1,0:T(8,128)S(1)} %get-tuple-element.37.t, ...), custom_call_target="tpu_custom_call" | custom-call | tf_op jit(solution)/shard_map/pallas_call | solution.py:562
  15.5 2.5 %collective-permute-start.6 = (bf16[576,128]{1,0:T(8,128)(2,1)S(1)}, bf16[576,128]{1,0:T(8,128)(2,1)S(1)}, u32[]{:S(2)}, u32[]{:S(2)}) collective-permute-start(bf16[576,128]{1,0:T(8,128)(2,1)S(1)} %get-tuple-element.50), channel_id=1, source_target_pairs={{0,24},{4,28},{8,16},{12,20},{16,8},{20,12},{24,0},{28,4},{1,25},{... | collective-permute-start | bytes 442376 | tf_op jit(solution)/shard_map/ppermute | solution.py:587
  18.0 0.7 %collective-permute-start.8 = (bf16[288,128]{1,0:T(8,128)(2,1)S(1)}, bf16[288,128]{1,0:T(8,128)(2,1)S(1)}, u32[]{:S(2)}, u32[]{:S(2)}) collective-permute-start(bf16[288,128]{1,0:T(8,128)(2,1)S(1)} %get-tuple-element.51), channel_id=1, source_target_pairs={{0,16},{4,20},{8,24},{12,28},{16,0},{20,4},{24,8},{28,12},{1,17},{... | collective-permute-start | bytes 221192 | tf_op jit(solution)/shard_map/ppermute | solution.py:587
  18.7 0.3 %collective-permute-start.9 = (bf16[288,128]{1,0:T(8,128)(2,1)S(1)}, bf16[288,128]{1,0:T(8,128)(2,1)S(1)}, u32[]{:S(2)}, u32[]{:S(2)}) collective-permute-start(bf16[288,128]{1,0:T(8,128)(2,1)S(1)} %get-tuple-element.52), channel_id=1, source_target_pairs={{0,8},{4,12},{8,0},{12,4},{16,24},{20,28},{24,16},{28,20},{1,9},{5... | collective-permute-start | bytes 221192 | tf_op jit(solution)/shard_map/ppermute | solution.py:587
  19.0 0.6 %collective-permute-start.10 = (bf16[288,128]{1,0:T(8,128)(2,1)S(1)}, bf16[288,128]{1,0:T(8,128)(2,1)S(1)}, u32[]{:S(2)}, u32[]{:S(2)}) collective-permute-start(bf16[288,128]{1,0:T(8,128)(2,1)S(1)} %get-tuple-element.53), channel_id=1, source_target_pairs={{0,20},{4,16},{8,28},{12,24},{16,4},{20,0},{24,12},{28,8},{1,21},{... | collective-permute-start | bytes 221192 | tf_op jit(solution)/shard_map/ppermute | solution.py:587
  19.6 2.1 %collective-permute-start.11 = (bf16[288,128]{1,0:T(8,128)(2,1)S(1)}, bf16[288,128]{1,0:T(8,128)(2,1)S(1)}, u32[]{:S(2)}, u32[]{:S(2)}) collective-permute-start(bf16[288,128]{1,0:T(8,128)(2,1)S(1)} %get-tuple-element.54), channel_id=1, source_target_pairs={{0,12},{4,8},{8,4},{12,0},{16,28},{20,24},{24,20},{28,16},{1,13},{... | collective-permute-start | bytes 221192 | tf_op jit(solution)/shard_map/ppermute | solution.py:587
  21.7 0.0 copy-start.1
  21.7 0.9 %shard_map.116.filter_ref = f32[128,1024]{1,0:T(8,128)S(1)} custom-call(f32[4,512,128]{2,1,0:T(8,128)S(1)} %get-tuple-element.47.spec_x, f32[4,512,128]{2,1,0:T(8,128)S(1)} %get-tuple-element.48.spec_g, bf16[256,512]{1,0:T(8,128)(2,1)S(1)} %copy-done), custom_call_target="tpu_custom_call" | custom-call | tf_op jit(solution)/shard_map/pallas_call | solution.py:562
  22.6 0.4 %collective-permute-done.6.first_ref.refs_0_ = bf16[576,128]{1,0:T(8,128)(2,1)S(1)} collective-permute-done((bf16[576,128]{1,0:T(8,128)(2,1)S(1)}, bf16[576,128]{1,0:T(8,128)(2,1)S(1)}, u32[]{:S(2)}, u32[]{:S(2)}) %collective-permute-start.6) | collective-permute-done | bytes 147488 | tf_op jit(solution)/shard_map/ppermute | solution.py:587
  23.0 0.1 collective-permute-start.7
  23.1 0.0 copy-done.1
  23.1 1.0 %shard_map.118 = (bf16[128,1024]{1,0:T(8,128)(2,1)}, bf16[3,128,1024]{2,1,0:T(8,128)(2,1)}, f32[1,128,1024]{2,1,0:T(8,128)}) custom-call(f32[3,7,1024]{2,1,0:T(8,128)S(1)} %copy-done.1, f32[6,4,128,128]{3,2,1,0:T(8,128)S(1)} %get-tuple-element.32.far_ref, f32[2,4,128,128]{3,2,1,0:T(8,128)S(1)} %get-tuple-element.36.near_ref, ...), custom_call_target="tpu_custom_call" | custom-call | flops 10000000000 | bytes 100000000 | tf_op jit(solution)/shard_map/pallas_call | solution.py:562
  24.2 0.0 collective-permute-done.8.refs_1_
  24.2 0.8 %collective-permute-done.9.refs_2_ = bf16[288,128]{1,0:T(8,128)(2,1)S(1)} collective-permute-done((bf16[288,128]{1,0:T(8,128)(2,1)S(1)}, bf16[288,128]{1,0:T(8,128)(2,1)S(1)}, u32[]{:S(2)}, u32[]{:S(2)}) %collective-permute-start.9) | collective-permute-done | bytes 73760 | tf_op jit(solution)/shard_map/ppermute | solution.py:587
  24.9 0.5 %collective-permute-done.10.refs_3_ = bf16[288,128]{1,0:T(8,128)(2,1)S(1)} collective-permute-done((bf16[288,128]{1,0:T(8,128)(2,1)S(1)}, bf16[288,128]{1,0:T(8,128)(2,1)S(1)}, u32[]{:S(2)}, u32[]{:S(2)}) %collective-permute-start.10) | collective-permute-done | bytes 73760 | tf_op jit(solution)/shard_map/ppermute | solution.py:587
  25.4 0.0 collective-permute-done.11.refs_4_
  25.4 0.0 collective-permute-done.7.refs_0_.refs_5_
  25.4 1.6 %shard_map.119 = (bf16[128,1024]{1,0:T(8,128)(2,1)}, bf16[3,128,1024]{2,1,0:T(8,128)(2,1)}) custom-call(f32[3,7,1024]{2,1,0:T(8,128)S(1)} %copy-done.1, f32[6,4,128,128]{3,2,1,0:T(8,128)S(1)} %get-tuple-element.32.far_ref, f32[2,4,128,128]{3,2,1,0:T(8,128)S(1)} %get-tuple-element.36.near_ref, ...), custom_call_target="tpu_custom_call", output_to_operand_aliasing={{0}: (9, {}), {1}: (10, {})} | custom-call | tf_op jit(solution)/shard_map/pallas_call | solution.py:562
  (1 shorter events, 0.0 us)
Async XLA Ops:
  2.7 8.3 %collective-permute-start = (bf16[576,128]{1,0:T(8,128)(2,1)S(1)}, bf16[576,128]{1,0:T(8,128)(2,1)S(1)}, u32[]{:S(2)}, u32[]{:S(2)}) collective-permute-start(bf16[576,128]{1,0:T(8,128)(2,1)S(1)} %get-tuple-element.35), channel_id=1, source_target_pairs={{0,24},{4,28},{8,16},{12,20},{16,8},{20,12},{24,0},{28,4},{1,25},{... | collective-permute-start | bytes 442376 | tf_op jit(solution)/shard_map/ppermute | solution.py:587
  6.6 5.6 %collective-permute-start.1 = (bf16[288,128]{1,0:T(8,128)(2,1)S(1)}, bf16[288,128]{1,0:T(8,128)(2,1)S(1)}, u32[]{:S(2)}, u32[]{:S(2)}) collective-permute-start(bf16[288,128]{1,0:T(8,128)(2,1)S(1)} %get-tuple-element.41), channel_id=1, source_target_pairs={{0,16},{4,20},{8,24},{12,28},{16,0},{20,4},{24,8},{28,12},{1,17},{... | collective-permute-start | bytes 221192 | tf_op jit(solution)/shard_map/ppermute | solution.py:587
  7.1 5.8 %collective-permute-start.2 = (bf16[288,128]{1,0:T(8,128)(2,1)S(1)}, bf16[288,128]{1,0:T(8,128)(2,1)S(1)}, u32[]{:S(2)}, u32[]{:S(2)}) collective-permute-start(bf16[288,128]{1,0:T(8,128)(2,1)S(1)} %get-tuple-element.42), channel_id=1, source_target_pairs={{0,8},{4,12},{8,0},{12,4},{16,24},{20,28},{24,16},{28,20},{1,9},{5... | collective-permute-start | bytes 221192 | tf_op jit(solution)/shard_map/ppermute | solution.py:587
  7.3 6.3 %collective-permute-start.3 = (bf16[288,128]{1,0:T(8,128)(2,1)S(1)}, bf16[288,128]{1,0:T(8,128)(2,1)S(1)}, u32[]{:S(2)}, u32[]{:S(2)}) collective-permute-start(bf16[288,128]{1,0:T(8,128)(2,1)S(1)} %get-tuple-element.43), channel_id=1, source_target_pairs={{0,20},{4,16},{8,28},{12,24},{16,4},{20,0},{24,12},{28,8},{1,21},{... | collective-permute-start | bytes 221192 | tf_op jit(solution)/shard_map/ppermute | solution.py:587
  7.8 5.7 %collective-permute-start.4 = (bf16[288,128]{1,0:T(8,128)(2,1)S(1)}, bf16[288,128]{1,0:T(8,128)(2,1)S(1)}, u32[]{:S(2)}, u32[]{:S(2)}) collective-permute-start(bf16[288,128]{1,0:T(8,128)(2,1)S(1)} %get-tuple-element.44), channel_id=1, source_target_pairs={{0,12},{4,8},{8,4},{12,0},{16,28},{20,24},{24,20},{28,16},{1,13},{... | collective-permute-start | bytes 221192 | tf_op jit(solution)/shard_map/ppermute | solution.py:587
  11.2 2.4 %collective-permute-start.5 = (bf16[576,128]{1,0:T(8,128)(2,1)S(1)}, bf16[576,128]{1,0:T(8,128)(2,1)S(1)}, u32[]{:S(2)}, u32[]{:S(2)}) collective-permute-start(bf16[576,128]{1,0:T(8,128)(2,1)S(1)} %get-tuple-element.45), channel_id=1, source_target_pairs={{0,4},{4,0},{8,12},{12,8},{16,20},{20,16},{24,28},{28,24},{1,5},{5... | collective-permute-start | bytes 442376 | tf_op jit(solution)/shard_map/ppermute | solution.py:587
  11.3 2.3 %copy-start = (bf16[256,512]{1,0:T(8,128)(2,1)S(1)}, bf16[256,512]{1,0:T(8,128)(2,1)}, u32[]{:S(2)}) copy-start(bf16[256,512]{1,0:T(8,128)(2,1)} %constant.8.clone.inverse) | copy-start | bytes 786436
  15.5 7.6 %collective-permute-start.6 = (bf16[576,128]{1,0:T(8,128)(2,1)S(1)}, bf16[576,128]{1,0:T(8,128)(2,1)S(1)}, u32[]{:S(2)}, u32[]{:S(2)}) collective-permute-start(bf16[576,128]{1,0:T(8,128)(2,1)S(1)} %get-tuple-element.50), channel_id=1, source_target_pairs={{0,24},{4,28},{8,16},{12,20},{16,8},{20,12},{24,0},{28,4},{1,25},{... | collective-permute-start | bytes 442376 | tf_op jit(solution)/shard_map/ppermute | solution.py:587
  18.0 6.2 %collective-permute-start.8 = (bf16[288,128]{1,0:T(8,128)(2,1)S(1)}, bf16[288,128]{1,0:T(8,128)(2,1)S(1)}, u32[]{:S(2)}, u32[]{:S(2)}) collective-permute-start(bf16[288,128]{1,0:T(8,128)(2,1)S(1)} %get-tuple-element.51), channel_id=1, source_target_pairs={{0,16},{4,20},{8,24},{12,28},{16,0},{20,4},{24,8},{28,12},{1,17},{... | collective-permute-start | bytes 221192 | tf_op jit(solution)/shard_map/ppermute | solution.py:587
  18.7 6.3 %collective-permute-start.9 = (bf16[288,128]{1,0:T(8,128)(2,1)S(1)}, bf16[288,128]{1,0:T(8,128)(2,1)S(1)}, u32[]{:S(2)}, u32[]{:S(2)}) collective-permute-start(bf16[288,128]{1,0:T(8,128)(2,1)S(1)} %get-tuple-element.52), channel_id=1, source_target_pairs={{0,8},{4,12},{8,0},{12,4},{16,24},{20,28},{24,16},{28,20},{1,9},{5... | collective-permute-start | bytes 221192 | tf_op jit(solution)/shard_map/ppermute | solution.py:587
  19.0 6.4 %collective-permute-start.10 = (bf16[288,128]{1,0:T(8,128)(2,1)S(1)}, bf16[288,128]{1,0:T(8,128)(2,1)S(1)}, u32[]{:S(2)}, u32[]{:S(2)}) collective-permute-start(bf16[288,128]{1,0:T(8,128)(2,1)S(1)} %get-tuple-element.53), channel_id=1, source_target_pairs={{0,20},{4,16},{8,28},{12,24},{16,4},{20,0},{24,12},{28,8},{1,21},{... | collective-permute-start | bytes 221192 | tf_op jit(solution)/shard_map/ppermute | solution.py:587
  19.6 5.8 %collective-permute-start.11 = (bf16[288,128]{1,0:T(8,128)(2,1)S(1)}, bf16[288,128]{1,0:T(8,128)(2,1)S(1)}, u32[]{:S(2)}, u32[]{:S(2)}) collective-permute-start(bf16[288,128]{1,0:T(8,128)(2,1)S(1)} %get-tuple-element.54), channel_id=1, source_target_pairs={{0,12},{4,8},{8,4},{12,0},{16,28},{20,24},{24,20},{28,16},{1,13},{... | collective-permute-start | bytes 221192 | tf_op jit(solution)/shard_map/ppermute | solution.py:587
  21.7 1.4 %copy-start.1 = (f32[3,7,1024]{2,1,0:T(8,128)S(1)}, f32[3,7,1024]{2,1,0:T(8,128)}, u32[]{:S(2)}) copy-start(f32[3,7,1024]{2,1,0:T(8,128)} %taps_ref.5) | copy-start | bytes 258052
  23.0 2.4 %collective-permute-start.7 = (bf16[576,128]{1,0:T(8,128)(2,1)S(1)}, bf16[576,128]{1,0:T(8,128)(2,1)S(1)}, u32[]{:S(2)}, u32[]{:S(2)}) collective-permute-start(bf16[576,128]{1,0:T(8,128)(2,1)S(1)} %shard_map.117), channel_id=1, source_target_pairs={{0,4},{4,0},{8,12},{12,8},{16,20},{20,16},{24,28},{28,24},{1,5},{5... | collective-permute-start | bytes 442376 | tf_op jit(solution)/shard_map/ppermute | solution.py:587
